TPU v7x, 32 devices: a whole 2x2x4 slice. The times are simulated.
32 devices in a mesh: dp: 8 (over y, x, core), fsdp: 4 (over z).
Axes of the slice: x: 2, y: 2, z: 4, core: 2. Of those that a mesh axis runs over, the one named last changes fastest.
Arguments:
- tokens: bfloat16 [2, 32, 256, 1536], P(None, ('dp', 'fsdp')), may hold values from -6 to 6
- w_query: bfloat16 [1536, 1536], P(('dp', 'fsdp')), may hold values from -0.3125 to 0.3125
- w_keyval: bfloat16 [1536, 512], P(('dp', 'fsdp')), may hold values from -0.15625 to 0.15625
- w_out: bfloat16 [1536, 1536], P(('dp', 'fsdp')), may hold values from -1.25 to 1.25
- w_gate: bfloat16 [1536, 4608], P(('dp', 'fsdp')), may hold values from -0.15625 to 0.15625
- w_up: bfloat16 [1536, 4608], P(('dp', 'fsdp')), may hold values from -0.15625 to 0.15625
- w_down: bfloat16 [4608, 1536], P(('dp', 'fsdp')), may hold values from -0.09375 to 0.09375
- gain_attn: bfloat16 [1536], P(('dp', 'fsdp')), may hold values from 0.5 to 1.5
- gain_ffn: bfloat16 [1536], P(('dp', 'fsdp')), may hold values from 0.5 to 1.5
- cotangent: bfloat16 [2, 32, 256, 1536], P(None, ('dp', 'fsdp')), may hold values from -6 to 6
- block_perm: int32 [2, 32], replicated, may hold values from 0 to 31, each once within a row
- extra_len: int32 [2, 4], replicated, may hold values from 1 to 3073, 4100 in all within a row
Outputs:
- block_out: bfloat16 [2, 32, 256, 1536], P(None, ('dp', 'fsdp'))
- grad_tokens: bfloat16 [2, 32, 256, 1536], P(None, ('dp', 'fsdp'))
- grad_query: float32 [1536, 1536], P(('dp', 'fsdp'))
- grad_keyval: float32 [1536, 512], P(('dp', 'fsdp'))
- grad_out: float32 [1536, 1536], P(('dp', 'fsdp'))
- grad_gate: float32 [1536, 4608], P(('dp', 'fsdp'))
- grad_up: float32 [1536, 4608], P(('dp', 'fsdp'))
- grad_down: float32 [4608, 1536], P(('dp', 'fsdp'))
- grad_gain_attn: float32 [1536], P(('dp', 'fsdp'))
- grad_gain_ffn: float32 [1536], P(('dp', 'fsdp'))
Inputs may be any that keep to these rules, and one draw needn't show every extreme that they name: Each row of block_perm names every block of its micro-batch once. `extra_len`: each row sums to 8192 - 4 * (1023) and has an entry equal to 3073.
All inputs are finite; a program needn't handle non-finite values.
Results may differ from a plain program's by a relative error of at most 0.015.
The roundings to bfloat16 on the way count: a program that leaves them out, or rounds other values in their place, can miss the bound.
Values may be sent and summed in bfloat16 or wider, within the bound.
A program may use at most 320 MiB of HBM per device.

v0:
```python
import jax
import jax.numpy as jnp
from jax import lax
from jax.sharding import PartitionSpec as P

H = 6
HD = 256
WIN = 1024
BLK = 256


EPS = 1e-06


def for_sending(x):
    return jax.tree.map(lambda a: a.astype(jnp.bfloat16) if a.dtype == jnp.float32 else a, x)


def shifted(value, axis, steps):
    count = lax.axis_size(axis)
    leading, last = (max(0, -steps), min(count, count - steps))
    return lax.ppermute(value, axis, [(source, source + steps) for source in range(leading, last)])


def norm_rows(value, gain):
    inverse = lax.rsqrt(jnp.mean(value * value, axis=-1, keepdims=True) + EPS)
    return (value * inverse * gain, inverse)


def norm_back(value, inverse, gain, grad):
    scaled = grad * gain
    width = value.shape[-1]
    dvalue = (
        inverse * scaled
        - value * inverse**3 * jnp.sum(scaled * value, axis=-1, keepdims=True) / width
    )
    dgain = jnp.sum(grad * value * inverse, axis=0)
    return (dvalue, dgain)


def sequence_of(positions, ends):
    return jnp.sum((positions[:, None] >= ends[None, :]).astype(jnp.int32), axis=1)


def visible_mask(query_pos, key_pos, ends):
    same = sequence_of(query_pos, ends)[:, None] == sequence_of(key_pos, ends)[None, :]
    gap = query_pos[:, None] - key_pos[None, :]
    return same & (gap >= 0) & (gap < WIN) & (key_pos[None, :] >= 0)


def geglu(gate, up):
    return jax.nn.gelu(gate, approximate=True) * up


def move_keys(value, order, count):
    rows = value.shape[0]
    spread = lax.all_to_all(value, ("dp", "fsdp"), split_axis=1, concat_axis=0, tiled=True)
    pieces = spread.reshape(count, rows, spread.shape[1])
    placed = jnp.take(pieces, order, axis=0).reshape(count * rows, spread.shape[1])
    return lax.all_to_all(placed, ("dp", "fsdp"), split_axis=0, concat_axis=1, tiled=True)


def move_grads(value, order, count):
    rows = value.shape[0]
    spread = lax.all_to_all(
        for_sending(value), ("dp", "fsdp"), split_axis=1, concat_axis=0, tiled=True
    ).astype(value.dtype)
    pieces = spread.reshape(count, rows, spread.shape[1])
    placed = jnp.take(pieces, order, axis=0).reshape(count * rows, spread.shape[1])
    return lax.all_to_all(
        for_sending(placed), ("dp", "fsdp"), split_axis=0, concat_axis=1, tiled=True
    ).astype(placed.dtype)


def body(
    tokens,
    w_query,
    w_keyval,
    w_out,
    w_gate,
    w_up,
    w_down,
    gain_attn,
    gain_ffn,
    cotangent,
    block_perm,
    extra_len,
):
    count = lax.axis_size(("dp", "fsdp"))
    me = lax.axis_index(("dp", "fsdp"))
    batches = tokens.shape[0]
    sources = WIN // BLK + 1
    scale = HD ** (-0.5)
    shards = (w_query, w_keyval, w_out, w_gate, w_up, w_down, gain_attn, gain_ffn)
    device_ids = jnp.arange(count, dtype=jnp.int32)
    totals = None
    outputs = []
    input_grads = []
    for batch in range(batches):
        full = (
            lax.all_gather(shards[0], ("dp", "fsdp"), axis=0, tiled=True),
            lax.all_gather(shards[1], ("dp", "fsdp"), axis=0, tiled=True),
            lax.all_gather(shards[2], ("dp", "fsdp"), axis=0, tiled=True),
            lax.all_gather(shards[3], ("dp", "fsdp"), axis=0, tiled=True),
            lax.all_gather(shards[4], ("dp", "fsdp"), axis=0, tiled=True),
            lax.all_gather(shards[5], ("dp", "fsdp"), axis=0, tiled=True),
            lax.all_gather(shards[6], ("dp", "fsdp"), axis=0, tiled=True),
            lax.all_gather(shards[7], ("dp", "fsdp"), axis=0, tiled=True),
        )
        wq, wkv, wo, wg, wu, wd, g1b, g2b = full
        g1 = g1b.astype(jnp.float32)
        g2 = g2b.astype(jnp.float32)
        perm_row = block_perm[batch]
        ends = jnp.cumsum(extra_len[batch] + (WIN - 1))
        mine = lax.dynamic_slice_in_dim(perm_row, me, 1)[0]
        holder = jnp.sum(
            jnp.where(perm_row[None, :] == device_ids[:, None], device_ids[None, :], 0), axis=1
        )
        query_pos = mine * BLK + jnp.arange(BLK, dtype=jnp.int32)
        key_pos = (mine - (sources - 1)) * BLK + jnp.arange(sources * BLK, dtype=jnp.int32)
        mask = jnp.repeat(visible_mask(query_pos, key_pos, ends), H, axis=0)
        x = tokens[batch, 0].astype(jnp.float32)
        n1, r1 = norm_rows(x, g1)
        n1b = n1.astype(jnp.bfloat16)
        query = (jnp.dot(n1b, wq, preferred_element_type=jnp.float32) * scale).astype(jnp.bfloat16)
        query_rows = query.reshape(BLK * H, HD)
        keyval = jnp.dot(n1b, wkv, preferred_element_type=jnp.float32).astype(jnp.bfloat16)
        ordered = move_keys(keyval, holder, count)
        window = [ordered] * sources
        for back in range(1, sources):
            window[sources - 1 - back] = shifted(ordered, ("dp", "fsdp"), back)
        picked = move_keys(jnp.concatenate(window, axis=0), perm_row, count)
        keys_src = picked[:, :HD]
        values_src = picked[:, HD:]
        scores = jnp.einsum("qd,kd->qk", query_rows, keys_src, preferred_element_type=jnp.float32)
        masked = jnp.where(mask, scores, -1e30)
        top = jnp.max(masked, axis=1, keepdims=True)
        expd = jnp.exp(masked - top)
        rowsum = jnp.sum(expd, axis=1, keepdims=True)
        lse = top + jnp.log(rowsum)
        probs_low = (expd / rowsum).astype(jnp.bfloat16)
        att = jnp.dot(probs_low, values_src, preferred_element_type=jnp.float32)
        att_low = att.reshape(BLK, H * HD).astype(jnp.bfloat16)
        mixed = x + jnp.dot(att_low, wo, preferred_element_type=jnp.float32)
        n2, r2 = norm_rows(mixed, g2)
        n2b = n2.astype(jnp.bfloat16)
        gate = jnp.dot(n2b, wg, preferred_element_type=jnp.float32)
        up = jnp.dot(n2b, wu, preferred_element_type=jnp.float32)
        hidden = geglu(gate, up).astype(jnp.bfloat16)
        outputs.append(
            (mixed + jnp.dot(hidden, wd, preferred_element_type=jnp.float32)).astype(jnp.bfloat16)
        )
        wq, wkv, wo, wg, wu, wd, g1b, g2b = (
            lax.all_gather(shards[0], ("dp", "fsdp"), axis=0, tiled=True),
            lax.all_gather(shards[1], ("dp", "fsdp"), axis=0, tiled=True),
            lax.all_gather(shards[2], ("dp", "fsdp"), axis=0, tiled=True),
            lax.all_gather(shards[3], ("dp", "fsdp"), axis=0, tiled=True),
            lax.all_gather(shards[4], ("dp", "fsdp"), axis=0, tiled=True),
            lax.all_gather(shards[5], ("dp", "fsdp"), axis=0, tiled=True),
            lax.all_gather(shards[6], ("dp", "fsdp"), axis=0, tiled=True),
            lax.all_gather(shards[7], ("dp", "fsdp"), axis=0, tiled=True),
        )
        dy = cotangent[batch, 0]
        d_down = jnp.einsum("tf,td->fd", hidden, dy, preferred_element_type=jnp.float32)
        d_hidden = jnp.einsum("td,fd->tf", dy, wd, preferred_element_type=jnp.float32)
        _, geglu_pull = jax.vjp(geglu, gate, up)
        d_gate, d_up = geglu_pull(d_hidden)
        d_gate_low = d_gate.astype(jnp.bfloat16)
        d_up_low = d_up.astype(jnp.bfloat16)
        d_wgate = jnp.einsum("td,tf->df", n2b, d_gate_low, preferred_element_type=jnp.float32)
        d_wup = jnp.einsum("td,tf->df", n2b, d_up_low, preferred_element_type=jnp.float32)
        d_n2 = jnp.einsum("tf,df->td", d_gate_low, wg, preferred_element_type=jnp.float32)
        d_n2 = d_n2 + jnp.einsum("tf,df->td", d_up_low, wu, preferred_element_type=jnp.float32)
        d_mixed_norm, d_g2 = norm_back(mixed, r2, g2, d_n2)
        d_mixed = dy.astype(jnp.float32) + d_mixed_norm
        d_branch = d_mixed.astype(jnp.bfloat16)
        d_wout = jnp.einsum("ta,td->ad", att_low, d_branch, preferred_element_type=jnp.float32)
        d_att = jnp.einsum("td,ad->ta", d_branch, wo, preferred_element_type=jnp.float32)
        d_att_rows = d_att.astype(jnp.bfloat16).reshape(BLK * H, HD)
        again = jnp.einsum("qd,kd->qk", query_rows, keys_src, preferred_element_type=jnp.float32)
        probs = jnp.exp(jnp.where(mask, again, -1e30) - lse)
        d_probs = jnp.einsum(
            "qd,kd->qk", d_att_rows, values_src, preferred_element_type=jnp.float32
        )
        delta = jnp.sum(probs * d_probs, axis=1, keepdims=True)
        d_scores = (probs * (d_probs - delta)).astype(jnp.bfloat16)
        d_query = jnp.dot(d_scores, keys_src, preferred_element_type=jnp.float32).astype(
            jnp.bfloat16
        )
        d_query = d_query.reshape(BLK, H * HD)
        d_keys = jnp.einsum("qk,qd->kd", d_scores, query_rows, preferred_element_type=jnp.float32)
        d_values = jnp.einsum(
            "qk,qd->kd", probs.astype(jnp.bfloat16), d_att_rows, preferred_element_type=jnp.float32
        )
        d_keyval_flat = jnp.concatenate([d_keys, d_values], axis=1)
        ordered_grads = move_grads(d_keyval_flat, holder, count).reshape(sources, BLK, 2 * HD)
        summed = ordered_grads[sources - 1]
        for back in range(1, sources):
            summed = summed + shifted(
                ordered_grads[sources - 1 - back].astype(jnp.bfloat16), ("dp", "fsdp"), -back
            ).astype(jnp.float32)
        d_keyval = move_grads(summed, perm_row, count).astype(jnp.bfloat16)
        d_wquery = jnp.einsum("td,ta->da", n1b, d_query, preferred_element_type=jnp.float32) * scale
        d_wkeyval = jnp.einsum("td,tc->dc", n1b, d_keyval, preferred_element_type=jnp.float32)
        d_n1 = jnp.einsum("ta,da->td", d_query, wq, preferred_element_type=jnp.float32) * scale
        d_n1 = d_n1 + jnp.einsum("tc,dc->td", d_keyval, wkv, preferred_element_type=jnp.float32)
        d_x_norm, d_g1 = norm_back(x, r1, g1, d_n1)
        input_grads.append((d_mixed + d_x_norm).astype(jnp.bfloat16))
        local = (d_wquery, d_wkeyval, d_wout, d_wgate, d_wup, d_down, d_g1, d_g2)
        totals = local if totals is None else tuple((a + b for a, b in zip(totals, local)))
    totals = lax.psum_scatter(totals, ("dp", "fsdp"), scatter_dimension=0, tiled=True)
    block_out = jnp.stack(outputs)[:, None]
    grad_tokens = jnp.stack(input_grads)[:, None]
    return (
        block_out,
        grad_tokens,
        totals[0],
        totals[1],
        totals[2],
        totals[3],
        totals[4],
        totals[5],
        totals[6],
        totals[7],
    )


def solution(mesh):
    placed = (
        P(None, ("dp", "fsdp"), None, None),
        P(("dp", "fsdp"), None),
        P(("dp", "fsdp"), None),
        P(("dp", "fsdp"), None),
        P(("dp", "fsdp"), None),
        P(("dp", "fsdp"), None),
        P(("dp", "fsdp"), None),
        P(("dp", "fsdp")),
        P(("dp", "fsdp")),
        P(None, ("dp", "fsdp"), None, None),
        P(),
        P(),
    )
    return jax.shard_map(
        body,
        mesh=mesh,
        in_specs=placed,
        out_specs=(
            P(None, ("dp", "fsdp"), None, None),
            P(None, ("dp", "fsdp"), None, None),
            P(("dp", "fsdp"), None),
            P(("dp", "fsdp"), None),
            P(("dp", "fsdp"), None),
            P(("dp", "fsdp"), None),
            P(("dp", "fsdp"), None),
            P(("dp", "fsdp"), None),
            P(("dp", "fsdp")),
            P(("dp", "fsdp")),
        ),
        check_vma=False,
    )
```

profile of v0, /device:TPU:0, one launch (start us, length us, event | category | flops | bytes accessed | tf_op | source)
XLA Modules:
  0.0 2186.5 jit_solution(7207792569293828390)
XLA Ops:
  11.7 42.1 %all-reduce.5 = (bf16[1536]{0:T(1024)(128)(2,1)S(1)}, bf16[1536]{0:T(1024)(128)(2,1)S(1)}) all-reduce(bf16[1536]{0:T(1024)(128)(2,1)S(1)} %dynamic-update-slice, bf16[1536]{0:T(1024)(128)(2,1)S(1)} %dynamic-update-slice.1), channel_id=1, replica_groups=mesh['dp'=8,'fsdp'=4] {'dp','fsdp'}, use_global_device_ids=true, to_apply=%add | all-reduce | flops 3072 | bytes 12288
  55.0 13.8 all-gather.9.cloned.1.call-done
  178.7 21.3 collective-permute-done.5
  214.0 31.1 %all-to-all-start.6 = ((bf16[1280,32,16]{0,2,1:T(8,128)(2,1)}), bf16[1280,32,16]{0,2,1:T(8,128)(2,1)S(1)}, u32[]{:S(2)}, u32[]{:S(2)}) async-start(bf16[1280,32,16]{0,2,1:T(8,128)(2,1)} %copy-done.33), calls=%async_computation.6 | async-start | bytes 2621440 | tf_op jit(solution)/shard_map/all_to_all | solution.py:57
  251.8 33.4 %all-to-all-done.6 = bf16[1280,32,16]{0,2,1:T(8,128)(2,1)S(1)} async-done(((bf16[1280,32,16]{0,2,1:T(8,128)(2,1)}), bf16[1280,32,16]{0,2,1:T(8,128)(2,1)S(1)}, u32[]{:S(2)}, u32[]{:S(2)}) %all-to-all-start.6) | async-done | bytes 1310752 | tf_op jit(solution)/shard_map/all_to_all | solution.py:57
  321.5 12.7 all-to-all-done.3
  359.8 38.6 %all-to-all-done.7 = bf16[32,1280,16]{1,2,0:T(8,128)(2,1)} async-done(((bf16[32,1280,16]{1,2,0:T(8,128)(2,1)}), bf16[32,1280,16]{1,2,0:T(8,128)(2,1)}, u32[]{:S(2)}, u32[]{:S(2)}) %all-to-all-start.7) | async-done | bytes 1310752 | tf_op jit(solution)/shard_map/all_to_all | solution.py:60
  417.6 10.8 fusion.149
  428.4 80.0 %all-gather.15.cloned.1.call-done = bf16[1536,4608]{1,0:T(8,128)(2,1)} async-done(((bf16[48,4608]{1,0:T(8,128)(2,1)}), bf16[1536,4608]{1,0:T(8,128)(2,1)}) %all-gather.15.cloned.1.call-update) | async-done | bytes 14155792 | tf_op jit(solution)/shard_map/all_gather | solution.py:105
  518.9 93.5 %all-gather.17.cloned.1.call-done = bf16[4608,1536]{1,0:T(8,128)(2,1)} async-done(((bf16[144,1536]{1,0:T(8,128)(2,1)}), bf16[4608,1536]{1,0:T(8,128)(2,1)}) %all-gather.17.cloned.1.call-update) | async-done | bytes 14155792 | tf_op jit(solution)/shard_map/all_gather | solution.py:106
  612.5 12.5 multiply_convert_fusion.3
  634.2 12.9 multiply_reduce_fusion.3
  647.1 10.8 fusion.152
  668.4 12.5 multiply_convert_fusion.2
  690.1 16.8 multiply_reduce_fusion.2
  792.6 26.0 %all-to-all-done.12 = bf16[1280,32,16]{0,2,1:T(8,128)(2,1)S(1)} async-done(((bf16[1280,32,16]{0,2,1:T(8,128)(2,1)}), bf16[1280,32,16]{0,2,1:T(8,128)(2,1)S(1)}, u32[]{:S(2)}, u32[]{:S(2)}) %all-to-all-start.12) | async-done | bytes 1310752 | tf_op jit(solution)/shard_map/all_to_all | solution.py:65
  825.4 28.3 %all-to-all-done.9 = bf16[32,1280,16]{1,2,0:T(8,128)(2,1)} async-done(((bf16[32,1280,16]{1,2,0:T(8,128)(2,1)}), bf16[32,1280,16]{1,2,0:T(8,128)(2,1)}, u32[]{:S(2)}, u32[]{:S(2)}) %all-to-all-start.9) | async-done | bytes 1310752 | tf_op jit(solution)/shard_map/all_to_all | solution.py:70
  865.7 28.7 %all-to-all-done.13 = bf16[32,1280,16]{1,2,0:T(8,128)(2,1)S(1)} async-done(((bf16[32,1280,16]{1,2,0:T(8,128)(2,1)}), bf16[32,1280,16]{1,2,0:T(8,128)(2,1)S(1)}, u32[]{:S(2)}, u32[]{:S(2)}) %all-to-all-start.13) | async-done | bytes 1310752 | tf_op jit(solution)/shard_map/all_to_all | solution.py:70
  899.8 13.5 collective-permute-done.9
  915.3 14.3 all-to-all-start.10
  1011.9 13.2 fusion.156
  1025.0 20.8 convolution_add_fusion.1
  1045.9 13.1 fusion.155
  1059.1 19.5 convolution_add_fusion.2
  1079.9 13.1 fusion.102
  1093.1 22.0 %convolution_add_fusion = f32[4608,1536]{1,0:T(8,128)} fusion(f32[4608,1536]{1,0:T(8,128)} %fusion.102, bf16[256,4608]{1,0:T(8,128)(2,1)} %get-tuple-element.79, bf16[2,1,256,1536]{3,2,1,0:T(8,128)(2,1)S(1)} %copy-done.15), kind=kOutput, calls=%fused_computation.8 | convolution fusion | flops 3630956544 | bytes 59768832 | tf_op jit(solution)/shard_map/tf,td->fd/dot_general | solution.py:164
  1142.6 41.1 %all-reduce.4 = (f32[1536]{0:T(1024)S(1)}, f32[1536]{0:T(1024)S(1)}) all-reduce(f32[1536]{0:T(1024)S(1)} %add.330, f32[1536]{0:T(1024)S(1)} %add.331), channel_id=8, replica_groups=mesh['dp'=8,'fsdp'=4] {'dp','fsdp'}, use_global_device_ids=true, to_apply=%region_30.35.clone | all-reduce | flops 3072 | bytes 24576
  1189.4 37.5 %reduce-scatter.11.cloned.1.call-done = f32[48,1536]{1,0:T(8,128)} async-done(((f32[1536,1536]{1,0:T(8,128)}), f32[48,1536]{1,0:T(8,128)}) %reduce-scatter.11.cloned.1.call-update) | async-done | bytes 294928 | tf_op jit(solution)/shard_map/reduce_scatter | solution.py:211
  1226.9 142.2 %reduce-scatter.7.cloned.1.call-done = f32[48,1536]{1,0:T(8,128)} async-done(((f32[1536,1536]{1,0:T(8,128)}), f32[48,1536]{1,0:T(8,128)}) %reduce-scatter.7.cloned.1.call-update) | async-done | bytes 294928 | tf_op jit(solution)/shard_map/reduce_scatter | solution.py:211
  1369.1 269.5 %reduce-scatter.15.cloned.1.call-done = f32[48,4608]{1,0:T(8,128)} async-done(((f32[1536,4608]{1,0:T(8,128)}), f32[48,4608]{1,0:T(8,128)}) %reduce-scatter.15.cloned.1.call-update) | async-done | bytes 884752 | tf_op jit(solution)/shard_map/reduce_scatter | solution.py:211
  1638.5 270.4 %reduce-scatter.13.cloned.1.call-done = f32[48,4608]{1,0:T(8,128)} async-done(((f32[1536,4608]{1,0:T(8,128)}), f32[48,4608]{1,0:T(8,128)}) %reduce-scatter.13.cloned.1.call-update) | async-done | bytes 884752 | tf_op jit(solution)/shard_map/reduce_scatter | solution.py:211
  1909.0 270.2 %reduce-scatter.17.cloned.1.call-done = f32[144,1536]{1,0:T(8,128)} async-done(((f32[4608,1536]{1,0:T(8,128)}), f32[144,1536]{1,0:T(8,128)}) %reduce-scatter.17.cloned.1.call-update) | async-done | bytes 884752 | tf_op jit(solution)/shard_map/reduce_scatter | solution.py:211
  (373 shorter events, 481.5 us)
Async XLA Ops:
  7.2 61.6 %all-gather.9.cloned.1.call-start = ((), (), s32[]{:S(2)}) async-start(), calls=%async_computation.23 | async-start | bytes 1622016 | tf_op jit(solution)/shard_map/all_gather | solution.py:102
  8.0 308.8 %all-gather.7.cloned.1.call-start = ((), (), s32[]{:S(2)}) async-start(), calls=%async_computation.22 | async-start | bytes 4866048 | tf_op jit(solution)/shard_map/all_gather | solution.py:101
  8.7 401.7 %all-gather.11.cloned.1.call-start = ((), (), s32[]{:S(2)}) async-start(), calls=%async_computation.24 | async-start | bytes 4866048 | tf_op jit(solution)/shard_map/all_gather | solution.py:103
  9.4 408.2 %all-gather.13.cloned.1.call-start = ((), (), s32[]{:S(2)}) async-start(), calls=%async_computation.25 | async-start | bytes 14598144 | tf_op jit(solution)/shard_map/all_gather | solution.py:104
  10.0 498.4 %all-gather.15.cloned.1.call-start = ((), (), s32[]{:S(2)}) async-start(), calls=%async_computation.26 | async-start | bytes 14598144 | tf_op jit(solution)/shard_map/all_gather | solution.py:105
  10.6 601.9 %all-gather.17.cloned.1.call-start = ((), (), s32[]{:S(2)}) async-start(), calls=%async_computation.27 | async-start | bytes 14598144 | tf_op jit(solution)/shard_map/all_gather | solution.py:106
  121.9 39.8 %all-to-all-start.5 = ((bf16[32,256,16]{1,2,0:T(8,128)(2,1)}), bf16[32,256,16]{1,2,0:T(8,128)(2,1)S(1)}, u32[]{:S(2)}, u32[]{:S(2)}) async-start(bf16[32,256,16]{1,2,0:T(8,128)(2,1)} %broadcast_select_fusion.2), calls=%async_computation.5 | async-start | bytes 524288 | tf_op jit(solution)/shard_map/all_to_all | solution.py:60
  161.6 52.4 %all-to-all-start.2 = ((bf16[1280,32,16]{0,2,1:T(8,128)(2,1)}), bf16[1280,32,16]{0,2,1:T(8,128)(2,1)S(1)}, u32[]{:S(2)}, u32[]{:S(2)}) async-start(bf16[1280,32,16]{0,2,1:T(8,128)(2,1)} %bitcast_dynamic-update-slice_fusion.1), calls=%async_computation.2 | async-start | bytes 2621440 | tf_op jit(solution)/shard_map/all_to_all | solution.py:57
  167.3 32.8 %collective-permute-start.5 = (bf16[256,512]{0,1:T(8,128)(2,1)S(1)}, bf16[256,512]{0,1:T(8,128)(2,1)S(1)}, u32[]{:S(2)}, u32[]{:S(2)}) collective-permute-start(bf16[256,512]{0,1:T(8,128)(2,1)S(1)} %bitcast.316), channel_id=1, source_target_pairs={{0,3},{1,4},{2,5},{3,6},{4,7},{5,8},{6,9},{7,10},{8,11},{9,12},{10... | collective-permute-start | bytes 786440 | tf_op jit(solution)/shard_map/ppermute | solution.py:22
  172.8 34.5 %collective-permute-start.6 = (bf16[256,512]{0,1:T(8,128)(2,1)S(1)}, bf16[256,512]{0,1:T(8,128)(2,1)S(1)}, u32[]{:S(2)}, u32[]{:S(2)}) collective-permute-start(bf16[256,512]{0,1:T(8,128)(2,1)S(1)} %bitcast.317), channel_id=1, source_target_pairs={{0,2},{1,3},{2,4},{3,5},{4,6},{5,7},{6,8},{7,9},{8,10},{9,11},{10,... | collective-permute-start | bytes 786440 | tf_op jit(solution)/shard_map/ppermute | solution.py:22
  175.3 37.6 %collective-permute-start.7 = (bf16[256,512]{0,1:T(8,128)(2,1)S(1)}, bf16[256,512]{0,1:T(8,128)(2,1)S(1)}, u32[]{:S(2)}, u32[]{:S(2)}) collective-permute-start(bf16[256,512]{0,1:T(8,128)(2,1)S(1)} %bitcast.318), channel_id=1, source_target_pairs={{0,1},{1,2},{2,3},{3,4},{4,5},{5,6},{6,7},{7,8},{8,9},{9,10},{10,1... | collective-permute-start | bytes 786440 | tf_op jit(solution)/shard_map/ppermute | solution.py:22
  214.0 71.1 %all-to-all-start.6 = ((bf16[1280,32,16]{0,2,1:T(8,128)(2,1)}), bf16[1280,32,16]{0,2,1:T(8,128)(2,1)S(1)}, u32[]{:S(2)}, u32[]{:S(2)}) async-start(bf16[1280,32,16]{0,2,1:T(8,128)(2,1)} %copy-done.33), calls=%async_computation.6 | async-start | bytes 2621440 | tf_op jit(solution)/shard_map/all_to_all | solution.py:57
  285.1 49.1 %all-to-all-start.3 = ((bf16[32,1280,16]{1,2,0:T(8,128)(2,1)}), bf16[32,1280,16]{1,2,0:T(8,128)(2,1)}, u32[]{:S(2)}, u32[]{:S(2)}) async-start(bf16[32,1280,16]{1,2,0:T(8,128)(2,1)} %broadcast_select_fusion.1), calls=%async_computation.3 | async-start | bytes 2621440 | tf_op jit(solution)/shard_map/all_to_all | solution.py:60
  334.2 64.2 %all-to-all-start.7 = ((bf16[32,1280,16]{1,2,0:T(8,128)(2,1)}), bf16[32,1280,16]{1,2,0:T(8,128)(2,1)}, u32[]{:S(2)}, u32[]{:S(2)}) async-start(bf16[32,1280,16]{1,2,0:T(8,128)(2,1)} %broadcast_select_fusion), calls=%async_computation.7 | async-start | bytes 2621440 | tf_op jit(solution)/shard_map/all_to_all | solution.py:60
  744.8 37.4 %all-to-all-start.8 = ((bf16[1280,32,16]{0,2,1:T(8,128)(2,1)}), bf16[1280,32,16]{0,2,1:T(8,128)(2,1)S(1)}, u32[]{:S(2)}, u32[]{:S(2)}) async-start(bf16[1280,32,16]{0,2,1:T(8,128)(2,1)} %pad_maximum_fusion), calls=%async_computation.8 | async-start | bytes 2621440 | tf_op jit(solution)/shard_map/all_to_all | solution.py:65
  782.1 36.4 %all-to-all-start.12 = ((bf16[1280,32,16]{0,2,1:T(8,128)(2,1)}), bf16[1280,32,16]{0,2,1:T(8,128)(2,1)S(1)}, u32[]{:S(2)}, u32[]{:S(2)}) async-start(bf16[1280,32,16]{0,2,1:T(8,128)(2,1)} %pad_maximum_fusion.1), calls=%async_computation.12 | async-start | bytes 2621440 | tf_op jit(solution)/shard_map/all_to_all | solution.py:65
  818.6 35.2 %all-to-all-start.9 = ((bf16[32,1280,16]{1,2,0:T(8,128)(2,1)}), bf16[32,1280,16]{1,2,0:T(8,128)(2,1)}, u32[]{:S(2)}, u32[]{:S(2)}) async-start(bf16[32,1280,16]{1,2,0:T(8,128)(2,1)} %select_convert_fusion.1), calls=%async_computation.9 | async-start | bytes 2621440 | tf_op jit(solution)/shard_map/all_to_all | solution.py:70
  853.7 40.7 %all-to-all-start.13 = ((bf16[32,1280,16]{1,2,0:T(8,128)(2,1)}), bf16[32,1280,16]{1,2,0:T(8,128)(2,1)S(1)}, u32[]{:S(2)}, u32[]{:S(2)}) async-start(bf16[32,1280,16]{1,2,0:T(8,128)(2,1)} %select_convert_fusion), calls=%async_computation.13 | async-start | bytes 2621440 | tf_op jit(solution)/shard_map/all_to_all | solution.py:70
  860.5 35.3 %collective-permute-start.10 = (bf16[256,512]{0,1:T(8,128)(2,1)}, bf16[256,512]{0,1:T(8,128)(2,1)}, u32[]{:S(2)}, u32[]{:S(2)}) collective-permute-start(bf16[256,512]{0,1:T(8,128)(2,1)} %bitcast.54), channel_id=1, source_target_pairs={{3,0},{4,1},{5,2},{6,3},{7,4},{8,5},{9,6},{10,7},{11,8},{12,9},{13... | collective-permute-start | bytes 786440 | tf_op jit(solution)/shard_map/ppermute | solution.py:22
  861.8 35.4 %collective-permute-start.11 = (bf16[256,512]{0,1:T(8,128)(2,1)}, bf16[256,512]{0,1:T(8,128)(2,1)}, u32[]{:S(2)}, u32[]{:S(2)}) collective-permute-start(bf16[256,512]{0,1:T(8,128)(2,1)} %bitcast.55), channel_id=1, source_target_pairs={{4,0},{5,1},{6,2},{7,3},{8,4},{9,5},{10,6},{11,7},{12,8},{13,9},{1... | collective-permute-start | bytes 786440 | tf_op jit(solution)/shard_map/ppermute | solution.py:22
  863.1 35.4 %collective-permute-start.8 = (bf16[256,512]{0,1:T(8,128)(2,1)S(1)}, bf16[256,512]{0,1:T(8,128)(2,1)}, u32[]{:S(2)}, u32[]{:S(2)}) collective-permute-start(bf16[256,512]{0,1:T(8,128)(2,1)S(1)} %bitcast.331), channel_id=1, source_target_pairs={{1,0},{2,1},{3,2},{4,3},{5,4},{6,5},{7,6},{8,7},{9,8},{10,9},{11,1... | collective-permute-start | bytes 786440 | tf_op jit(solution)/shard_map/ppermute | solution.py:22
  864.4 48.9 %collective-permute-start.9 = (bf16[256,512]{0,1:T(8,128)(2,1)S(1)}, bf16[256,512]{0,1:T(8,128)(2,1)}, u32[]{:S(2)}, u32[]{:S(2)}) collective-permute-start(bf16[256,512]{0,1:T(8,128)(2,1)S(1)} %bitcast.327), channel_id=1, source_target_pairs={{2,0},{3,1},{4,2},{5,3},{6,4},{7,5},{8,6},{9,7},{10,8},{11,9},{12,... | collective-permute-start | bytes 786440 | tf_op jit(solution)/shard_map/ppermute | solution.py:22
  894.5 35.1 %collective-permute-start.12 = (bf16[256,512]{0,1:T(8,128)(2,1)S(1)}, bf16[256,512]{0,1:T(8,128)(2,1)S(1)}, u32[]{:S(2)}, u32[]{:S(2)}) collective-permute-start(bf16[256,512]{0,1:T(8,128)(2,1)S(1)} %bitcast.332), channel_id=1, source_target_pairs={{1,0},{2,1},{3,2},{4,3},{5,4},{6,5},{7,6},{8,7},{9,8},{10,9},{11,1... | collective-permute-start | bytes 786440 | tf_op jit(solution)/shard_map/ppermute | solution.py:22
  895.8 42.4 %collective-permute-start.13 = (bf16[256,512]{0,1:T(8,128)(2,1)S(1)}, bf16[256,512]{0,1:T(8,128)(2,1)S(1)}, u32[]{:S(2)}, u32[]{:S(2)}) collective-permute-start(bf16[256,512]{0,1:T(8,128)(2,1)S(1)} %bitcast.330), channel_id=1, source_target_pairs={{2,0},{3,1},{4,2},{5,3},{6,4},{7,5},{8,6},{9,7},{10,8},{11,9},{12,... | collective-permute-start | bytes 786440 | tf_op jit(solution)/shard_map/ppermute | solution.py:22
  897.1 41.0 %collective-permute-start.14 = (bf16[256,512]{0,1:T(8,128)(2,1)S(1)}, bf16[256,512]{0,1:T(8,128)(2,1)S(1)}, u32[]{:S(2)}, u32[]{:S(2)}) collective-permute-start(bf16[256,512]{0,1:T(8,128)(2,1)S(1)} %bitcast.329), channel_id=1, source_target_pairs={{3,0},{4,1},{5,2},{6,3},{7,4},{8,5},{9,6},{10,7},{11,8},{12,9},{13... | collective-permute-start | bytes 786440 | tf_op jit(solution)/shard_map/ppermute | solution.py:22
  898.5 39.7 %collective-permute-start.15 = (bf16[256,512]{0,1:T(8,128)(2,1)S(1)}, bf16[256,512]{0,1:T(8,128)(2,1)S(1)}, u32[]{:S(2)}, u32[]{:S(2)}) collective-permute-start(bf16[256,512]{0,1:T(8,128)(2,1)S(1)} %bitcast.328), channel_id=1, source_target_pairs={{4,0},{5,1},{6,2},{7,3},{8,4},{9,5},{10,6},{11,7},{12,8},{13,9},{1... | collective-permute-start | bytes 786440 | tf_op jit(solution)/shard_map/ppermute | solution.py:22
  970.1 219.3 %reduce-scatter.9.cloned.1.call-start = ((), (), s32[]{:S(2)}) async-start(), calls=%async_computation.29 | async-start | bytes 3244032 | tf_op jit(solution)/shard_map/reduce_scatter | solution.py:211
  984.8 242.2 %reduce-scatter.11.cloned.1.call-start = ((), (), s32[]{:S(2)}) async-start(), calls=%async_computation.30 | async-start | bytes 9732096 | tf_op jit(solution)/shard_map/reduce_scatter | solution.py:211
  993.1 376.0 %reduce-scatter.7.cloned.1.call-start = ((), (), s32[]{:S(2)}) async-start(), calls=%async_computation.28 | async-start | bytes 9732096 | tf_op jit(solution)/shard_map/reduce_scatter | solution.py:211
  1010.7 627.8 %reduce-scatter.15.cloned.1.call-start = ((), (), s32[]{:S(2)}) async-start(), calls=%async_computation.32 | async-start | bytes 29196288 | tf_op jit(solution)/shard_map/reduce_scatter | solution.py:211
  1045.9 863.1 %reduce-scatter.13.cloned.1.call-start = ((), (), s32[]{:S(2)}) async-start(), calls=%async_computation.31 | async-start | bytes 29196288 | tf_op jit(solution)/shard_map/reduce_scatter | solution.py:211
  1078.6 1100.6 %reduce-scatter.17.cloned.1.call-start = ((), (), s32[]{:S(2)}) async-start(), calls=%async_computation.33 | async-start | bytes 29196288 | tf_op jit(solution)/shard_map/reduce_scatter | solution.py:211
  (86 other events, 2088.3 us)
Sparse Core Ops, SparseCore 0:
  10.9 57.8 all-gather.8
  71.6 79.2 all-gather.6
  153.7 88.4 all-gather.10
  244.9 158.6 all-gather.12
  406.2 102.2 all-gather.14
  511.1 101.3 all-gather.16
  984.9 99.6 reduce-scatter.8
  1091.0 135.8 reduce-scatter.10
  1234.4 134.6 reduce-scatter.6
  1375.9 262.5 reduce-scatter.14
  1645.6 263.3 reduce-scatter.12
  1915.8 263.3 reduce-scatter.16
where the time goes:
time: 2190 us
  waiting for transfers between devices  1490 us (68%)
  matrix products  347 us (16%)
  starting transfers between devices  137 us (6%)
  blocking collectives  83.2 us (4%)
  local copies, waits for them, and re-layouts  66.3 us (3%)
  other arithmetic  48.5 us (2%)
    reduce_scatter x6, waiting for transfers between devices, body(): lax.psum_scatter(totals, ('dp', 'fsdp'), scatter_dimension=0, tiled=True)  990 us
    all_gather x1, waiting for transfers between devices, body(): lax.all_gather(shards[5], ('dp', 'fsdp'), axis=0, tiled=True)  93.5 us
    unnamed x2, blocking collectives  83.2 us
    all_gather x1, waiting for transfers between devices, body(): lax.all_gather(shards[4], ('dp', 'fsdp'), axis=0, tiled=True)  80 us
    ppermute x16, waiting for transfers between devices, shifted(): lax.ppermute(value, axis, [(source, source + steps) for source in range(l...  74.4 us
    all_to_all x4, waiting for transfers between devices, move_grads(): lax.all_to_all(for_sending(placed), ('dp', 'fsdp'), split_axis=0, concat_...  73.1 us
    all_to_all x4, waiting for transfers between devices, move_keys(): lax.all_to_all(placed, ('dp', 'fsdp'), split_axis=0, concat_axis=1, tiled...  68 us
    all_to_all x4, waiting for transfers between devices, move_keys(): lax.all_to_all(value, ('dp', 'fsdp'), split_axis=1, concat_axis=0, tiled=...  52.7 us
  transfers between devices with their start and end apart: 44, of which 30 were waited for; matrix products, arithmetic and copies ran while one was open for 14% of the time, Pallas kernels for 0%

commit v1 on v0

--- a/solution.py
+++ b/solution.py
@@ -1,6 +1,11 @@
+import functools
+import math
+
 import jax
 import jax.numpy as jnp
 from jax import lax
+from jax.experimental import pallas as pl
+from jax.experimental.pallas import tpu as pltpu
 from jax.sharding import PartitionSpec as P
 
 H = 6
@@ -10,6 +15,7 @@
 
 
 EPS = 1e-06
+VMEM = 60 * 1024 * 1024
 
 
 def for_sending(x):
@@ -225,7 +231,504 @@
     )
 
 
+MESH = pl.DeviceIdType.MESH
+
+class Place:
+    def __init__(self, grid):
+        self.A, self.B, self.C, self.Z = grid
+        dp = lax.axis_index("dp")
+        self.z = lax.axis_index("fsdp")
+        self.c = dp % 2
+        self.x = (dp // 2) % 2
+        self.y = dp // 4
+    def dev(self, y=None, x=None, c=None, z=None):
+        y = self.y if y is None else y
+        x = self.x if x is None else x
+        c = self.c if c is None else c
+        z = self.z if z is None else z
+        return ((y * 2 + x) * 2 + c, z)
+
+def barrier(p):
+    sem = pltpu.get_barrier_semaphore()
+    peers = [p.dev(c=1 - p.c), p.dev(x=1 - p.x), p.dev(y=1 - p.y)] + [p.dev(z=(p.z + i) % p.Z) for i in range(1, p.Z)]
+    for q in peers:
+        pl.semaphore_signal(sem, inc=1, device_id=q, device_id_type=MESH)
+    pl.semaphore_wait(sem, len(peers))
+
+class Gather:
+    COPIES = 12
+    def __init__(self, p, src, dst, rows, cols, send, recv, local):
+        self.p, self.dst, self.send, self.recv, self.local = p, dst, send, recv, local
+        self.src = src.at[pl.ds(*rows), pl.ds(*cols)]
+        self.r = pl.ds(*rows)
+        self.all = pl.ds(*cols)
+        half = (cols[1] // 256) * 128 if cols[1] > 128 else 128
+        half = cols[1] - half if cols[1] - half >= half else half
+        self.h = [pl.ds(cols[0], half), pl.ds(cols[0] + half, cols[1] - half)] if cols[1] > 128 else None
+    def copy(self, k, src, dst, dev):
+        return pltpu.make_async_remote_copy(src, dst, self.send.at[k], self.recv.at[k], device_id=dev, device_id_type=MESH)
+    def own(self):
+        p = self.p
+        return pltpu.make_async_copy(self.src, self.dst.at[p.y, p.x, p.c, p.z, self.r, self.all], self.local)
+    def zs(self):
+        p = self.p
+        out = []
+        for i in range(1, p.Z):
+            out.append((self.copy(i - 1, self.src, self.dst.at[p.y, p.x, p.c, p.z, self.r, self.all], p.dev(z=(p.z + i) % p.Z)),
+                        self.dst.at[p.y, p.x, p.c, (p.z + p.Z - i) % p.Z, self.r, self.all]))
+        return [a for a, _ in out]
+    def same(self, k, ref, dev):
+        return self.copy(k, ref, ref, dev)
+    def p1(self):
+        p, d = self.p, self.dst
+        return [self.same(3, d.at[p.y, p.x, p.c, :, self.r, self.h[0]], p.dev(x=1 - p.x)),
+                self.same(4, d.at[p.y, p.x, p.c, :, self.r, self.h[1]], p.dev(y=1 - p.y))]
+    def p2(self):
+        p, d = self.p, self.dst
+        return [self.same(5, d.at[p.y, :, p.c, :, self.r, self.h[0]], p.dev(y=1 - p.y)),
+                self.same(6, d.at[:, p.x, p.c, :, self.r, self.h[1]], p.dev(x=1 - p.x))]
+    def c0(self):
+        p, d = self.p, self.dst
+        return [self.same(7, d.at[p.y, p.x, p.c, :, self.r, self.all], p.dev(c=1 - p.c))]
+    def c1(self):
+        p, d = self.p, self.dst
+        o = p.dev(c=1 - p.c)
+        return [self.same(8, d.at[p.y, 1 - p.x, p.c, :, self.r, self.h[0]], o),
+                self.same(9, d.at[1 - p.y, p.x, p.c, :, self.r, self.h[1]], o)]
+    def c2(self):
+        p, d = self.p, self.dst
+        o = p.dev(c=1 - p.c)
+        return [self.same(10, d.at[1 - p.y, :, p.c, :, self.r, self.h[0]], o),
+                self.same(11, d.at[:, 1 - p.x, p.c, :, self.r, self.h[1]], o)]
+
+def start(cs):
+    for c in cs: c.start()
+def wait_recv(cs):
+    for c in cs: c.wait_recv()
+def wait_send(cs):
+    for c in cs: c.wait_send()
+
+def gather_kernel(grid, units, nin, *refs):
+    ins, outs = refs[:nin], refs[nin:2 * nin]
+    send, recv, local = refs[2 * nin:]
+    p = Place(grid)
+    barrier(p)
+    U = len(units)
+    gs = [Gather(p, ins[i], outs[i], rows, cols, send.at[u], recv.at[u], local.at[u]) for u, (i, rows, cols) in enumerate(units)]
+    for s in range(U + 4):
+        if s < U:
+            gs[s].own().start(); start(gs[s].zs())
+        if 0 <= s - 1 < U:
+            g = gs[s - 1]; g.own().wait(); wait_recv(g.zs()); start(g.p1()); start(g.c0())
+        if 0 <= s - 2 < U:
+            g = gs[s - 2]; wait_recv(g.p1()); start(g.p2()); start(g.c1())
+        if 0 <= s - 3 < U:
+            g = gs[s - 3]; wait_recv(g.p2()); start(g.c2())
+        if 0 <= s - 4 < U:
+            g = gs[s - 4]
+            wait_recv(g.c0() + g.c1() + g.c2())
+            wait_send(g.zs() + g.p1() + g.p2() + g.c0() + g.c1() + g.c2())
+
+def gather(grid, shards, units, collective_id):
+    n = len(shards)
+    outs = pl.pallas_call(
+        functools.partial(gather_kernel, grid, units, n),
+        out_shape=[jax.ShapeDtypeStruct(tuple(grid) + s.shape, s.dtype) for s in shards],
+        in_specs=[pl.BlockSpec(memory_space=pl.ANY)] * n,
+        out_specs=[pl.BlockSpec(memory_space=pl.ANY)] * n,
+        scratch_shapes=[pltpu.SemaphoreType.DMA((len(units), 12)), pltpu.SemaphoreType.DMA((len(units), 12)), pltpu.SemaphoreType.DMA((len(units),))],
+        compiler_params=pltpu.CompilerParams(collective_id=collective_id, has_side_effects=True),
+        name="gather",
+    )(*shards)
+    return [o.reshape(-1, s.shape[-1]) for o, s in zip(outs, shards)]
+
+class Scatter:
+    def __init__(self, p, u, slot, src, out, rows, cols, bufs, sems):
+        self.p, self.u, self.slot = p, u, slot
+        self.rb0, self.rb1, self.rb2, self.rb3, self.own, self.fin = bufs
+        self.send, self.recv, self.lsem = sems
+        self.src, self.out = src, out
+        self.r, self.cols = pl.ds(*rows), pl.ds(*cols)
+        w = cols[1]
+        half = w - (w // 256) * 128
+        self.w, self.h = w, [pl.ds(0, half), pl.ds(half, w - half)]
+        self.hs = [half, w - half]
+        self.R = rows[1]
+        self.rows, self.colsl = rows, cols
+        self.all = pl.ds(0, w)
+        self.P = self.own.at[slot]
+    def copy(self, k, src, dst, dev):
+        return pltpu.make_async_remote_copy(src, dst, self.send.at[self.u, k], self.recv.at[self.u, k], device_id=dev, device_id_type=MESH)
+    def r0(self):
+        p = self.p
+        return [self.copy(0, self.src.at[:, :, 1 - p.c, :, self.r, self.cols], self.rb0.at[self.u, :, :, :, :, self.all], p.dev(c=1 - p.c))]
+    def load_own(self):
+        p = self.p
+        return pltpu.make_async_copy(self.src.at[:, :, p.c, :, self.r, self.cols], self.P.at[..., self.all], self.lsem.at[self.u, 0])
+    def load_r0(self, tmp):
+        return pltpu.make_async_copy(self.rb0.at[self.u, :, :, :, :, self.all], tmp.at[..., self.all], self.lsem.at[self.u, 1])
+    def add0(self, tmp):
+        P, w, Z = self.P, self.w, self.p.Z
+        @pl.loop(0, P.shape[0] * P.shape[1] * Z)
+        def _(i):
+            a, b, d = i // (P.shape[1] * Z), (i // Z) % P.shape[1], i % Z
+            P[a, b, d, :, pl.ds(0, w)] = (P[a, b, d, :, pl.ds(0, w)].astype(jnp.float32) + tmp[a, b, d, :, pl.ds(0, w)].astype(jnp.float32)).astype(jnp.bfloat16)
+    def r1(self):
+        p, P = self.p, self.P
+        return [self.copy(1, P.at[1 - p.y, :, :, :, self.h[0]], self.rb1.at[self.u, 0, :, :, :, pl.ds(0, self.hs[0])], p.dev(y=1 - p.y)),
+                self.copy(2, P.at[:, 1 - p.x, :, :, self.h[1]], self.rb1.at[self.u, 1, :, :, :, pl.ds(0, self.hs[1])], p.dev(x=1 - p.x))]
+    def add1(self):
+        p, P, Z = self.p, self.P, self.p.Z
+        @pl.loop(0, 2 * Z)
+        def _(i):
+            b, d = i // Z, i % Z
+            P[p.y, b, d, :, self.h[0]] = (P[p.y, b, d, :, self.h[0]].astype(jnp.float32) + self.rb1[self.u, 0, b, d, :, pl.ds(0, self.hs[0])].astype(jnp.float32)).astype(jnp.bfloat16)
+            P[b, p.x, d, :, self.h[1]] = (P[b, p.x, d, :, self.h[1]].astype(jnp.float32) + self.rb1[self.u, 1, b, d, :, pl.ds(0, self.hs[1])].astype(jnp.float32)).astype(jnp.bfloat16)
+    def r2(self):
+        p, P = self.p, self.P
+        return [self.copy(3, P.at[p.y, 1 - p.x, :, :, self.h[0]], self.rb2.at[self.u, :, :, self.h[0]], p.dev(x=1 - p.x)),
+                self.copy(4, P.at[1 - p.y, p.x, :, :, self.h[1]], self.rb2.at[self.u, :, :, self.h[1]], p.dev(y=1 - p.y))]
+    def add2(self):
+        p, P, Z = self.p, self.P, self.p.Z
+        @pl.loop(0, Z)
+        def _(d):
+            P[p.y, p.x, d, :, self.all] = (P[p.y, p.x, d, :, self.all].astype(jnp.float32) + self.rb2[self.u, d, :, self.all].astype(jnp.float32)).astype(jnp.bfloat16)
+    def r3(self):
+        p, P = self.p, self.P
+        return [self.copy(4 + i, P.at[p.y, p.x, (p.z + i) % p.Z, :, self.all], self.rb3.at[self.u, i - 1, :, self.all], p.dev(z=(p.z + i) % p.Z)) for i in range(1, p.Z)]
+    def add3(self, f):
+        p, P = self.p, self.P
+        s = P[p.y, p.x, p.z, :, self.all].astype(jnp.float32)
+        for i in range(p.Z - 1):
+            s = s + self.rb3[self.u, i, :, self.all].astype(jnp.float32)
+        self.fin[f, :, self.all] = s
+    def store(self, f):
+        return pltpu.make_async_copy(self.fin.at[f, :, self.all], self.out.at[pl.ds(*self.rows), self.cols], self.lsem.at[self.u, 2])
+
+def scatter_kernel(grid, units, nin, *refs):
+    ins, outs = refs[:nin], refs[nin:2 * nin]
+    rb0 = refs[2 * nin]
+    rb1, rb2, rb3, own, tmp, fin, send, recv, lsem = refs[2 * nin + 1:]
+    p = Place(grid)
+    barrier(p)
+    U, NS = len(units), own.shape[0]
+    gs = [Scatter(p, u, u % NS, ins[i], outs[i], rows, cols, (rb0, rb1, rb2, rb3, own, fin), (send, recv, lsem)) for u, (i, rows, cols) in enumerate(units)]
+    for s in range(U + 5):
+        if s < U:
+            g = gs[s]
+            start(g.r0())
+            if s >= NS:
+                pass
+            g.load_own().start()
+        if 0 <= s - 1 < U:
+            g = gs[s - 1]; t = tmp
+            wait_recv(g.r0()); g.load_r0(t).start(); g.load_own().wait(); g.load_r0(t).wait(); g.add0(t); start(g.r1())
+        if 0 <= s - 2 < U:
+            g = gs[s - 2]; wait_recv(g.r1()); wait_send(g.r1()); g.add1(); start(g.r2())
+        if 0 <= s - 3 < U:
+            g = gs[s - 3]; wait_recv(g.r2()); wait_send(g.r2()); g.add2(); start(g.r3())
+        if 0 <= s - 4 < U:
+            g = gs[s - 4]; wait_recv(g.r3()); wait_send(g.r0() + g.r3())
+            f = (s - 4) % 2
+            if s - 6 >= 0:
+                gs[s - 6].store(f).wait()
+            g.add3(f); g.store(f).start()
+    for u in range(max(0, U - 2), U):
+        gs[u].store(u % 2).wait()
+
+def scatter(grid, fulls, units, collective_id):
+    n = len(fulls)
+    A, B, C, Z = grid
+    ndev = A * B * C * Z
+    U = len(units)
+    shards = [(f.shape[0] // ndev, f.shape[1]) for f in fulls]
+    W = max(c[1] for _, _, c in units)
+    R = units[0][1][1]
+    NS = 5
+    outs = pl.pallas_call(
+        functools.partial(scatter_kernel, grid, units, n),
+        out_shape=[jax.ShapeDtypeStruct(s, jnp.float32) for s in shards] + [jax.ShapeDtypeStruct((U, A, B, Z, R, W), jnp.bfloat16)],
+        in_specs=[pl.BlockSpec(memory_space=pl.ANY)] * n,
+        out_specs=[pl.BlockSpec(memory_space=pl.ANY)] * (n + 1),
+        scratch_shapes=[
+            pltpu.VMEM((U, 2, 2, Z, R, W - (W // 256) * 128), jnp.bfloat16),
+            pltpu.VMEM((U, Z, R, W), jnp.bfloat16),
+            pltpu.VMEM((U, Z - 1, R, W), jnp.bfloat16),
+            pltpu.VMEM((NS, A, B, Z, R, W), jnp.bfloat16),
+            pltpu.VMEM((A, B, Z, R, W), jnp.bfloat16),
+            pltpu.VMEM((2, R, W), jnp.float32),
+            pltpu.SemaphoreType.DMA((U, 8)), pltpu.SemaphoreType.DMA((U, 8)), pltpu.SemaphoreType.DMA((U, 3))],
+        compiler_params=pltpu.CompilerParams(collective_id=collective_id, has_side_effects=True, vmem_limit_bytes=60 * 1024 * 1024),
+        name="scatter",
+    )(*[f.reshape(tuple(grid) + (s[0], s[1])) for f, s in zip(fulls, shards)])
+    return outs[:n]
+
+
+def window_mask(start, ends, nseq, m, queries, keys):
+    qpos = start + lax.broadcasted_iota(jnp.int32, (queries, 1), 0)
+    first = jnp.maximum(qpos - (WIN - 1), 0)
+    for k in range(nseq):
+        end = ends[m, k]
+        first = jnp.maximum(first, jnp.where(qpos >= end, end, 0))
+    kpos = start - (keys - queries) + lax.broadcasted_iota(jnp.int32, (1, keys), 1)
+    return (kpos >= first) & (kpos <= qpos)
+
+
+def softmax_rows(q, k, mask):
+    scores = lax.dot_general(q, k, (((1,), (1,)), ((), ())), preferred_element_type=jnp.float32)
+    masked = jnp.where(mask, scores, -1e30)
+    expd = jnp.exp(masked - jnp.max(masked, axis=1, keepdims=True))
+    return expd * (1.0 / jnp.sum(expd, axis=1, keepdims=True))
+
+
+def attend_kernel(nseq, start, ends, q_ref, kv_ref, o_ref):
+    m = pl.program_id(0)
+    mask = window_mask(start[m], ends, nseq, m, q_ref.shape[0], kv_ref.shape[1])
+    p = softmax_rows(q_ref[...], kv_ref[0, :, :HD], mask)
+    o_ref[...] = jnp.dot(p.astype(jnp.bfloat16), kv_ref[0, :, HD:], preferred_element_type=jnp.float32).astype(jnp.bfloat16)
+
+
+def attend(q, window, start, ends):
+    batches, keys, _ = window.shape
+    return pl.pallas_call(
+        functools.partial(attend_kernel, ends.shape[1]),
+        out_shape=jax.ShapeDtypeStruct(q.shape, jnp.bfloat16),
+        grid_spec=pltpu.PrefetchScalarGridSpec(
+            num_scalar_prefetch=2,
+            grid=(batches, H),
+            in_specs=[
+                pl.BlockSpec((BLK, HD), lambda m, h, *_: (m, h)),
+                pl.BlockSpec((1, keys, 2 * HD), lambda m, h, *_: (m, 0, 0)),
+            ],
+            out_specs=pl.BlockSpec((BLK, HD), lambda m, h, *_: (m, h)),
+        ),
+        compiler_params=pltpu.CompilerParams(vmem_limit_bytes=VMEM),
+        name="attend",
+    )(start, ends, q, window)
+
+
+def attend_back_kernel(nseq, start, ends, q_ref, kv_ref, d_ref, dq_ref, dkv_ref, dkv):
+    m, h = pl.program_id(0), pl.program_id(1)
+    mask = window_mask(start[m], ends, nseq, m, q_ref.shape[0], kv_ref.shape[1])
+    q, k, v, d = q_ref[...], kv_ref[0, :, :HD], kv_ref[0, :, HD:], d_ref[...]
+    p = softmax_rows(q, k, mask)
+    dp = lax.dot_general(d, v, (((1,), (1,)), ((), ())), preferred_element_type=jnp.float32)
+    ds = (p * (dp - jnp.sum(p * dp, axis=1, keepdims=True))).astype(jnp.bfloat16)
+    dq_ref[...] = jnp.dot(ds, k, preferred_element_type=jnp.float32).astype(jnp.bfloat16)
+    dk = lax.dot_general(ds, q, (((0,), (0,)), ((), ())), preferred_element_type=jnp.float32)
+    dv = lax.dot_general(p.astype(jnp.bfloat16), d, (((0,), (0,)), ((), ())), preferred_element_type=jnp.float32)
+
+    @pl.when(h == 0)
+    def _():
+        dkv[:, :HD] = dk
+        dkv[:, HD:] = dv
+
+    @pl.when(h > 0)
+    def _():
+        dkv[:, :HD] += dk
+        dkv[:, HD:] += dv
+
+    @pl.when(h == pl.num_programs(1) - 1)
+    def _():
+        dkv_ref[0] = dkv[...].astype(jnp.bfloat16)
+
+
+def attend_back(q, window, datt, start, ends):
+    batches, keys, _ = window.shape
+    return pl.pallas_call(
+        functools.partial(attend_back_kernel, ends.shape[1]),
+        out_shape=[jax.ShapeDtypeStruct(q.shape, jnp.bfloat16), jax.ShapeDtypeStruct(window.shape, jnp.bfloat16)],
+        grid_spec=pltpu.PrefetchScalarGridSpec(
+            num_scalar_prefetch=2,
+            grid=(batches, H),
+            in_specs=[
+                pl.BlockSpec((BLK, HD), lambda m, h, *_: (m, h)),
+                pl.BlockSpec((1, keys, 2 * HD), lambda m, h, *_: (m, 0, 0)),
+                pl.BlockSpec((BLK, HD), lambda m, h, *_: (m, h)),
+            ],
+            out_specs=[
+                pl.BlockSpec((BLK, HD), lambda m, h, *_: (m, h)),
+                pl.BlockSpec((1, keys, 2 * HD), lambda m, h, *_: (m, 0, 0)),
+            ],
+            scratch_shapes=[pltpu.VMEM((keys, 2 * HD), jnp.float32)],
+        ),
+        compiler_params=pltpu.CompilerParams(vmem_limit_bytes=VMEM),
+        name="attend_back",
+    )(start, ends, q, window, datt)
+
+
+def geglu_parts(gate):
+    c = math.sqrt(2.0 / math.pi)
+    square = gate * gate
+    t = jnp.tanh(c * gate * (1.0 + 0.044715 * square))
+    half = 0.5 * (1.0 + t)
+    value = gate * half
+    slope = half + 0.5 * gate * (1.0 - t * t) * c * (1.0 + 3 * 0.044715 * square)
+    return value, slope
+
+
+def ffn_kernel(n2_ref, n2t_ref, dy_ref, wg_ref, wu_ref, wd_ref, out_ref, dn2_ref, dwg_ref, dwu_ref, dwd_ref):
+    n2, dy = n2_ref[...], dy_ref[...]
+    wg, wu, wd = wg_ref[...], wu_ref[...], wd_ref[...]
+    f32 = jnp.float32
+    gate = jnp.dot(n2, wg, preferred_element_type=f32)
+    up = jnp.dot(n2, wu, preferred_element_type=f32)
+    value, slope = geglu_parts(gate)
+    hidden = (value * up).astype(jnp.bfloat16)
+    dh = lax.dot_general(dy, wd, (((1,), (1,)), ((), ())), preferred_element_type=f32)
+    dgate = (dh * up * slope).astype(jnp.bfloat16)
+    dup = (dh * value).astype(jnp.bfloat16)
+    out = jnp.dot(hidden, wd, preferred_element_type=f32)
+    dn2 = lax.dot_general(dgate, wg, (((1,), (1,)), ((), ())), preferred_element_type=f32)
+    dn2 += lax.dot_general(dup, wu, (((1,), (1,)), ((), ())), preferred_element_type=f32)
+    dwd_ref[...] = lax.dot_general(hidden, dy, (((0,), (0,)), ((), ())), preferred_element_type=f32).astype(jnp.bfloat16)
+    dwg_ref[...] = jnp.dot(n2t_ref[...], dgate, preferred_element_type=f32).astype(jnp.bfloat16)
+    dwu_ref[...] = jnp.dot(n2t_ref[...], dup, preferred_element_type=f32).astype(jnp.bfloat16)
+
+    @pl.when(pl.program_id(0) == 0)
+    def _():
+        out_ref[...] = out
+        dn2_ref[...] = dn2
+
+    @pl.when(pl.program_id(0) > 0)
+    def _():
+        out_ref[...] += out
+        dn2_ref[...] += dn2
+
+
+def ffn(n2, dy, wg, wu, wd, tile):
+    tok, width = n2.shape
+    hidden = wg.shape[1]
+    whole = pl.BlockSpec((tok, width), lambda i: (0, 0))
+    cols = pl.BlockSpec((width, tile), lambda i: (0, i))
+    rows = pl.BlockSpec((tile, width), lambda i: (i, 0))
+    return pl.pallas_call(
+        ffn_kernel,
+        grid=(hidden // tile,),
+        in_specs=[whole, pl.BlockSpec((width, tok), lambda i: (0, 0)), whole, cols, cols, rows],
+        out_specs=[whole, whole, cols, cols, rows],
+        out_shape=[jax.ShapeDtypeStruct((tok, width), jnp.float32)] * 2
+        + [jax.ShapeDtypeStruct(wg.shape, jnp.bfloat16), jax.ShapeDtypeStruct(wu.shape, jnp.bfloat16), jax.ShapeDtypeStruct(wd.shape, jnp.bfloat16)],
+        compiler_params=pltpu.CompilerParams(vmem_limit_bytes=VMEM),
+        name="ffn",
+    )(n2, n2.T, dy, wg, wu, wd)
+
+def place_of(perm):
+    return jnp.argsort(perm, axis=1).astype(jnp.int32)
+
+
+def windows_of(kv, perm, sources):
+    axes = ("dp", "fsdp")
+    batches, rows, cols = kv.shape
+    count = perm.shape[1]
+    part = rows // count
+    pieces = kv.reshape(batches, count, part, cols).transpose(1, 0, 2, 3)
+    spread = lax.all_to_all(pieces, axes, split_axis=0, concat_axis=0, tiled=True)
+    holder = place_of(perm)
+    block = perm[:, :, None] - (sources - 1) + jnp.arange(sources, dtype=jnp.int32)
+    source = jnp.take_along_axis(holder[:, None, :], jnp.maximum(block, 0), axis=2)
+    index = (source * batches + jnp.arange(batches, dtype=jnp.int32)[:, None, None]).transpose(1, 0, 2).reshape(-1)
+    picked = jnp.take(spread.reshape(count * batches, part, cols), index, axis=0).reshape(count, batches * sources, part, cols)
+    arrived = lax.all_to_all(picked, axes, split_axis=0, concat_axis=0, tiled=True)
+    return arrived.transpose(1, 0, 2, 3).reshape(batches, sources * rows, cols)
+
+
+def window_sums(grads, perm, sources):
+    axes = ("dp", "fsdp")
+    batches, wide, cols = grads.shape
+    rows = wide // sources
+    count = perm.shape[1]
+    part = rows // count
+    pieces = grads.reshape(batches * sources, count, part, cols).transpose(1, 0, 2, 3)
+    spread = lax.all_to_all(pieces, axes, split_axis=0, concat_axis=0, tiled=True)
+    holder = place_of(perm)
+    block = perm[:, :, None] + (sources - 1) - jnp.arange(sources, dtype=jnp.int32)
+    reader = jnp.take_along_axis(holder[:, None, :], jnp.minimum(block, count - 1), axis=2)
+    slot = jnp.arange(batches, dtype=jnp.int32)[:, None, None] * sources + jnp.arange(sources, dtype=jnp.int32)
+    index = (reader * (batches * sources) + slot).transpose(1, 0, 2)
+    picked = jnp.take(spread.reshape(count * batches * sources, part, cols), index.reshape(-1), axis=0)
+    picked = picked.reshape(count, batches, sources, part, cols).astype(jnp.float32)
+    valid = (block < count).transpose(1, 0, 2)[..., None, None]
+    summed = jnp.sum(jnp.where(valid, picked, 0.0), axis=2).astype(jnp.bfloat16)
+    arrived = lax.all_to_all(summed, axes, split_axis=0, concat_axis=0, tiled=True)
+    return arrived.transpose(1, 0, 2, 3).reshape(batches, rows, cols)
+
+
+def fast_body(grid, tokens, w_query, w_keyval, w_out, w_gate, w_up, w_down, gain_attn, gain_ffn, cotangent, block_perm, extra_len):
+    f32, bf16 = jnp.float32, jnp.bfloat16
+    batches, _, rows, width = tokens.shape
+    tok = batches * rows
+    me = lax.axis_index(("dp", "fsdp"))
+    sources = WIN // BLK + 1
+    scale = HD ** (-0.5)
+    kvw = w_keyval.shape[1]
+    gains = jnp.stack([gain_attn, gain_ffn], axis=1)
+    small = jnp.concatenate([w_keyval, jnp.pad(gains, ((0, 0), (0, 126)))], axis=1)
+    shards = [small, w_query, w_out, w_gate, w_up, w_down]
+    units = units_of(shards, width)
+    small, wq, wo, wg, wu, wd = gather(grid, shards, units, 0)
+    wkv = small[:, :kvw]
+    g1, g2 = small[:, kvw].astype(f32), small[:, kvw + 1].astype(f32)
+
+    x = tokens.reshape(tok, width).astype(f32)
+    dy = cotangent.reshape(tok, width)
+    n1, r1 = norm_rows(x, g1)
+    n1b = n1.astype(bf16)
+    query = (jnp.dot(n1b, wq, preferred_element_type=f32) * scale).astype(bf16)
+    keyval = jnp.dot(n1b, wkv, preferred_element_type=f32).astype(bf16)
+    window = windows_of(keyval.reshape(batches, rows, kvw), block_perm, sources)
+    start = lax.dynamic_slice_in_dim(block_perm, me, 1, axis=1)[:, 0] * BLK
+    ends = jnp.cumsum(extra_len + (WIN - 1), axis=1).astype(jnp.int32)
+    att = attend(query, window, start, ends)
+    mixed = x + jnp.dot(att, wo, preferred_element_type=f32)
+    n2, r2 = norm_rows(mixed, g2)
+    out, d_n2, d_wgate, d_wup, d_down = ffn(n2.astype(bf16), dy, wg, wu, wd, 512)
+    block_out = (mixed + out).astype(bf16)
+    d_mixed_norm, d_g2 = norm_back(mixed, r2, g2, d_n2)
+    d_mixed = dy.astype(f32) + d_mixed_norm
+    d_branch = d_mixed.astype(bf16)
+    d_wout = jnp.einsum("ta,td->ad", att, d_branch, preferred_element_type=f32).astype(bf16)
+    d_att = jnp.einsum("td,ad->ta", d_branch, wo, preferred_element_type=f32).astype(bf16)
+    d_query, d_window = attend_back(query, window, d_att, start, ends)
+    d_keyval = window_sums(d_window, block_perm, sources).reshape(tok, kvw)
+    d_wquery = (jnp.einsum("td,ta->da", n1b, d_query, preferred_element_type=f32) * scale).astype(bf16)
+    d_wkeyval = jnp.einsum("td,tc->dc", n1b, d_keyval, preferred_element_type=f32)
+    d_n1 = jnp.einsum("ta,da->td", d_query, wq, preferred_element_type=f32) * scale
+    d_n1 = d_n1 + jnp.einsum("tc,dc->td", d_keyval, wkv, preferred_element_type=f32)
+    d_x_norm, d_g1 = norm_back(x, r1, g1, d_n1)
+    grad_tokens = (d_mixed + d_x_norm).astype(bf16)
+    d_gains = jnp.pad(jnp.stack([d_g1, d_g2], axis=1), ((0, 0), (0, 126)))
+    d_small = jnp.concatenate([d_wkeyval, d_gains], axis=1).astype(bf16)
+    small, dq, do, dg, du, dd = scatter(grid, [d_small, d_wquery, d_wout, d_wgate, d_wup, d_down], units, 1)
+    return (
+        block_out.reshape(tokens.shape),
+        grad_tokens.reshape(tokens.shape),
+        dq,
+        small[:, :kvw],
+        do,
+        dg,
+        du,
+        dd,
+        small[:, kvw],
+        small[:, kvw + 1],
+    )
+
+
+def units_of(shards, width):
+    rows = min(s.shape[0] for s in shards)
+    units = []
+    for i, s in enumerate(shards):
+        for r in range(0, s.shape[0], rows):
+            for c in range(0, s.shape[1], width):
+                units.append((i, (r, rows), (c, min(width, s.shape[1] - c))))
+    return units
+
+
 def solution(mesh):
+    count = mesh.shape["dp"] * mesh.shape["fsdp"]
+    grid = (2, 2, 2, mesh.shape["fsdp"])
+    whole_tiles = mesh.shape["dp"] == 8 and 1536 % (16 * count) == 0
+    run = functools.partial(fast_body, grid) if whole_tiles else body
     placed = (
         P(None, ("dp", "fsdp"), None, None),
         P(("dp", "fsdp"), None),
@@ -241,7 +744,7 @@
         P(),
     )
     return jax.shard_map(
-        body,
+        run,
         mesh=mesh,
         in_specs=placed,
         out_specs=(

time: 2190 us -> 884 us (0.40)
  waiting for transfers between devices: 1490 us -> 106 us
  Pallas kernels: 0 us -> 622 us
  matrix products: 347 us -> 44.4 us
  starting transfers between devices: 137 us -> 36.2 us
  blocking collectives: 83.2 us -> 0 us
  local copies, waits for them, and re-layouts: 66.3 us -> 41 us
    reduce_scatter x6 -> x0, waiting for transfers between devices: 990 us -> none  [body(): lax.psum_scatter(totals, ('dp', 'fsdp'), scatter_dimension=0, tiled=True)]
    pallas_call x0 -> x5, Pallas kernels: none -> 622 us  [the longest x1 248 us: scatter(): pl.pallas_call(functools.partial(scatter_kernel, grid, units, n), out_sha...]
    dot_general x48 -> x9, matrix products: 347 us -> 44.4 us  [the longest x1 6.81 us: fast_body(): jnp.einsum('td,ta->da', n1b, d_query, preferred_element_type=f32) * scale]
    all_gather x6 -> x0, waiting for transfers between devices: 187 us -> none  [the longest x1 93.5 us: body(): lax.all_gather(shards[5], ('dp', 'fsdp'), axis=0, tiled=True)]
    all_to_all x16 -> x4, waiting for transfers between devices: 230 us -> 106 us  [the longest x1 49.7 us: windows_of(): lax.all_to_all(picked, axes, split_axis=0, concat_axis=0, tiled=True)]
    unnamed x2 -> x0, blocking collectives: 83.2 us -> none
    ppermute x16 -> x0, waiting for transfers between devices: 74.4 us -> none  [shifted(): lax.ppermute(value, axis, [(source, source + steps) for source in range(l...]
    all_to_all x16 -> x4, starting transfers between devices: 101 us -> 36.2 us  [the longest x1 15.5 us: window_sums(): lax.all_to_all(pieces, axes, split_axis=0, concat_axis=0, tiled=True)]
  transfers between devices with their start and end apart: 44 -> 4, of which waited for: 30 -> 4; matrix products, arithmetic and copies ran while one was open for 14% -> 4% of each run, Pallas kernels for 0% -> 0%
where the time goes in v1:
time: 884 us; the launch traced here: 879 us
  Pallas kernels  622 us (70%)
  waiting for transfers between devices  106 us (12%)
  matrix products  44.4 us (5%)
  local copies, waits for them, and re-layouts  41 us (5%)
  starting transfers between devices  36.2 us (4%)
  other arithmetic  28.9 us (3%)
    pallas_call x1, Pallas kernels, scatter(): pl.pallas_call(functools.partial(scatter_kernel, grid, units, n), out_sha...  248 us
    pallas_call x1, Pallas kernels, gather(): pl.pallas_call(functools.partial(gather_kernel, grid, units, n), out_shap...  246 us
    pallas_call x1, Pallas kernels, ffn(): pl.pallas_call(ffn_kernel, grid=(hidden // tile,), in_specs=[whole, pl.Bl...  83 us
    all_to_all x1, waiting for transfers between devices, windows_of(): lax.all_to_all(picked, axes, split_axis=0, concat_axis=0, tiled=True)  49.7 us
    all_to_all x1, waiting for transfers between devices, window_sums(): lax.all_to_all(pieces, axes, split_axis=0, concat_axis=0, tiled=True)  46 us
    pallas_call x1, Pallas kernels, attend_back(): pl.pallas_call(functools.partial(attend_back_kernel, ends.shape[1]), out_...  26.3 us
    pallas_call x1, Pallas kernels, attend(): pl.pallas_call(functools.partial(attend_kernel, ends.shape[1]), out_shape...  18.4 us
  transfers between devices with their start and end apart: 4, of which 4 were waited for; matrix products, arithmetic and copies ran while one was open for 4% of the time, Pallas kernels for 0%

profile of v1, /device:TPU:0, one launch (start us, length us, event | category | flops | bytes accessed | tf_op | source)
XLA Modules:
  0.0 879.4 jit_solution(5521437636294240704)
XLA Ops:
  3.0 246.5 %gather.30 = (bf16[2,2,2,4,48,640]{5,4,3,2,1,0:T(8,128)(2,1)}, bf16[2,2,2,4,48,1536]{5,4,3,2,1,0:T(8,128)(2,1)}, bf16[2,2,2,4,48,1536]{5,4,3,2,1,0:T(8,128)(2,1)...) custom-call(bf16[48,640]{1,0:T(8,128)(2,1)} %fusion.24.refs_0_, ...), custom_call_target="tpu_custom_call" | custom-call | tf_op jit(solution)/shard_map/gather/pallas_call | solution.py:334
  254.6 12.0 %all-to-all-start = ((bf16[32,2,8,512]{3,2,1,0:T(8,128)(2,1)}), bf16[32,2,8,512]{3,2,1,0:T(8,128)(2,1)S(1)}, u32[]{:S(2)}, u32[]{:S(2)}) async-start(bf16[32,2,8,512]{3,2,1,0:T(8,128)(2,1)} %bitcast.112), calls=%async_computation | async-start | bytes 1048576 | tf_op jit(solution)/shard_map/all_to_all | solution.py:626
  267.7 3.1 gather_fusion.2
  271.5 9.3 %all-to-all-done = bf16[32,2,8,512]{3,2,1,0:T(8,128)(2,1)S(1)} async-done(((bf16[32,2,8,512]{3,2,1,0:T(8,128)(2,1)}), bf16[32,2,8,512]{3,2,1,0:T(8,128)(2,1)S(1)}, u32[]{:S(2)}, u32[]{:S(2)}) %all-to-all-start) | async-done | bytes 524320 | tf_op jit(solution)/shard_map/all_to_all | solution.py:626
  280.9 3.0 gather_fusion
  283.9 3.1 broadcast_select_fusion
  287.0 4.2 all-to-all-start.1
  294.5 6.0 fusion.14.q_ref
  300.5 49.7 %all-to-all-done.1 = bf16[32,10,8,512]{3,2,1,0:T(8,128)(2,1)} async-done(((bf16[32,10,8,512]{3,2,1,0:T(8,128)(2,1)}), bf16[32,10,8,512]{3,2,1,0:T(8,128)(2,1)}, u32[]{:S(2)}, u32[]{:S(2)}) %all-to-all-start.1) | async-done | bytes 2621472 | tf_op jit(solution)/shard_map/all_to_all | solution.py:632
  350.2 3.5 copy.58
  353.7 18.4 %attend.1 = bf16[512,1536]{1,0:T(8,128)(2,1)} custom-call(s32[2]{0:T(128)} %multiply_reduce_fusion.3.start, s32[2,4]{1,0:T(2,128)} %reduce_window_sum.11.ends, bf16[512,1536]{1,0:T(8,128)(2,1)} %fusion.14.q_ref, bf16[2,1280,512]{2,1,0:T(8,128)(2,1)} %bitcast.114), custom_call_target="tpu_custom_call" | custom-call | tf_op jit(solution)/shard_map/attend/pallas_call | solution.py:493
  372.1 6.0 multiply_reduce_fusion.2
  381.0 2.6 copy.60.n2t_ref
  383.6 83.0 %ffn.1 = (f32[512,1536]{1,0:T(8,128)}, f32[512,1536]{1,0:T(8,128)}, bf16[1536,4608]{1,0:T(8,128)(2,1)}, bf16[1536,4608]{1,0:T(8,128)(2,1)}, bf16[4608,1536]{1,0:T(8,128)(2,1)}) custom-call(bf16[512,1536]{1,0:T(8,128)(2,1)} %multiply_convert_fusion.n2_ref, bf16[1536,512]{1,0:T(8,128)(2,1)} %copy.60.n2t_ref, bf16[512,1536]{1,0:T(8,128)(2,1)} %bitcast.125, ...), custom_call_target="tpu_custom_call" | custom-call | tf_op jit(solution)/shard_map/ffn/pallas_call | solution.py:605
  466.6 2.9 multiply_reduce_fusion
  469.9 4.0 subtract_add_fusion
  475.6 3.8 convolution_convert_fusion.1.d_ref
  479.4 26.3 %attend_back.1 = (bf16[512,1536]{1,0:T(8,128)(2,1)}, bf16[2,1280,512]{2,1,0:T(8,128)(2,1)}) custom-call(s32[2]{0:T(128)} %multiply_reduce_fusion.3.start, s32[2,4]{1,0:T(2,128)} %reduce_window_sum.11.ends, bf16[512,1536]{1,0:T(8,128)(2,1)} %fusion.14.q_ref, bf16[2,1280,512]{2,1,0:T(8,128)(2,1)} %bitcast.115, bf16[512,1536]{1,0:T(8,128)(2,1)} %convolution_convert_fusion.1.d_ref), custom_call_target="tpu_custom_call" | custom-call | tf_op jit(solution)/shard_map/attend_back/pallas_call | solution.py:538
  505.7 3.6 copy.77
  509.3 15.5 %all-to-all-start.2 = ((bf16[32,10,8,512]{3,2,1,0:T(8,128)(2,1)}), bf16[32,10,8,512]{3,2,1,0:T(8,128)(2,1)}, u32[]{:S(2)}, u32[]{:S(2)}) async-start(bf16[32,10,8,512]{3,2,1,0:T(8,128)(2,1)} %bitcast.111), calls=%async_computation.2 | async-start | bytes 5242880 | tf_op jit(solution)/shard_map/all_to_all | solution.py:643
  524.9 3.1 gather_fusion.3
  528.7 2.9 copy.66
  531.8 5.8 convolution_convert_fusion
  537.6 46.0 %all-to-all-done.2 = bf16[32,10,8,512]{3,2,1,0:T(8,128)(2,1)} async-done(((bf16[32,10,8,512]{3,2,1,0:T(8,128)(2,1)}), bf16[32,10,8,512]{3,2,1,0:T(8,128)(2,1)}, u32[]{:S(2)}, u32[]{:S(2)}) %all-to-all-start.2) | async-done | bytes 2621472 | tf_op jit(solution)/shard_map/all_to_all | solution.py:643
  583.5 2.9 gather_fusion.1
  586.4 2.4 select_reduce_fusion
  588.8 4.5 all-to-all-start.3
  593.3 6.8 fusion
  600.1 6.8 convolution_multiply_fusion.1
  607.7 6.2 fusion.13
  619.2 247.7 %scatter.1 = (f32[48,640]{1,0:T(8,128)}, f32[48,1536]{1,0:T(8,128)}, f32[48,1536]{1,0:T(8,128)}, f32[48,4608]{1,0:T(8,128)}, f32[48,4608]{1,0:T(8,128)}, /*index...) custom-call(bf16[2,2,2,4,48,640]{5,4,3,2,1,0:T(8,128)(2,1)} %pad_maximum_fusion.refs_0_, ...), custom_call_target="tpu_custom_call" | custom-call | tf_op jit(solution)/shard_map/scatter/pallas_call | solution.py:448
  870.0 5.0 fusion.10
  (112 shorter events, 31.5 us)
Async XLA Ops:
  0.6 250.4 %copy-start = (bf16[2,1,256,1536]{3,2,1,0:T(8,128)(2,1)S(1)}, bf16[2,1,256,1536]{3,2,1,0:T(8,128)(2,1)}, u32[]{:S(2)}) copy-start(bf16[2,1,256,1536]{3,2,1,0:T(8,128)(2,1)} %param.14) | copy-start | bytes 4718596
  251.0 1.6 copy-start.13
  252.6 1.1 copy-start.8
  252.6 14.0 %copy-start.16 = (s32[2,32]{1,0:T(2,128)S(1)}, s32[2,32]{1,0:T(2,128)}, u32[]{:S(2)}) copy-start(s32[2,32]{1,0:T(2,128)} %param.24) | copy-start | bytes 772
  254.6 26.3 %all-to-all-start = ((bf16[32,2,8,512]{3,2,1,0:T(8,128)(2,1)}), bf16[32,2,8,512]{3,2,1,0:T(8,128)(2,1)S(1)}, u32[]{:S(2)}, u32[]{:S(2)}) async-start(bf16[32,2,8,512]{3,2,1,0:T(8,128)(2,1)} %bitcast.112), calls=%async_computation | async-start | bytes 1048576 | tf_op jit(solution)/shard_map/all_to_all | solution.py:626
  287.0 4.2 copy-start.18
  287.0 63.2 %all-to-all-start.1 = ((bf16[32,10,8,512]{3,2,1,0:T(8,128)(2,1)}), bf16[32,10,8,512]{3,2,1,0:T(8,128)(2,1)}, u32[]{:S(2)}, u32[]{:S(2)}) async-start(bf16[32,10,8,512]{3,2,1,0:T(8,128)(2,1)} %broadcast_select_fusion), calls=%async_computation.1 | async-start | bytes 5242880 | tf_op jit(solution)/shard_map/all_to_all | solution.py:632
  293.3 1.1 copy-start.6
  466.6 2.9 copy-start.2
  466.6 3.3 copy-start.5
  466.6 9.0 %slice-start = ((s8[4718592]{0:T(1024)(128)(4,1)}), s8[4194304]{0:T(1024)(128)(4,1)S(1)}, s32[]{:S(2)}) async-start(s8[4718592]{0:T(1024)(128)(4,1)} %bitcast.149), calls=%async_computation.4 | async-start | bytes 8388608
  469.9 5.7 slice-start.1
  473.9 1.7 copy-start.3
  509.3 74.2 %all-to-all-start.2 = ((bf16[32,10,8,512]{3,2,1,0:T(8,128)(2,1)}), bf16[32,10,8,512]{3,2,1,0:T(8,128)(2,1)}, u32[]{:S(2)}, u32[]{:S(2)}) async-start(bf16[32,10,8,512]{3,2,1,0:T(8,128)(2,1)} %bitcast.111), calls=%async_computation.2 | async-start | bytes 5242880 | tf_op jit(solution)/shard_map/all_to_all | solution.py:643
  528.1 3.7 copy-start.4
  588.8 18.9 %all-to-all-start.3 = ((bf16[32,2,8,512]{3,2,1,0:T(8,128)(2,1)}), bf16[32,2,8,512]{3,2,1,0:T(8,128)(2,1)S(1)}, u32[]{:S(2)}, u32[]{:S(2)}) async-start(bf16[32,2,8,512]{3,2,1,0:T(8,128)(2,1)} %select_reduce_fusion), calls=%async_computation.3 | async-start | bytes 1048576 | tf_op jit(solution)/shard_map/all_to_all | solution.py:653
  593.3 6.8 copy-start.19
  600.1 7.6 copy-start.1
  607.7 6.3 copy-start.12
  607.7 7.8 copy-start.7
  619.2 250.8 %copy-start.17 = (f32[512]{0:T(512)S(1)}, f32[512]{0:T(512)}, u32[]{:S(2)}) copy-start(f32[512]{0:T(512)} %get-tuple-element.84) | copy-start | bytes 6148
  870.0 5.1 copy-start.15
  870.0 5.8 copy-start.14
  870.0 6.5 copy-start.11
  875.1 2.4 copy-start.10
  875.1 3.3 copy-start.9

commit v2 on v1

--- a/solution.py
+++ b/solution.py
@@ -613,6 +613,248 @@
         name="ffn",
     )(n2, n2.T, dy, wg, wu, wd)
 
+
+class Exchange:
+    def __init__(self, p, count, send, recv, local):
+        self.count, self.send, self.recv, self.local = count, send, recv, local
+        self.me = (p.y * 8 + p.x * 4 + p.c * 2) // 2 * p.Z + p.z
+        self.Z = p.Z
+        self.groups = BLK // 16
+        self.wide = 2 * HD * self.groups // count
+
+    def piece(self, d):
+        return d % self.groups, pl.ds(pl.multiple_of((d // self.groups) * self.wide, self.wide), self.wide)
+
+    def dev(self, d):
+        return (d // self.Z, d % self.Z)
+
+    def copy(self, off, src, dst):
+        t = lax.rem(self.me + off, self.count)
+        return pltpu.make_async_remote_copy(
+            src(t), dst(t), self.send.at[off - 1], self.recv.at[off - 1], device_id=self.dev(t), device_id_type=MESH
+        )
+
+    def begin(self, src, dst):
+        @pl.loop(1, self.count)
+        def _(off):
+            self.copy(off, src, dst).start()
+
+        pltpu.make_async_copy(src(self.me), dst(self.me), self.local).start()
+
+    def end(self, src, dst):
+        pltpu.make_async_copy(src(self.me), dst(self.me), self.local).wait()
+
+        @pl.loop(1, self.count)
+        def _(off):
+            self.copy(off, src, dst).wait()
+
+
+def barrier_all(p, count):
+    sem = pltpu.get_barrier_semaphore()
+    me = (p.y * 4 + p.x * 2 + p.c) * p.Z + p.z
+
+    @pl.loop(1, count)
+    def _(off):
+        t = lax.rem(me + off, count)
+        pl.semaphore_signal(sem, inc=1, device_id=(t // p.Z, t % p.Z), device_id_type=MESH)
+
+    pl.semaphore_wait(sem, count - 1)
+
+
+def gather_steps(gs):
+    U = len(gs)
+    steps = []
+
+    def first(g):
+        g.own().start()
+        start(g.zs())
+
+    def second(g):
+        g.own().wait()
+        wait_recv(g.zs())
+        start(g.p1())
+        start(g.c0())
+
+    def third(g):
+        wait_recv(g.p1())
+        start(g.p2())
+        start(g.c1())
+
+    def fourth(g):
+        wait_recv(g.p2())
+        start(g.c2())
+
+    def fifth(g):
+        wait_recv(g.c0() + g.c1() + g.c2())
+        wait_send(g.zs() + g.p1() + g.p2() + g.c0() + g.c1() + g.c2())
+
+    for s in range(U + 4):
+        for lag, f in enumerate((first, second, third, fourth, fifth)):
+            if 0 <= s - lag < U:
+                steps.append(((lag, s - lag), functools.partial(f, gs[s - lag])))
+    return steps
+
+
+def forward_kernel(grid, units, nseq, sources, kvw, *refs):
+    f32, bf16 = jnp.float32, jnp.bfloat16
+    n = 6
+    start_ref, ends_ref, index_ref, x_ref = refs[:4]
+    ins, refs = refs[4 : 4 + n], refs[4 + n :]
+    fulls, refs = refs[:n], refs[n:]
+    n1_ref, q_ref, win_ref, att_ref, mixed_ref, n2_ref, gains_ref, refs = *refs[:7], refs[7:]
+    wbuf, small, kv, got, picked, send, recv, local, xsend, xrecv, xlocal, lsem = refs
+    p = Place(grid)
+    A, B, C, Z = grid
+    count = A * B * C * Z
+    tok, width = x_ref.shape
+    batches = tok // BLK
+    barrier_all(p, count)
+    gs = [Gather(p, ins[i], fulls[i], rows, cols, send.at[u], recv.at[u], local.at[u]) for u, (i, rows, cols) in enumerate(units)]
+    steps = gather_steps(gs)
+    last = {i: max(u for u, (j, _, _) in enumerate(units) if j == i) for i in range(n)}
+    at = [0]
+
+    def advance(count_=1):
+        for _ in range(count_):
+            if at[0] < len(steps):
+                steps[at[0]][1]()
+                at[0] += 1
+
+    def advance_to(i):
+        mark = [k for k, (label, _) in enumerate(steps) if label == (4, last[i])][0]
+        while at[0] <= mark:
+            advance()
+
+    def load(i, dst, sem):
+        return pltpu.make_async_copy(fulls[i], dst, lsem.at[sem])
+
+    advance(5)
+    x = x_ref[...].astype(f32)
+    normed = x * lax.rsqrt(jnp.mean(x * x, axis=-1, keepdims=True) + EPS)
+    mixed_ref[...] = normed
+    advance_to(0)
+    load(0, small, 0).start()
+    load(0, small, 0).wait()
+    gains = small[..., kvw:].reshape(width, 128).astype(f32).T
+    gains_ref[...] = gains[:8]
+    n1_ref[...] = (mixed_ref[...] * gains[0:1]).astype(bf16)
+    ex1 = Exchange(p, count, xsend.at[0], xrecv.at[0], xlocal.at[0])
+    ex2 = Exchange(p, count, xsend.at[1], xrecv.at[1], xlocal.at[1])
+
+    kv_value = jnp.dot(n1_ref[...], small[..., :kvw].reshape(width, kvw), preferred_element_type=f32).astype(bf16)
+    kv[...] = kv_value.reshape(kv.shape)
+
+    def src1(t):
+        g, c = ex1.piece(t)
+        return kv.at[:, g, :, c]
+
+    def dst1(t):
+        return got.at[ex1.me]
+
+    ex1.begin(src1, dst1)
+    advance_to(1)
+    load(1, wbuf, 1).start()
+    ex1.end(src1, dst1)
+
+    @pl.loop(0, count)
+    def _(t):
+        for m in range(batches):
+            for i in range(sources):
+                picked[t, m, i] = got[index_ref[t, m * sources + i], m]
+
+    def src2(t):
+        return picked.at[t]
+
+    def dst2(t):
+        g, c = ex2.piece(ex2.me)
+        return win_ref.at[:, :, g, :, c]
+
+    ex2.begin(src2, dst2)
+    load(1, wbuf, 1).wait()
+    tile = 512
+    for j in range(0, width, tile):
+        w = wbuf[..., j : j + tile].reshape(width, tile)
+        q_ref[:, j : j + tile] = (jnp.dot(n1_ref[...], w, preferred_element_type=f32) * (HD**-0.5)).astype(bf16)
+        advance()
+    advance_to(2)
+    load(2, wbuf, 2).start()
+    advance(10)
+    ex2.end(src2, dst2)
+    for m in range(batches):
+        mask = window_mask(start_ref[m], ends_ref, nseq, m, BLK, sources * BLK)
+        for h0 in range(0, H, 2):
+
+            @pl.loop(h0, h0 + 2)
+            def _(h):
+                cols = pl.ds(pl.multiple_of(h * HD, HD), HD)
+                rows = pl.ds(m * BLK, BLK)
+                mask = window_mask(start_ref[m], ends_ref, nseq, m, BLK, sources * BLK)
+                k = win_ref[m, :, :, :, :HD].reshape(sources * BLK, HD)
+                v = win_ref[m, :, :, :, HD:].reshape(sources * BLK, HD)
+                prob = softmax_rows(q_ref[rows, cols], k, mask)
+                att_ref[rows, cols] = jnp.dot(prob.astype(bf16), v, preferred_element_type=f32).astype(bf16)
+
+            advance(2)
+    load(2, wbuf, 2).wait()
+    for j in range(0, width, tile):
+        w = wbuf[..., j : j + tile].reshape(width, tile)
+        mixed_ref[:, j : j + tile] = x_ref[:, j : j + tile].astype(f32) + jnp.dot(att_ref[...], w, preferred_element_type=f32)
+        advance()
+    mixed = mixed_ref[...]
+    inverse = lax.rsqrt(jnp.mean(mixed * mixed, axis=-1, keepdims=True) + EPS)
+    n2_ref[...] = (mixed * inverse * gains_ref[1:2]).astype(bf16)
+    while at[0] < len(steps):
+        advance()
+
+
+def forward(grid, shards, units, x, start, ends, index, sources, kvw, collective_id):
+    A, B, C, Z = grid
+    count = A * B * C * Z
+    tok, width = x.shape
+    batches = tok // BLK
+    bf16 = jnp.bfloat16
+    groups = BLK // 16
+    wide = 2 * HD * groups // count
+    rows = shards[1].shape[0]
+    U = len(units)
+    any_, vmem, smem = (pl.BlockSpec(memory_space=s) for s in (pl.ANY, pltpu.VMEM, pltpu.SMEM))
+    dma = pltpu.SemaphoreType.DMA
+    sds = jax.ShapeDtypeStruct
+    outs = pl.pallas_call(
+        functools.partial(forward_kernel, grid, units, ends.shape[1], sources, kvw),
+        out_shape=[sds(tuple(grid) + s.shape, s.dtype) for s in shards]
+        + [
+            sds((tok, width), bf16),
+            sds((tok, width), bf16),
+            sds((batches, sources, groups, 16, 2 * HD), bf16),
+            sds((tok, width), bf16),
+            sds((tok, width), jnp.float32),
+            sds((tok, width), bf16),
+            sds((8, width), jnp.float32),
+        ],
+        in_specs=[smem, smem, smem, vmem] + [any_] * 6,
+        out_specs=[any_] * 6 + [vmem] * 7,
+        scratch_shapes=[
+            pltpu.VMEM(tuple(grid) + (rows, width), bf16),
+            pltpu.VMEM(tuple(grid) + (rows, shards[0].shape[1]), bf16),
+            pltpu.VMEM((batches, groups, 16, 2 * HD), bf16),
+            pltpu.VMEM((count, batches, 16, wide), bf16),
+            pltpu.VMEM((count, batches, sources, 16, wide), bf16),
+            dma((U, 12)),
+            dma((U, 12)),
+            dma((U,)),
+            dma((2, count - 1)),
+            dma((2, count - 1)),
+            dma((2,)),
+            dma((3,)),
+        ],
+        compiler_params=pltpu.CompilerParams(collective_id=collective_id, has_side_effects=True, vmem_limit_bytes=VMEM),
+        name="forward",
+    )(start, ends, index, x, *shards)
+    fulls = [o.reshape(-1, s.shape[-1]) for o, s in zip(outs, shards)]
+    n1, q, window, att, mixed, n2, gains = outs[6:]
+    return fulls, n1, q, window.reshape(batches, sources * BLK, 2 * HD), att, mixed, n2, gains
+
 def place_of(perm):
     return jnp.argsort(perm, axis=1).astype(jnp.int32)
 
@@ -666,23 +908,22 @@
     small = jnp.concatenate([w_keyval, jnp.pad(gains, ((0, 0), (0, 126)))], axis=1)
     shards = [small, w_query, w_out, w_gate, w_up, w_down]
     units = units_of(shards, width)
-    small, wq, wo, wg, wu, wd = gather(grid, shards, units, 0)
-    wkv = small[:, :kvw]
-    g1, g2 = small[:, kvw].astype(f32), small[:, kvw + 1].astype(f32)
-
-    x = tokens.reshape(tok, width).astype(f32)
-    dy = cotangent.reshape(tok, width)
-    n1, r1 = norm_rows(x, g1)
-    n1b = n1.astype(bf16)
-    query = (jnp.dot(n1b, wq, preferred_element_type=f32) * scale).astype(bf16)
-    keyval = jnp.dot(n1b, wkv, preferred_element_type=f32).astype(bf16)
-    window = windows_of(keyval.reshape(batches, rows, kvw), block_perm, sources)
+    holder = place_of(block_perm)
+    block = block_perm[:, :, None] - (sources - 1) + jnp.arange(sources, dtype=jnp.int32)
+    index = jnp.take_along_axis(holder[:, None, :], jnp.maximum(block, 0), axis=2)
+    index = index.transpose(1, 0, 2).reshape(-1, batches * sources)
     start = lax.dynamic_slice_in_dim(block_perm, me, 1, axis=1)[:, 0] * BLK
     ends = jnp.cumsum(extra_len + (WIN - 1), axis=1).astype(jnp.int32)
-    att = attend(query, window, start, ends)
-    mixed = x + jnp.dot(att, wo, preferred_element_type=f32)
-    n2, r2 = norm_rows(mixed, g2)
-    out, d_n2, d_wgate, d_wup, d_down = ffn(n2.astype(bf16), dy, wg, wu, wd, 512)
+    x = tokens.reshape(tok, width)
+    fulls, n1b, query, window, att, mixed, n2b, gains = forward(grid, shards, units, x, start, ends, index, sources, kvw, 0)
+    small, wq, wo, wg, wu, wd = fulls
+    wkv = small[:, :kvw]
+    g1, g2 = gains[0], gains[1]
+    x = x.astype(f32)
+    dy = cotangent.reshape(tok, width)
+    r1 = lax.rsqrt(jnp.mean(x * x, axis=-1, keepdims=True) + EPS)
+    r2 = lax.rsqrt(jnp.mean(mixed * mixed, axis=-1, keepdims=True) + EPS)
+    out, d_n2, d_wgate, d_wup, d_down = ffn(n2b, dy, wg, wu, wd, 512)
     block_out = (mixed + out).astype(bf16)
     d_mixed_norm, d_g2 = norm_back(mixed, r2, g2, d_n2)
     d_mixed = dy.astype(f32) + d_mixed_norm

time: 884 us -> 823 us (0.931)
  waiting for transfers between devices: 106 us -> 48.3 us
  Pallas kernels: 622 us -> 663 us
  starting transfers between devices: 36.2 us -> 13.1 us
  matrix products: 44.4 us -> 29.3 us
    all_to_all x2 -> x0, waiting for transfers between devices: 59.1 us -> none  [the longest x1 49.7 us: windows_of(): lax.all_to_all(picked, axes, split_axis=0, concat_axis=0, tiled=True)]
    pallas_call x2 -> x1, Pallas kernels: 265 us -> 307 us  [forward(): pl.pallas_call(functools.partial(forward_kernel, grid, units, ends.shape[...]
    all_to_all x2 -> x0, starting transfers between devices: 16.1 us -> none  [the longest x1 12 us: windows_of(): lax.all_to_all(pieces, axes, split_axis=0, concat_axis=0, tiled=True)]
    dot_general x3 -> x0, matrix products: 13 us -> none  [the longest x1 6 us: fast_body(): query = (jnp.dot(n1b, wq, preferred_element_type=f32) * scale).astype(bf16)]
  transfers between devices with their start and end apart: 4 -> 2, of which waited for: 4 -> 2; matrix products, arithmetic and copies ran while one was open for 4% -> 3% of each run, Pallas kernels for 0% -> 0%
where the time goes in v2:
time: 823 us; the launch traced here: 813 us
  Pallas kernels  663 us (81%)
  waiting for transfers between devices  48.3 us (6%)
  local copies, waits for them, and re-layouts  33.6 us (4%)
  matrix products  29.3 us (4%)
  other arithmetic  24.2 us (3%)
  starting transfers between devices  13.1 us (2%)
    pallas_call x1, Pallas kernels, forward(): pl.pallas_call(functools.partial(forward_kernel, grid, units, ends.shape[...  307 us
    pallas_call x1, Pallas kernels, scatter(): pl.pallas_call(functools.partial(scatter_kernel, grid, units, n), out_sha...  247 us
    pallas_call x1, Pallas kernels, ffn(): pl.pallas_call(ffn_kernel, grid=(hidden // tile,), in_specs=[whole, pl.Bl...  82.7 us
    all_to_all x1, waiting for transfers between devices, window_sums(): lax.all_to_all(pieces, axes, split_axis=0, concat_axis=0, tiled=True)  44.3 us
    pallas_call x1, Pallas kernels, attend_back(): pl.pallas_call(functools.partial(attend_back_kernel, ends.shape[1]), out_...  26.3 us
  transfers between devices with their start and end apart: 2, of which 2 were waited for; matrix products, arithmetic and copies ran while one was open for 3% of the time, Pallas kernels for 0%

profile of v2, /device:TPU:0, one launch (start us, length us, event | category | flops | bytes accessed | tf_op | source)
XLA Modules:
  0.0 813.4 jit_solution(11766828699655383860)
XLA Ops:
  2.1 1.4 multiply_reduce_fusion.4.refs_0_.start
  4.6 3.1 gather_fusion.1
  10.3 307.4 %forward.1 = (bf16[2,2,2,4,48,640]{5,4,3,2,1,0:T(8,128)(2,1)}, bf16[2,2,2,4,48,1536]{5,4,3,2,1,0:T(8,128)(2,1)}, bf16[2,2,2,4,48,1536]{5,4,3,2,1,0:T(8,128)(2,1)...) custom-call(s32[2]{0:T(128)} %multiply_reduce_fusion.4.refs_0_.start, ...), custom_call_target="tpu_custom_call" | custom-call | tf_op jit(solution)/shard_map/forward/pallas_call | solution.py:823
  317.7 2.7 copy.51
  320.8 0.9 slice_reduce_fusion.2
  321.7 82.7 %ffn.1 = (f32[512,1536]{1,0:T(8,128)}, f32[512,1536]{1,0:T(8,128)}, bf16[1536,4608]{1,0:T(8,128)(2,1)}, bf16[1536,4608]{1,0:T(8,128)(2,1)}, bf16[4608,1536]{1,0:T(8,128)(2,1)}) custom-call(bf16[512,1536]{1,0:T(8,128)(2,1)} %get-tuple-element.40.n2_ref, bf16[1536,512]{1,0:T(8,128)(2,1)} %bitcast.85, bf16[512,1536]{1,0:T(8,128)(2,1)} %bitcast.84, ...), custom_call_target="tpu_custom_call" | custom-call | tf_op jit(solution)/shard_map/ffn/pallas_call | solution.py:605
  404.4 2.9 multiply_reduce_fusion
  407.7 4.1 subtract_add_fusion
  411.8 1.7 copy-done.3
  413.5 3.7 convolution_convert_fusion.1.d_ref
  417.2 26.3 %attend_back.1 = (bf16[512,1536]{1,0:T(8,128)(2,1)}, bf16[2,1280,512]{2,1,0:T(8,128)(2,1)}) custom-call(s32[2]{0:T(128)} %multiply_reduce_fusion.4.refs_0_.start, s32[2,4]{1,0:T(2,128)} %reduce_window_sum.11.refs_1_.ends, bf16[512,1536]{1,0:T(8,128)(2,1)} %get-tuple-element.47.q_ref, bf16[2,1280,512]{2,1,0:T(8,128)(2,1)} %bitcast.88, ...), custom_call_target="tpu_custom_call" | custom-call | tf_op jit(solution)/shard_map/attend_back/pallas_call | solution.py:538
  443.5 3.6 copy.65
  447.1 8.3 %all-to-all-start = ((bf16[32,10,8,512]{3,2,1,0:T(8,128)(2,1)}), bf16[32,10,8,512]{3,2,1,0:T(8,128)(2,1)}, u32[]{:S(2)}, u32[]{:S(2)}) async-start(bf16[32,10,8,512]{3,2,1,0:T(8,128)(2,1)} %bitcast.75), calls=%async_computation | async-start | bytes 5242880 | tf_op jit(solution)/shard_map/all_to_all | solution.py:885
  455.6 3.1 gather_fusion.2
  460.0 5.8 fusion
  465.8 4.4 convolution_convert_fusion
  470.2 44.3 %all-to-all-done = bf16[32,10,8,512]{3,2,1,0:T(8,128)(2,1)} async-done(((bf16[32,10,8,512]{3,2,1,0:T(8,128)(2,1)}), bf16[32,10,8,512]{3,2,1,0:T(8,128)(2,1)}, u32[]{:S(2)}, u32[]{:S(2)}) %all-to-all-start) | async-done | bytes 2621472 | tf_op jit(solution)/shard_map/all_to_all | solution.py:885
  514.4 4.5 gather_fusion
  518.9 4.1 select_reduce_fusion
  523.0 4.8 all-to-all-start.1
  527.8 2.6 copy.57
  531.0 7.1 convolution_multiply_fusion.1
  538.1 4.0 all-to-all-done.1
  542.2 6.3 fusion.8
  549.1 1.0 copy.62
  550.1 2.0 convolution_convert_fusion.2
  552.2 1.5 pad_maximum_fusion.refs_0_
  553.8 246.8 %scatter.1 = (f32[48,640]{1,0:T(8,128)}, f32[48,1536]{1,0:T(8,128)}, f32[48,1536]{1,0:T(8,128)}, f32[48,4608]{1,0:T(8,128)}, f32[48,4608]{1,0:T(8,128)}, /*index...) custom-call(bf16[2,2,2,4,48,640]{5,4,3,2,1,0:T(8,128)(2,1)} %pad_maximum_fusion.refs_0_, ...), custom_call_target="tpu_custom_call" | custom-call | tf_op jit(solution)/shard_map/scatter/pallas_call | solution.py:448
  800.6 1.5 slice.21
  802.2 1.5 slice_reduce_fusion
  803.7 5.0 fusion.5
  810.2 0.9 copy.73
  (94 shorter events, 11.6 us)
Async XLA Ops:
  4.6 4.2 copy-start.19
  4.6 4.9 copy-start.21
  4.6 4.9 copy-start.22
  4.6 5.0 copy-start.14
  317.7 2.8 copy-start
  404.4 2.9 copy-start.2
  404.4 3.3 copy-start.5
  404.4 9.0 %slice-start = ((s8[4718592]{0:T(1024)(128)(4,1)}), s8[4194304]{0:T(1024)(128)(4,1)S(1)}, s32[]{:S(2)}) async-start(s8[4718592]{0:T(1024)(128)(4,1)} %bitcast.102), calls=%async_computation.2 | async-start | bytes 8388608
  407.7 5.7 slice-start.1
  411.8 1.7 copy-start.3
  447.1 67.3 %all-to-all-start = ((bf16[32,10,8,512]{3,2,1,0:T(8,128)(2,1)}), bf16[32,10,8,512]{3,2,1,0:T(8,128)(2,1)}, u32[]{:S(2)}, u32[]{:S(2)}) async-start(bf16[32,10,8,512]{3,2,1,0:T(8,128)(2,1)} %bitcast.75), calls=%async_computation | async-start | bytes 5242880 | tf_op jit(solution)/shard_map/all_to_all | solution.py:885
  455.6 3.8 copy-start.1
  455.6 4.3 copy-start.6
  459.9 5.8 copy-start.4
  460.0 5.8 copy-start.20
  523.0 19.1 %all-to-all-start.1 = ((bf16[32,2,8,512]{3,2,1,0:T(8,128)(2,1)}), bf16[32,2,8,512]{3,2,1,0:T(8,128)(2,1)S(1)}, u32[]{:S(2)}, u32[]{:S(2)}) async-start(bf16[32,2,8,512]{3,2,1,0:T(8,128)(2,1)} %select_reduce_fusion), calls=%async_computation.1 | async-start | bytes 1048576 | tf_op jit(solution)/shard_map/all_to_all | solution.py:895
  530.4 11.8 %copy-start.15 = (f32[1,2,2,128]{3,1,2,0:T(2,128)}, f32[1,2,2,128]{3,1,2,0:T(2,128)S(1)}, u32[]{:S(2)}) copy-start(f32[1,2,2,128]{3,1,2,0:T(2,128)S(1)} %copy.63) | copy-start | bytes 6148
  542.2 6.3 copy-start.11
  542.2 7.9 copy-start.7
  553.8 249.9 %copy-start.16 = (f32[1,2,2,128]{3,1,2,0:T(2,128)S(1)}, f32[1,2,2,128]{3,1,2,0:T(2,128)}, u32[]{:S(2)}) copy-start(f32[1,2,2,128]{3,1,2,0:T(2,128)} %copy-done.15) | copy-start | bytes 6148
  553.8 249.9 %copy-start.17 = (f32[512]{0:T(512)S(1)}, f32[512]{0:T(512)}, u32[]{:S(2)}) copy-start(f32[512]{0:T(512)} %multiply_multiply_fusion) | copy-start | bytes 6148
  553.8 249.9 %copy-start.18 = (f32[512]{0:T(512)S(1)}, f32[512]{0:T(512)}, u32[]{:S(2)}) copy-start(f32[512]{0:T(512)} %get-tuple-element.98) | copy-start | bytes 6148
  803.7 5.1 copy-start.13
  803.7 5.8 copy-start.12
  803.7 6.5 copy-start.10
  808.7 2.4 copy-start.9
  808.7 3.3 copy-start.8

commit v3 on v2

--- a/solution.py
+++ b/solution.py
@@ -232,15 +232,28 @@
 
 
 MESH = pl.DeviceIdType.MESH
+BF16, F32 = jnp.bfloat16, jnp.float32
+
 
 class Place:
     def __init__(self, grid):
-        self.A, self.B, self.C, self.Z = grid
+        self.grid = grid
+        self.Z = grid[3]
+        self.count = grid[0] * grid[1] * grid[2] * grid[3]
         dp = lax.axis_index("dp")
         self.z = lax.axis_index("fsdp")
         self.c = dp % 2
         self.x = (dp // 2) % 2
         self.y = dp // 4
+        self.me = dp * self.Z + self.z
+        self.half = self.z % 2
+        self.pair = self.z // 2
+        self.core = self.dev(c=1 - self.c)
+        self.xdev = self.dev(x=1 - self.x)
+        self.ydev = self.dev(y=1 - self.y)
+        self.mate = self.dev(z=self.z + 1 - 2 * self.half)
+        self.far = self.dev(z=(self.z + 2) % self.Z)
+
     def dev(self, y=None, x=None, c=None, z=None):
         y = self.y if y is None else y
         x = self.x if x is None else x
@@ -248,221 +261,318 @@
         z = self.z if z is None else z
         return ((y * 2 + x) * 2 + c, z)
 
-def barrier(p):
-    sem = pltpu.get_barrier_semaphore()
-    peers = [p.dev(c=1 - p.c), p.dev(x=1 - p.x), p.dev(y=1 - p.y)] + [p.dev(z=(p.z + i) % p.Z) for i in range(1, p.Z)]
-    for q in peers:
-        pl.semaphore_signal(sem, inc=1, device_id=q, device_id_type=MESH)
-    pl.semaphore_wait(sem, len(peers))
+    def barrier(self):
+        sem = pltpu.get_barrier_semaphore()
+
+        @pl.loop(1, self.count)
+        def _(off):
+            t = lax.rem(self.me + off, self.count)
+            pl.semaphore_signal(sem, inc=1, device_id=(t // self.Z, t % self.Z), device_id_type=MESH)
+
+        pl.semaphore_wait(sem, self.count - 1)
+
+
+def start(copies):
+    for c in copies:
+        c.start()
+
+
+def wait_recv(copies):
+    for c in copies:
+        c.wait_recv()
+
+
+def wait_send(copies):
+    for c in copies:
+        c.wait_send()
+
+
+def halves(width):
+    first = width - (width // 256) * 128
+    return [(0, first), (first, width - first)]
+
+
+class Unit:
+    def __init__(self, array, kind, rows, cols):
+        self.array, self.kind, self.rows, self.cols = array, kind, rows, cols
+        self.width = cols[1]
+
+    def shape(self, grid):
+        return grid[:2] + (grid[3] // 2 if self.kind == "rows" else grid[3],) + (self.rows[1], self.width)
+
+    def link_buffers(self, grid):
+        a, b, z, r, w = self.shape(grid)
+        h = halves(w)
+        out = [(a, b, z, r, w), (b, z, r, h[0][1]), (a, z, r, h[1][1]), (z, r, h[0][1]), (z, r, h[1][1])]
+        if self.kind == "all":
+            return out + [(z - 1, r, w)]
+        if self.kind == "cols":
+            return out + [(z // 2, r, w), (r, w)]
+        return out + [(r, w)]
+
 
 class Gather:
-    COPIES = 12
-    def __init__(self, p, src, dst, rows, cols, send, recv, local):
-        self.p, self.dst, self.send, self.recv, self.local = p, dst, send, recv, local
-        self.src = src.at[pl.ds(*rows), pl.ds(*cols)]
-        self.r = pl.ds(*rows)
-        self.all = pl.ds(*cols)
-        half = (cols[1] // 256) * 128 if cols[1] > 128 else 128
-        half = cols[1] - half if cols[1] - half >= half else half
-        self.h = [pl.ds(cols[0], half), pl.ds(cols[0] + half, cols[1] - half)] if cols[1] > 128 else None
+    def __init__(self, p, unit, src, dst, send, recv, local):
+        self.p, self.dst, self.send, self.recv, self.local, self.kind = p, dst, send, recv, local, unit.kind
+        self.r, self.all = pl.ds(*unit.rows), pl.ds(*unit.cols)
+        self.h = [pl.ds(unit.cols[0] + a, b) for a, b in halves(unit.width)]
+        self.src = (lambda half: src.at[half, self.r, self.all]) if unit.kind == "cols" else (lambda half: src.at[self.r, self.all])
+        self.spot = p.pair if unit.kind == "rows" else p.z
+
     def copy(self, k, src, dst, dev):
         return pltpu.make_async_remote_copy(src, dst, self.send.at[k], self.recv.at[k], device_id=dev, device_id_type=MESH)
+
+    def same(self, k, ref, dev):
+        return self.copy(k, ref, ref, dev)
+
+    def block(self, y, x, cols):
+        return self.dst.at[y, x, self.p.c, :, self.r, cols]
+
     def own(self):
         p = self.p
-        return pltpu.make_async_copy(self.src, self.dst.at[p.y, p.x, p.c, p.z, self.r, self.all], self.local)
-    def zs(self):
+        return pltpu.make_async_copy(self.src(p.half), self.dst.at[p.y, p.x, p.c, self.spot, self.r, self.all], self.local)
+
+    def z1(self):
         p = self.p
-        out = []
-        for i in range(1, p.Z):
-            out.append((self.copy(i - 1, self.src, self.dst.at[p.y, p.x, p.c, p.z, self.r, self.all], p.dev(z=(p.z + i) % p.Z)),
-                        self.dst.at[p.y, p.x, p.c, (p.z + p.Z - i) % p.Z, self.r, self.all]))
-        return [a for a, _ in out]
-    def same(self, k, ref, dev):
-        return self.copy(k, ref, ref, dev)
+        there = self.dst.at[p.y, p.x, p.c, self.spot, self.r, self.all]
+        if self.kind == "all":
+            return [self.copy(i - 1, self.src(0), there, p.dev(z=(p.z + i) % p.Z)) for i in range(1, p.Z)]
+        if self.kind == "cols":
+            return [self.copy(0, self.src(1 - p.half), there, p.mate)]
+        return [self.copy(0, self.src(0), there, p.far)]
+
+    def z2(self):
+        p = self.p
+        return [self.same(1, self.dst.at[p.y, p.x, p.c, pl.ds(2 * p.pair, 2), self.r, self.all], p.far)]
+
     def p1(self):
-        p, d = self.p, self.dst
-        return [self.same(3, d.at[p.y, p.x, p.c, :, self.r, self.h[0]], p.dev(x=1 - p.x)),
-                self.same(4, d.at[p.y, p.x, p.c, :, self.r, self.h[1]], p.dev(y=1 - p.y))]
+        p = self.p
+        return [self.same(3, self.block(p.y, p.x, self.h[0]), p.xdev), self.same(4, self.block(p.y, p.x, self.h[1]), p.ydev)]
+
     def p2(self):
-        p, d = self.p, self.dst
-        return [self.same(5, d.at[p.y, :, p.c, :, self.r, self.h[0]], p.dev(y=1 - p.y)),
-                self.same(6, d.at[:, p.x, p.c, :, self.r, self.h[1]], p.dev(x=1 - p.x))]
+        p, every = self.p, slice(None)
+        return [self.same(5, self.block(p.y, every, self.h[0]), p.ydev), self.same(6, self.block(every, p.x, self.h[1]), p.xdev)]
+
     def c0(self):
-        p, d = self.p, self.dst
-        return [self.same(7, d.at[p.y, p.x, p.c, :, self.r, self.all], p.dev(c=1 - p.c))]
+        p = self.p
+        return [self.same(7, self.block(p.y, p.x, self.all), p.core)]
+
     def c1(self):
-        p, d = self.p, self.dst
-        o = p.dev(c=1 - p.c)
-        return [self.same(8, d.at[p.y, 1 - p.x, p.c, :, self.r, self.h[0]], o),
-                self.same(9, d.at[1 - p.y, p.x, p.c, :, self.r, self.h[1]], o)]
+        p = self.p
+        return [self.same(8, self.block(p.y, 1 - p.x, self.h[0]), p.core), self.same(9, self.block(1 - p.y, p.x, self.h[1]), p.core)]
+
     def c2(self):
-        p, d = self.p, self.dst
-        o = p.dev(c=1 - p.c)
-        return [self.same(10, d.at[1 - p.y, :, p.c, :, self.r, self.h[0]], o),
-                self.same(11, d.at[:, 1 - p.x, p.c, :, self.r, self.h[1]], o)]
-
-def start(cs):
-    for c in cs: c.start()
-def wait_recv(cs):
-    for c in cs: c.wait_recv()
-def wait_send(cs):
-    for c in cs: c.wait_send()
-
-def gather_kernel(grid, units, nin, *refs):
-    ins, outs = refs[:nin], refs[nin:2 * nin]
-    send, recv, local = refs[2 * nin:]
-    p = Place(grid)
-    barrier(p)
-    U = len(units)
-    gs = [Gather(p, ins[i], outs[i], rows, cols, send.at[u], recv.at[u], local.at[u]) for u, (i, rows, cols) in enumerate(units)]
-    for s in range(U + 4):
-        if s < U:
-            gs[s].own().start(); start(gs[s].zs())
-        if 0 <= s - 1 < U:
-            g = gs[s - 1]; g.own().wait(); wait_recv(g.zs()); start(g.p1()); start(g.c0())
-        if 0 <= s - 2 < U:
-            g = gs[s - 2]; wait_recv(g.p1()); start(g.p2()); start(g.c1())
-        if 0 <= s - 3 < U:
-            g = gs[s - 3]; wait_recv(g.p2()); start(g.c2())
-        if 0 <= s - 4 < U:
-            g = gs[s - 4]
-            wait_recv(g.c0() + g.c1() + g.c2())
-            wait_send(g.zs() + g.p1() + g.p2() + g.c0() + g.c1() + g.c2())
-
-def gather(grid, shards, units, collective_id):
-    n = len(shards)
-    outs = pl.pallas_call(
-        functools.partial(gather_kernel, grid, units, n),
-        out_shape=[jax.ShapeDtypeStruct(tuple(grid) + s.shape, s.dtype) for s in shards],
-        in_specs=[pl.BlockSpec(memory_space=pl.ANY)] * n,
-        out_specs=[pl.BlockSpec(memory_space=pl.ANY)] * n,
-        scratch_shapes=[pltpu.SemaphoreType.DMA((len(units), 12)), pltpu.SemaphoreType.DMA((len(units), 12)), pltpu.SemaphoreType.DMA((len(units),))],
-        compiler_params=pltpu.CompilerParams(collective_id=collective_id, has_side_effects=True),
-        name="gather",
-    )(*shards)
-    return [o.reshape(-1, s.shape[-1]) for o, s in zip(outs, shards)]
+        p, every = self.p, slice(None)
+        return [self.same(10, self.block(1 - p.y, every, self.h[0]), p.core), self.same(11, self.block(every, 1 - p.x, self.h[1]), p.core)]
+
+    def stages(self):
+        def first():
+            self.own().start()
+            start(self.z1())
+
+        def second():
+            self.own().wait()
+            wait_recv(self.z1())
+            start(self.z2())
+
+        def third():
+            if self.kind == "cols":
+                wait_recv(self.z2())
+            else:
+                self.own().wait()
+                wait_recv(self.z1())
+            start(self.p1() + self.c0())
+
+        def fourth():
+            wait_recv(self.p1())
+            start(self.p2() + self.c1())
+
+        def fifth():
+            wait_recv(self.p2())
+            start(self.c2())
+
+        def last():
+            wait_recv(self.c0() + self.c1() + self.c2())
+            wait_send(self.z1() + (self.z2() if self.kind == "cols" else []) + self.p1() + self.p2() + self.c0() + self.c1() + self.c2())
+
+        return [first] + ([second] if self.kind == "cols" else []) + [third, fourth, fifth, last]
+
 
 class Scatter:
-    def __init__(self, p, u, slot, src, out, rows, cols, bufs, sems):
-        self.p, self.u, self.slot = p, u, slot
-        self.rb0, self.rb1, self.rb2, self.rb3, self.own, self.fin = bufs
-        self.send, self.recv, self.lsem = sems
-        self.src, self.out = src, out
-        self.r, self.cols = pl.ds(*rows), pl.ds(*cols)
-        w = cols[1]
-        half = w - (w // 256) * 128
-        self.w, self.h = w, [pl.ds(0, half), pl.ds(half, w - half)]
-        self.hs = [half, w - half]
-        self.R = rows[1]
-        self.rows, self.colsl = rows, cols
-        self.all = pl.ds(0, w)
-        self.P = self.own.at[slot]
+    def __init__(self, p, unit, src, out, buffers, tmp, send, recv, local):
+        self.p, self.unit, self.kind = p, unit, unit.kind
+        self.src, self.out, self.tmp, self.send, self.recv, self.local = src, out, tmp, send, recv, local
+        self.r, self.cols = pl.ds(*unit.rows), pl.ds(*unit.cols)
+        self.h = [pl.ds(a, b) for a, b in halves(unit.width)]
+        self.P, self.rest = buffers[0], buffers[1:]
+        self.spot = p.pair if unit.kind == "rows" else p.z
+        self.n = unit.shape(p.grid)[2]
+        self.part = tmp
+
     def copy(self, k, src, dst, dev):
-        return pltpu.make_async_remote_copy(src, dst, self.send.at[self.u, k], self.recv.at[self.u, k], device_id=dev, device_id_type=MESH)
+        return pltpu.make_async_remote_copy(src, dst, self.send.at[k], self.recv.at[k], device_id=dev, device_id_type=MESH)
+
     def r0(self):
         p = self.p
-        return [self.copy(0, self.src.at[:, :, 1 - p.c, :, self.r, self.cols], self.rb0.at[self.u, :, :, :, :, self.all], p.dev(c=1 - p.c))]
-    def load_own(self):
-        p = self.p
-        return pltpu.make_async_copy(self.src.at[:, :, p.c, :, self.r, self.cols], self.P.at[..., self.all], self.lsem.at[self.u, 0])
-    def load_r0(self, tmp):
-        return pltpu.make_async_copy(self.rb0.at[self.u, :, :, :, :, self.all], tmp.at[..., self.all], self.lsem.at[self.u, 1])
-    def add0(self, tmp):
-        P, w, Z = self.P, self.w, self.p.Z
-        @pl.loop(0, P.shape[0] * P.shape[1] * Z)
-        def _(i):
-            a, b, d = i // (P.shape[1] * Z), (i // Z) % P.shape[1], i % Z
-            P[a, b, d, :, pl.ds(0, w)] = (P[a, b, d, :, pl.ds(0, w)].astype(jnp.float32) + tmp[a, b, d, :, pl.ds(0, w)].astype(jnp.float32)).astype(jnp.bfloat16)
+        return [self.copy(0, self.src.at[:, :, 1 - p.c, :, self.r, self.cols], self.P, p.core)]
+
+    def load(self):
+        return pltpu.make_async_copy(self.src.at[:, :, self.p.c, :, self.r, self.cols], self.part, self.local)
+
     def r1(self):
         p, P = self.p, self.P
-        return [self.copy(1, P.at[1 - p.y, :, :, :, self.h[0]], self.rb1.at[self.u, 0, :, :, :, pl.ds(0, self.hs[0])], p.dev(y=1 - p.y)),
-                self.copy(2, P.at[:, 1 - p.x, :, :, self.h[1]], self.rb1.at[self.u, 1, :, :, :, pl.ds(0, self.hs[1])], p.dev(x=1 - p.x))]
-    def add1(self):
-        p, P, Z = self.p, self.P, self.p.Z
-        @pl.loop(0, 2 * Z)
-        def _(i):
-            b, d = i // Z, i % Z
-            P[p.y, b, d, :, self.h[0]] = (P[p.y, b, d, :, self.h[0]].astype(jnp.float32) + self.rb1[self.u, 0, b, d, :, pl.ds(0, self.hs[0])].astype(jnp.float32)).astype(jnp.bfloat16)
-            P[b, p.x, d, :, self.h[1]] = (P[b, p.x, d, :, self.h[1]].astype(jnp.float32) + self.rb1[self.u, 1, b, d, :, pl.ds(0, self.hs[1])].astype(jnp.float32)).astype(jnp.bfloat16)
+        return [self.copy(1, P.at[1 - p.y, :, :, :, self.h[0]], self.rest[0], p.ydev), self.copy(2, P.at[:, 1 - p.x, :, :, self.h[1]], self.rest[1], p.xdev)]
+
     def r2(self):
         p, P = self.p, self.P
-        return [self.copy(3, P.at[p.y, 1 - p.x, :, :, self.h[0]], self.rb2.at[self.u, :, :, self.h[0]], p.dev(x=1 - p.x)),
-                self.copy(4, P.at[1 - p.y, p.x, :, :, self.h[1]], self.rb2.at[self.u, :, :, self.h[1]], p.dev(y=1 - p.y))]
-    def add2(self):
-        p, P, Z = self.p, self.P, self.p.Z
-        @pl.loop(0, Z)
-        def _(d):
-            P[p.y, p.x, d, :, self.all] = (P[p.y, p.x, d, :, self.all].astype(jnp.float32) + self.rb2[self.u, d, :, self.all].astype(jnp.float32)).astype(jnp.bfloat16)
+        return [self.copy(3, P.at[p.y, 1 - p.x, :, :, self.h[0]], self.rest[2], p.xdev), self.copy(4, P.at[1 - p.y, p.x, :, :, self.h[1]], self.rest[3], p.ydev)]
+
     def r3(self):
         p, P = self.p, self.P
-        return [self.copy(4 + i, P.at[p.y, p.x, (p.z + i) % p.Z, :, self.all], self.rb3.at[self.u, i - 1, :, self.all], p.dev(z=(p.z + i) % p.Z)) for i in range(1, p.Z)]
-    def add3(self, f):
+        if self.kind == "all":
+            return [self.copy(4 + i, P.at[p.y, p.x, (p.z + i) % p.Z], self.rest[4].at[i - 1], p.dev(z=(p.z + i) % p.Z)) for i in range(1, p.Z)]
+        if self.kind == "cols":
+            return [self.copy(5, P.at[p.y, p.x, pl.ds(2 * (1 - p.pair), 2)], self.rest[4], p.far)]
+        return [self.copy(5, P.at[p.y, p.x, 1 - p.pair], self.rest[4], p.far)]
+
+    def r4(self):
+        p = self.p
+        return [self.copy(6, self.P.at[p.y, p.x, 2 * p.pair + 1 - p.half], self.rest[5], p.mate)]
+
+    def add0(self):
+        P, tmp = self.P, self.part
+        b, n = P.shape[1], self.n
+
+        @pl.loop(0, P.shape[0] * b * n)
+        def _(i):
+            at = (i // (b * n), (i // n) % b, i % n)
+            P[at] = (P[at].astype(F32) + tmp[at].astype(F32)).astype(BF16)
+
+    def add1(self):
+        p, P, n = self.p, self.P, self.n
+
+        @pl.loop(0, 2 * n)
+        def _(i):
+            b, d = i // n, i % n
+            P[p.y, b, d, :, self.h[0]] = (P[p.y, b, d, :, self.h[0]].astype(F32) + self.rest[0][b, d].astype(F32)).astype(BF16)
+            P[b, p.x, d, :, self.h[1]] = (P[b, p.x, d, :, self.h[1]].astype(F32) + self.rest[1][b, d].astype(F32)).astype(BF16)
+
+    def add2(self):
         p, P = self.p, self.P
-        s = P[p.y, p.x, p.z, :, self.all].astype(jnp.float32)
-        for i in range(p.Z - 1):
-            s = s + self.rb3[self.u, i, :, self.all].astype(jnp.float32)
-        self.fin[f, :, self.all] = s
-    def store(self, f):
-        return pltpu.make_async_copy(self.fin.at[f, :, self.all], self.out.at[pl.ds(*self.rows), self.cols], self.lsem.at[self.u, 2])
-
-def scatter_kernel(grid, units, nin, *refs):
-    ins, outs = refs[:nin], refs[nin:2 * nin]
-    rb0 = refs[2 * nin]
-    rb1, rb2, rb3, own, tmp, fin, send, recv, lsem = refs[2 * nin + 1:]
+
+        @pl.loop(0, self.n)
+        def _(d):
+            for k in (0, 1):
+                P[p.y, p.x, d, :, self.h[k]] = (P[p.y, p.x, d, :, self.h[k]].astype(F32) + self.rest[2 + k][d].astype(F32)).astype(BF16)
+
+    def add3(self):
+        p, P, got = self.p, self.P, self.rest[4]
+        if self.kind == "all":
+            s = P[p.y, p.x, p.z].astype(F32)
+            for i in range(p.Z - 1):
+                s = s + got[i].astype(F32)
+            self.out[self.r, self.cols] = s
+        elif self.kind == "rows":
+            self.out[self.r, self.cols] = P[p.y, p.x, p.pair].astype(F32) + got[...].astype(F32)
+        else:
+            theirs = 2 * p.pair + 1 - p.half
+            self.out[p.half, self.r, self.cols] = P[p.y, p.x, p.z].astype(F32) + got[p.half].astype(F32)
+            P[p.y, p.x, theirs] = (P[p.y, p.x, theirs].astype(F32) + got[1 - p.half].astype(F32)).astype(BF16)
+
+    def stages(self):
+        def first():
+            start(self.r0())
+            self.load().start()
+
+        def second():
+            self.load().wait()
+            wait_recv(self.r0())
+            self.add0()
+            start(self.r1())
+
+        def third():
+            wait_recv(self.r1())
+            wait_send(self.r1())
+            self.add1()
+            start(self.r2())
+
+        def fourth():
+            wait_recv(self.r2())
+            wait_send(self.r2())
+            self.add2()
+            start(self.r3())
+
+        def fifth():
+            wait_recv(self.r3())
+            wait_send(self.r3() + self.r0())
+            self.add3()
+            if self.kind == "cols":
+                start(self.r4())
+
+        def last():
+            wait_recv(self.r4())
+            wait_send(self.r4())
+            self.out[1 - self.p.half, self.r, self.cols] = self.rest[5][...].astype(F32)
+
+        return [first, second, third, fourth, fifth] + ([last] if self.kind == "cols" else [])
+
+
+def staggered(items, starts=None):
+    lists = [i.stages() for i in items]
+    starts = starts or list(range(len(items)))
+    steps = []
+    for s in range(max(b + len(l) for b, l in zip(starts, lists))):
+        for u in reversed(range(len(lists))):
+            k = s - starts[u]
+            if 0 <= k < len(lists[u]):
+                steps.append((u, k == len(lists[u]) - 1, lists[u][k]))
+    return steps
+
+
+class Steps:
+    def __init__(self, steps):
+        self.steps, self.at = steps, 0
+
+    def advance(self, count=1):
+        for _ in range(count):
+            if self.at < len(self.steps):
+                self.steps[self.at][2]()
+                self.at += 1
+
+    def through(self, item):
+        mark = [k for k, (u, done, _) in enumerate(self.steps) if u == item and done][0]
+        self.advance(mark + 1 - self.at)
+
+    def finish(self):
+        self.advance(len(self.steps) - self.at)
+
+
+def scatter_kernel(grid, units, n, *refs):
+    ins, outs, refs = refs[:n], refs[n : 2 * n], refs[2 * n :]
+    send, recv, local = refs[-3:]
+    buffers = list(refs[:-3])
     p = Place(grid)
-    barrier(p)
-    U, NS = len(units), own.shape[0]
-    gs = [Scatter(p, u, u % NS, ins[i], outs[i], rows, cols, (rb0, rb1, rb2, rb3, own, fin), (send, recv, lsem)) for u, (i, rows, cols) in enumerate(units)]
-    for s in range(U + 5):
-        if s < U:
-            g = gs[s]
-            start(g.r0())
-            if s >= NS:
-                pass
-            g.load_own().start()
-        if 0 <= s - 1 < U:
-            g = gs[s - 1]; t = tmp
-            wait_recv(g.r0()); g.load_r0(t).start(); g.load_own().wait(); g.load_r0(t).wait(); g.add0(t); start(g.r1())
-        if 0 <= s - 2 < U:
-            g = gs[s - 2]; wait_recv(g.r1()); wait_send(g.r1()); g.add1(); start(g.r2())
-        if 0 <= s - 3 < U:
-            g = gs[s - 3]; wait_recv(g.r2()); wait_send(g.r2()); g.add2(); start(g.r3())
-        if 0 <= s - 4 < U:
-            g = gs[s - 4]; wait_recv(g.r3()); wait_send(g.r0() + g.r3())
-            f = (s - 4) % 2
-            if s - 6 >= 0:
-                gs[s - 6].store(f).wait()
-            g.add3(f); g.store(f).start()
-    for u in range(max(0, U - 2), U):
-        gs[u].store(u % 2).wait()
-
-def scatter(grid, fulls, units, collective_id):
-    n = len(fulls)
-    A, B, C, Z = grid
-    ndev = A * B * C * Z
-    U = len(units)
-    shards = [(f.shape[0] // ndev, f.shape[1]) for f in fulls]
-    W = max(c[1] for _, _, c in units)
-    R = units[0][1][1]
-    NS = 5
-    outs = pl.pallas_call(
+    p.barrier()
+    items = []
+    for u, unit in enumerate(units):
+        tmp, mine = buffers.pop(0), [buffers.pop(0) for _ in unit.link_buffers(grid)]
+        items.append(Scatter(p, unit, ins[unit.array], outs[unit.array], mine, tmp, send.at[u], recv.at[u], local.at[u]))
+    Steps(staggered(items)).finish()
+
+
+def scatter(grid, grads, outs, units, collective_id):
+    n, U = len(grads), len(units)
+    dma = pltpu.SemaphoreType.DMA
+    return pl.pallas_call(
         functools.partial(scatter_kernel, grid, units, n),
-        out_shape=[jax.ShapeDtypeStruct(s, jnp.float32) for s in shards] + [jax.ShapeDtypeStruct((U, A, B, Z, R, W), jnp.bfloat16)],
+        out_shape=[jax.ShapeDtypeStruct(o, F32) for o in outs],
         in_specs=[pl.BlockSpec(memory_space=pl.ANY)] * n,
-        out_specs=[pl.BlockSpec(memory_space=pl.ANY)] * (n + 1),
-        scratch_shapes=[
-            pltpu.VMEM((U, 2, 2, Z, R, W - (W // 256) * 128), jnp.bfloat16),
-            pltpu.VMEM((U, Z, R, W), jnp.bfloat16),
-            pltpu.VMEM((U, Z - 1, R, W), jnp.bfloat16),
-            pltpu.VMEM((NS, A, B, Z, R, W), jnp.bfloat16),
-            pltpu.VMEM((A, B, Z, R, W), jnp.bfloat16),
-            pltpu.VMEM((2, R, W), jnp.float32),
-            pltpu.SemaphoreType.DMA((U, 8)), pltpu.SemaphoreType.DMA((U, 8)), pltpu.SemaphoreType.DMA((U, 3))],
-        compiler_params=pltpu.CompilerParams(collective_id=collective_id, has_side_effects=True, vmem_limit_bytes=60 * 1024 * 1024),
+        out_specs=[pl.BlockSpec(memory_space=pltpu.VMEM)] * n,
+        scratch_shapes=[pltpu.VMEM(s, BF16) for u in units for s in [u.shape(grid)] + u.link_buffers(grid)]
+        + [dma((U, 8)), dma((U, 8)), dma((U,))],
+        compiler_params=pltpu.CompilerParams(collective_id=collective_id, has_side_effects=True, vmem_limit_bytes=VMEM),
         name="scatter",
-    )(*[f.reshape(tuple(grid) + (s[0], s[1])) for f, s in zip(fulls, shards)])
-    return outs[:n]
-
+    )(*grads)
 
 def window_mask(start, ends, nseq, m, queries, keys):
     qpos = start + lax.broadcasted_iota(jnp.int32, (queries, 1), 0)
@@ -599,13 +709,13 @@
 def ffn(n2, dy, wg, wu, wd, tile):
     tok, width = n2.shape
     hidden = wg.shape[1]
-    whole = pl.BlockSpec((tok, width), lambda i: (0, 0))
+    whole = pl.BlockSpec((tok, width), lambda i: (0, 0), pipeline_mode=pl.Buffered(1))
     cols = pl.BlockSpec((width, tile), lambda i: (0, i))
     rows = pl.BlockSpec((tile, width), lambda i: (i, 0))
     return pl.pallas_call(
         ffn_kernel,
         grid=(hidden // tile,),
-        in_specs=[whole, pl.BlockSpec((width, tok), lambda i: (0, 0)), whole, cols, cols, rows],
+        in_specs=[whole, pl.BlockSpec((width, tok), lambda i: (0, 0), pipeline_mode=pl.Buffered(1)), whole, cols, cols, rows],
         out_specs=[whole, whole, cols, cols, rows],
         out_shape=[jax.ShapeDtypeStruct((tok, width), jnp.float32)] * 2
         + [jax.ShapeDtypeStruct(wg.shape, jnp.bfloat16), jax.ShapeDtypeStruct(wu.shape, jnp.bfloat16), jax.ShapeDtypeStruct(wd.shape, jnp.bfloat16)],
@@ -617,7 +727,7 @@
 class Exchange:
     def __init__(self, p, count, send, recv, local):
         self.count, self.send, self.recv, self.local = count, send, recv, local
-        self.me = (p.y * 8 + p.x * 4 + p.c * 2) // 2 * p.Z + p.z
+        self.me = p.me
         self.Z = p.Z
         self.groups = BLK // 16
         self.wide = 2 * HD * self.groups // count
@@ -649,90 +759,39 @@
             self.copy(off, src, dst).wait()
 
 
-def barrier_all(p, count):
-    sem = pltpu.get_barrier_semaphore()
-    me = (p.y * 4 + p.x * 2 + p.c) * p.Z + p.z
-
-    @pl.loop(1, count)
-    def _(off):
-        t = lax.rem(me + off, count)
-        pl.semaphore_signal(sem, inc=1, device_id=(t // p.Z, t % p.Z), device_id_type=MESH)
-
-    pl.semaphore_wait(sem, count - 1)
-
-
-def gather_steps(gs):
-    U = len(gs)
-    steps = []
-
-    def first(g):
-        g.own().start()
-        start(g.zs())
-
-    def second(g):
-        g.own().wait()
-        wait_recv(g.zs())
-        start(g.p1())
-        start(g.c0())
-
-    def third(g):
-        wait_recv(g.p1())
-        start(g.p2())
-        start(g.c1())
-
-    def fourth(g):
-        wait_recv(g.p2())
-        start(g.c2())
-
-    def fifth(g):
-        wait_recv(g.c0() + g.c1() + g.c2())
-        wait_send(g.zs() + g.p1() + g.p2() + g.c0() + g.c1() + g.c2())
-
-    for s in range(U + 4):
-        for lag, f in enumerate((first, second, third, fourth, fifth)):
-            if 0 <= s - lag < U:
-                steps.append(((lag, s - lag), functools.partial(f, gs[s - lag])))
-    return steps
-
-
 def forward_kernel(grid, units, nseq, sources, kvw, *refs):
     f32, bf16 = jnp.float32, jnp.bfloat16
     n = 6
-    start_ref, ends_ref, index_ref, x_ref = refs[:4]
-    ins, refs = refs[4 : 4 + n], refs[4 + n :]
+    start_ref, ends_ref, index_ref, x_ref, dy_ref = refs[:5]
+    ins, refs = refs[5 : 5 + n], refs[5 + n :]
     fulls, refs = refs[:n], refs[n:]
-    n1_ref, q_ref, win_ref, att_ref, mixed_ref, n2_ref, gains_ref, refs = *refs[:7], refs[7:]
-    wbuf, small, kv, got, picked, send, recv, local, xsend, xrecv, xlocal, lsem = refs
+    dyx_ref, n2x_ref, refs = *refs[:2], refs[2:]
+    n1_ref, q_ref, win_ref, att_ref, mixed_ref, gains_ref, refs = *refs[:6], refs[6:]
+    n2, wbuf, small, kv, got, picked, send, recv, local, xsend, xrecv, xlocal, lsem, msend, mrecv = refs
     p = Place(grid)
-    A, B, C, Z = grid
-    count = A * B * C * Z
+    count = p.count
     tok, width = x_ref.shape
     batches = tok // BLK
-    barrier_all(p, count)
-    gs = [Gather(p, ins[i], fulls[i], rows, cols, send.at[u], recv.at[u], local.at[u]) for u, (i, rows, cols) in enumerate(units)]
-    steps = gather_steps(gs)
-    last = {i: max(u for u, (j, _, _) in enumerate(units) if j == i) for i in range(n)}
-    at = [0]
-
-    def advance(count_=1):
-        for _ in range(count_):
-            if at[0] < len(steps):
-                steps[at[0]][1]()
-                at[0] += 1
-
-    def advance_to(i):
-        mark = [k for k, (label, _) in enumerate(steps) if label == (4, last[i])][0]
-        while at[0] <= mark:
-            advance()
+    p.barrier()
+    items = [Gather(p, t, ins[t.array], fulls[t.array], send.at[u], recv.at[u], local.at[u]) for u, t in enumerate(units)]
+    steps = Steps(staggered(items, [0] + list(range(2, len(items) + 1))))
+    advance, through = steps.advance, steps.through
 
     def load(i, dst, sem):
         return pltpu.make_async_copy(fulls[i], dst, lsem.at[sem])
 
-    advance(5)
+    def to_mate(k, src, dst):
+        return (
+            pltpu.make_async_copy(src, dst, lsem.at[3 + k]),
+            pltpu.make_async_remote_copy(src, dst, msend.at[k], mrecv.at[k], device_id=p.mate, device_id_type=MESH),
+        )
+
+    advance(1)
+    shared = [to_mate(0, dy_ref, dyx_ref.at[p.half])]
+    start(shared[0])
     x = x_ref[...].astype(f32)
-    normed = x * lax.rsqrt(jnp.mean(x * x, axis=-1, keepdims=True) + EPS)
-    mixed_ref[...] = normed
-    advance_to(0)
+    mixed_ref[...] = x * lax.rsqrt(jnp.mean(x * x, axis=-1, keepdims=True) + EPS)
+    through(0)
     load(0, small, 0).start()
     load(0, small, 0).wait()
     gains = small[..., kvw:].reshape(width, 128).astype(f32).T
@@ -751,9 +810,15 @@
     def dst1(t):
         return got.at[ex1.me]
 
+    def src2(t):
+        return picked.at[t]
+
+    def dst2(t):
+        g, c = ex2.piece(ex2.me)
+        return win_ref.at[:, :, g, :, c]
+
     ex1.begin(src1, dst1)
-    advance_to(1)
-    load(1, wbuf, 1).start()
+    advance(6)
     ex1.end(src1, dst1)
 
     @pl.loop(0, count)
@@ -762,54 +827,53 @@
             for i in range(sources):
                 picked[t, m, i] = got[index_ref[t, m * sources + i], m]
 
-    def src2(t):
-        return picked.at[t]
-
-    def dst2(t):
-        g, c = ex2.piece(ex2.me)
-        return win_ref.at[:, :, g, :, c]
-
     ex2.begin(src2, dst2)
+    through(1)
+    load(1, wbuf, 1).start()
+    advance(2)
     load(1, wbuf, 1).wait()
     tile = 512
     for j in range(0, width, tile):
         w = wbuf[..., j : j + tile].reshape(width, tile)
         q_ref[:, j : j + tile] = (jnp.dot(n1_ref[...], w, preferred_element_type=f32) * (HD**-0.5)).astype(bf16)
         advance()
-    advance_to(2)
+    through(2)
     load(2, wbuf, 2).start()
-    advance(10)
+    advance(0)
     ex2.end(src2, dst2)
+    load(2, wbuf, 2).wait()
     for m in range(batches):
-        mask = window_mask(start_ref[m], ends_ref, nseq, m, BLK, sources * BLK)
+        rows = pl.ds(m * BLK, BLK)
         for h0 in range(0, H, 2):
 
             @pl.loop(h0, h0 + 2)
             def _(h):
                 cols = pl.ds(pl.multiple_of(h * HD, HD), HD)
-                rows = pl.ds(m * BLK, BLK)
                 mask = window_mask(start_ref[m], ends_ref, nseq, m, BLK, sources * BLK)
                 k = win_ref[m, :, :, :, :HD].reshape(sources * BLK, HD)
                 v = win_ref[m, :, :, :, HD:].reshape(sources * BLK, HD)
                 prob = softmax_rows(q_ref[rows, cols], k, mask)
                 att_ref[rows, cols] = jnp.dot(prob.astype(bf16), v, preferred_element_type=f32).astype(bf16)
 
-            advance(2)
-    load(2, wbuf, 2).wait()
-    for j in range(0, width, tile):
-        w = wbuf[..., j : j + tile].reshape(width, tile)
-        mixed_ref[:, j : j + tile] = x_ref[:, j : j + tile].astype(f32) + jnp.dot(att_ref[...], w, preferred_element_type=f32)
-        advance()
-    mixed = mixed_ref[...]
-    inverse = lax.rsqrt(jnp.mean(mixed * mixed, axis=-1, keepdims=True) + EPS)
-    n2_ref[...] = (mixed * inverse * gains_ref[1:2]).astype(bf16)
-    while at[0] < len(steps):
-        advance()
-
-
-def forward(grid, shards, units, x, start, ends, index, sources, kvw, collective_id):
-    A, B, C, Z = grid
-    count = A * B * C * Z
+            advance()
+        for j in range(0, width, tile):
+            w = wbuf[..., j : j + tile].reshape(width, tile)
+            mixed_ref[rows, j : j + tile] = x_ref[rows, j : j + tile].astype(f32) + jnp.dot(att_ref[rows], w, preferred_element_type=f32)
+        mixed = mixed_ref[rows]
+        inverse = lax.rsqrt(jnp.mean(mixed * mixed, axis=-1, keepdims=True) + EPS)
+        n2[rows] = (mixed * inverse * gains_ref[1:2]).astype(bf16)
+        shared.append(to_mate(1 + m, n2.at[rows], n2x_ref.at[p.half, rows]))
+        start(shared[-1])
+        advance(2)
+    steps.finish()
+    for copies in shared:
+        for c in copies:
+            c.wait()
+
+
+def forward(grid, shards, units, x, dy, start, ends, index, sources, kvw, collective_id):
+    a, b, c, z = grid
+    count = a * b * c * z
     tok, width = x.shape
     batches = tok // BLK
     bf16 = jnp.bfloat16
@@ -820,21 +884,24 @@
     any_, vmem, smem = (pl.BlockSpec(memory_space=s) for s in (pl.ANY, pltpu.VMEM, pltpu.SMEM))
     dma = pltpu.SemaphoreType.DMA
     sds = jax.ShapeDtypeStruct
+    kinds = {t.array: t.kind for t in units}
+    whole = [tuple(grid[:3]) + (z // 2 if kinds[i] == "rows" else z,) + s.shape[-2:] for i, s in enumerate(shards)]
     outs = pl.pallas_call(
         functools.partial(forward_kernel, grid, units, ends.shape[1], sources, kvw),
-        out_shape=[sds(tuple(grid) + s.shape, s.dtype) for s in shards]
+        out_shape=[sds(w, bf16) for w in whole]
+        + [sds((2, tok, width), bf16)] * 2
         + [
             sds((tok, width), bf16),
             sds((tok, width), bf16),
             sds((batches, sources, groups, 16, 2 * HD), bf16),
             sds((tok, width), bf16),
             sds((tok, width), jnp.float32),
-            sds((tok, width), bf16),
             sds((8, width), jnp.float32),
         ],
-        in_specs=[smem, smem, smem, vmem] + [any_] * 6,
-        out_specs=[any_] * 6 + [vmem] * 7,
+        in_specs=[smem, smem, smem, vmem, any_] + [any_] * 6,
+        out_specs=[any_] * 8 + [vmem] * 6,
         scratch_shapes=[
+            pltpu.VMEM((tok, width), bf16),
             pltpu.VMEM(tuple(grid) + (rows, width), bf16),
             pltpu.VMEM(tuple(grid) + (rows, shards[0].shape[1]), bf16),
             pltpu.VMEM((batches, groups, 16, 2 * HD), bf16),
@@ -846,14 +913,16 @@
             dma((2, count - 1)),
             dma((2, count - 1)),
             dma((2,)),
-            dma((3,)),
+            dma((4 + batches,)),
+            dma((1 + batches,)),
+            dma((1 + batches,)),
         ],
         compiler_params=pltpu.CompilerParams(collective_id=collective_id, has_side_effects=True, vmem_limit_bytes=VMEM),
         name="forward",
-    )(start, ends, index, x, *shards)
+    )(start, ends, index, x, dy, *shards)
     fulls = [o.reshape(-1, s.shape[-1]) for o, s in zip(outs, shards)]
-    n1, q, window, att, mixed, n2, gains = outs[6:]
-    return fulls, n1, q, window.reshape(batches, sources * BLK, 2 * HD), att, mixed, n2, gains
+    dy_pair, n2_pair, n1, q, window, att, mixed, gains = outs[6:]
+    return fulls, dy_pair, n2_pair, n1, q, window.reshape(batches, sources * BLK, 2 * HD), att, mixed, gains
 
 def place_of(perm):
     return jnp.argsort(perm, axis=1).astype(jnp.int32)
@@ -906,8 +975,13 @@
     kvw = w_keyval.shape[1]
     gains = jnp.stack([gain_attn, gain_ffn], axis=1)
     small = jnp.concatenate([w_keyval, jnp.pad(gains, ((0, 0), (0, 126)))], axis=1)
-    shards = [small, w_query, w_out, w_gate, w_up, w_down]
-    units = units_of(shards, width)
+    sub = w_down.shape[0]
+    half = w_gate.shape[1] // 2
+    shards = [small, w_query, w_out, by_parity(w_gate, sub), by_parity(w_up, sub), w_down]
+    units = [Unit(i, "all", (0, s.shape[0]), (0, s.shape[1])) for i, s in enumerate(shards[:3])]
+    for k in (0, 1):
+        units += [Unit(i, "cols", (0, w_gate.shape[0]), (k * half // 2, half // 2)) for i in (3, 4)]
+        units += [Unit(5, "rows", (0, sub), (k * width // 2, width // 2))]
     holder = place_of(block_perm)
     block = block_perm[:, :, None] - (sources - 1) + jnp.arange(sources, dtype=jnp.int32)
     index = jnp.take_along_axis(holder[:, None, :], jnp.maximum(block, 0), axis=2)
@@ -915,15 +989,17 @@
     start = lax.dynamic_slice_in_dim(block_perm, me, 1, axis=1)[:, 0] * BLK
     ends = jnp.cumsum(extra_len + (WIN - 1), axis=1).astype(jnp.int32)
     x = tokens.reshape(tok, width)
-    fulls, n1b, query, window, att, mixed, n2b, gains = forward(grid, shards, units, x, start, ends, index, sources, kvw, 0)
+    dy = cotangent.reshape(tok, width)
+    fulls, dy_pair, n2_pair, n1b, query, window, att, mixed, gains = forward(grid, shards, units, x, dy, start, ends, index, sources, kvw, 0)
     small, wq, wo, wg, wu, wd = fulls
     wkv = small[:, :kvw]
     g1, g2 = gains[0], gains[1]
     x = x.astype(f32)
-    dy = cotangent.reshape(tok, width)
     r1 = lax.rsqrt(jnp.mean(x * x, axis=-1, keepdims=True) + EPS)
     r2 = lax.rsqrt(jnp.mean(mixed * mixed, axis=-1, keepdims=True) + EPS)
-    out, d_n2, d_wgate, d_wup, d_down = ffn(n2b, dy, wg, wu, wd, 512)
+    out, d_n2, d_wgate, d_wup, d_down = ffn(n2_pair.reshape(2 * tok, width), dy_pair.reshape(2 * tok, width), wg, wu, wd, 256)
+    d_n2 = from_mate(d_n2.reshape(2, tok, width))
+    out = from_mate(out.reshape(2, tok, width))
     block_out = (mixed + out).astype(bf16)
     d_mixed_norm, d_g2 = norm_back(mixed, r2, g2, d_n2)
     d_mixed = dy.astype(f32) + d_mixed_norm
@@ -940,7 +1016,15 @@
     grad_tokens = (d_mixed + d_x_norm).astype(bf16)
     d_gains = jnp.pad(jnp.stack([d_g1, d_g2], axis=1), ((0, 0), (0, 126)))
     d_small = jnp.concatenate([d_wkeyval, d_gains], axis=1).astype(bf16)
-    small, dq, do, dg, du, dd = scatter(grid, [d_small, d_wquery, d_wout, d_wgate, d_wup, d_down], units, 1)
+    grads = [d_small, d_wquery, d_wout, d_wgate, d_wup, d_down]
+    kinds = ["all"] * 3 + ["cols"] * 2 + ["rows"]
+    grads = [
+        g.reshape(tuple(grid[:3]) + (grid[3] // 2 if k == "rows" else grid[3], -1, g.shape[1]))
+        for g, k in zip(grads, kinds)
+    ]
+    order = units[3:] + units[2:3] + units[1:2] + units[:1]
+    small, dq, do, dg, du, dd = scatter(grid, grads, [s.shape for s in shards], order, 1)
+    dg, du = from_parity(dg, sub), from_parity(du, sub)
     return (
         block_out.reshape(tokens.shape),
         grad_tokens.reshape(tokens.shape),
@@ -955,14 +1039,22 @@
     )
 
 
-def units_of(shards, width):
-    rows = min(s.shape[0] for s in shards)
-    units = []
-    for i, s in enumerate(shards):
-        for r in range(0, s.shape[0], rows):
-            for c in range(0, s.shape[1], width):
-                units.append((i, (r, rows), (c, min(width, s.shape[1] - c))))
-    return units
+def by_parity(w, sub):
+    rows, hidden = w.shape
+    return w.reshape(rows, -1, 2, sub).transpose(2, 0, 1, 3).reshape(2, rows, hidden // 2)
+
+
+def from_parity(w, sub):
+    _, rows, part = w.shape
+    return w.reshape(2, rows, -1, sub).transpose(1, 2, 0, 3).reshape(rows, 2 * part)
+
+
+def from_mate(parts):
+    z = lax.axis_index("fsdp")
+    count = lax.axis_size("fsdp")
+    theirs = lax.dynamic_index_in_dim(parts, 1 - z % 2, 0, keepdims=False)
+    got = lax.ppermute(theirs.astype(jnp.bfloat16), "fsdp", [(i, i ^ 1) for i in range(count)])
+    return lax.dynamic_index_in_dim(parts, z % 2, 0, keepdims=False) + got.astype(jnp.float32)
 
 
 def solution(mesh):

time: 823 us -> 787 us (0.956)
  Pallas kernels: 663 us -> 536 us
  waiting for transfers between devices: 48.3 us -> 107 us
  local copies, waits for them, and re-layouts: 33.6 us -> 61.9 us
    pallas_call x1, Pallas kernels: 247 us -> 165 us  [scatter(): pl.pallas_call(functools.partial(scatter_kernel, grid, units, n), out_sha...]
    ppermute x0 -> x2, waiting for transfers between devices: none -> 60.9 us  [from_mate(): lax.ppermute(theirs.astype(jnp.bfloat16), 'fsdp', [(i, i ^ 1) for i in ra...]
    pallas_call x1, Pallas kernels: 307 us -> 254 us  [forward(): pl.pallas_call(functools.partial(forward_kernel, grid, units, ends.shape[...]
    reshape x0 -> x11, local copies, waits for them, and re-layouts: none -> 25.1 us  [the longest x4 13.7 us: from_parity(): w.reshape(2, rows, -1, sub).transpose(1, 2, 0, 3).reshape(rows, 2 * part)]
    pallas_call x1, Pallas kernels: 82.7 us -> 91.1 us  [ffn(): pl.pallas_call(ffn_kernel, grid=(hidden // tile,), in_specs=[whole, pl.Bl...]
  transfers between devices with their start and end apart: 2 -> 4, of which waited for: 2 -> 4; matrix products, arithmetic and copies ran while one was open for 3% -> 5% of each run, Pallas kernels for 0% -> 0%
where the time goes in v3:
time: 787 us; the launch traced here: 777 us
  Pallas kernels  536 us (68%)
  waiting for transfers between devices  107 us (14%)
  local copies, waits for them, and re-layouts  61.9 us (8%)
  matrix products  32.9 us (4%)
  other arithmetic  24.8 us (3%)
  starting transfers between devices  13.1 us (2%)
    pallas_call x1, Pallas kernels, forward(): pl.pallas_call(functools.partial(forward_kernel, grid, units, ends.shape[...  254 us
    pallas_call x1, Pallas kernels, scatter(): pl.pallas_call(functools.partial(scatter_kernel, grid, units, n), out_sha...  165 us
    pallas_call x1, Pallas kernels, ffn(): pl.pallas_call(ffn_kernel, grid=(hidden // tile,), in_specs=[whole, pl.Bl...  91.1 us
    ppermute x2, waiting for transfers between devices, from_mate(): lax.ppermute(theirs.astype(jnp.bfloat16), 'fsdp', [(i, i ^ 1) for i in ra...  60.9 us
    all_to_all x1, waiting for transfers between devices, window_sums(): lax.all_to_all(pieces, axes, split_axis=0, concat_axis=0, tiled=True)  45.1 us
    pallas_call x1, Pallas kernels, attend_back(): pl.pallas_call(functools.partial(attend_back_kernel, ends.shape[1]), out_...  26.3 us
  transfers between devices with their start and end apart: 4, of which 4 were waited for; matrix products, arithmetic and copies ran while one was open for 5% of the time, Pallas kernels for 0%

profile of v3, /device:TPU:0, one launch (start us, length us, event | category | flops | bytes accessed | tf_op | source)
XLA Modules:
  0.0 777.0 jit_solution(3958019441283842245)
XLA Ops:
  4.6 3.1 gather_fusion.1
  17.1 253.9 %forward.1 = (bf16[2,2,2,4,48,640]{5,4,3,2,1,0:T(8,128)(2,1)}, bf16[2,2,2,4,48,1536]{5,4,3,2,1,0:T(8,128)(2,1)}, bf16[2,2,2,4,48,1536]{5,4,3,2,1,0:T(8,128)(2,1)...) custom-call(s32[2]{0:T(128)} %fusion.26.refs_0_.start, ...), custom_call_target="tpu_custom_call" | custom-call | tf_op jit(solution)/shard_map/forward/pallas_call | solution.py:889
  271.0 4.7 copy.77
  275.7 91.1 %ffn.1 = (f32[1024,1536]{1,0:T(8,128)}, f32[1024,1536]{1,0:T(8,128)}, bf16[1536,2304]{1,0:T(8,128)(2,1)}, bf16[1536,2304]{1,0:T(8,128)(2,1)}, bf16[2304,1536]{1,0:T(8,128)(2,1)}) custom-call(bf16[1024,1536]{1,0:T(8,128)(2,1)} %bitcast.112, bf16[1536,1024]{1,0:T(8,128)(2,1)} %bitcast.113, bf16[1024,1536]{1,0:T(8,128)(2,1)} %bitcast.131, ...), custom_call_target="tpu_custom_call" | custom-call | tf_op jit(solution)/shard_map/ffn/pallas_call | solution.py:715
  366.8 3.4 fusion.12
  370.2 4.9 collective-permute-start.1
  375.0 3.2 fusion.11
  379.5 31.1 %collective-permute-done.1 = bf16[512,1536]{1,0:T(8,128)(2,1)} collective-permute-done((bf16[512,1536]{1,0:T(8,128)(2,1)}, bf16[512,1536]{1,0:T(8,128)(2,1)}, u32[]{:S(2)}, u32[]{:S(2)}) %collective-permute-start.1) | collective-permute-done | bytes 1572896 | tf_op jit(solution)/shard_map/ppermute | solution.py:1056
  410.6 3.6 multiply_reduce_fusion
  414.2 29.8 %collective-permute-done = bf16[512,1536]{1,0:T(8,128)(2,1)} collective-permute-done((bf16[512,1536]{1,0:T(8,128)(2,1)}, bf16[512,1536]{1,0:T(8,128)(2,1)}, u32[]{:S(2)}, u32[]{:S(2)}) %collective-permute-start) | collective-permute-done | bytes 1572896 | tf_op jit(solution)/shard_map/ppermute | solution.py:1056
  444.0 4.6 subtract_add_fusion
  448.6 3.9 convolution_convert_fusion.1.d_ref
  452.5 26.3 %attend_back.1 = (bf16[512,1536]{1,0:T(8,128)(2,1)}, bf16[2,1280,512]{2,1,0:T(8,128)(2,1)}) custom-call(s32[2]{0:T(128)} %fusion.26.refs_0_.start, s32[2,4]{1,0:T(2,128)} %reduce_window_sum.11.refs_1_.ends, bf16[512,1536]{1,0:T(8,128)(2,1)} %get-tuple-element.49.q_ref, bf16[2,1280,512]{2,1,0:T(8,128)(2,1)} %bitcast.134, ...), custom_call_target="tpu_custom_call" | custom-call | tf_op jit(solution)/shard_map/attend_back/pallas_call | solution.py:648
  478.8 3.6 copy.83
  482.4 3.5 all-to-all-start
  486.1 3.1 gather_fusion.2
  492.6 7.2 convolution_convert_fusion
  499.8 45.1 %all-to-all-done = bf16[32,10,8,512]{3,2,1,0:T(8,128)(2,1)} async-done(((bf16[32,10,8,512]{3,2,1,0:T(8,128)(2,1)}), bf16[32,10,8,512]{3,2,1,0:T(8,128)(2,1)}, u32[]{:S(2)}, u32[]{:S(2)}) %all-to-all-start) | async-done | bytes 2621472 | tf_op jit(solution)/shard_map/all_to_all | solution.py:954
  544.9 4.4 gather_fusion
  549.3 4.1 select_reduce_fusion
  553.4 4.7 all-to-all-start.1
  558.2 6.9 fusion
  565.1 6.6 convolution_multiply_fusion.1
  572.6 6.2 fusion.8
  582.8 164.5 %scatter.1 = (f32[48,640]{1,0:T(8,128)}, f32[48,1536]{1,0:T(8,128)}, f32[48,1536]{1,0:T(8,128)}, f32[2,48,2304]{2,1,0:T(8,128)}, f32[2,48,2304]{2,1,0:T(8,128)}, /*index=5*/f32[144,1536]{1,0:T(8,128)}) custom-call(bf16[2,2,2,4,48,640]{5,4,3,2,1,0:T(8,128)(2,1)} %pad_maximum_fusion.refs_0_, bf16[2,2,2,4,48,1536]{5,4,3,2,1,0:T(8,128)(2,1)} %bitcast.128, ...), custom_call_target="tpu_custom_call" | custom-call | tf_op jit(solution)/shard_map/scatter/pallas_call | solution.py:566
  750.3 2.6 reshape.275
  752.9 2.5 copy.72
  755.4 4.4 reshape.276
  759.8 2.3 reshape.277
  762.2 2.5 copy.73
  764.7 4.4 reshape.278
  769.1 5.0 fusion.5
  (108 shorter events, 28.0 us)
Async XLA Ops:
  4.6 4.2 copy-start.18
  4.6 4.9 copy-start.9
  7.7 5.2 copy-start.10
  10.9 5.4 copy-start.20
  10.9 5.4 copy-start.21
  10.9 5.5 copy-start.13
  366.8 12.4 %copy-start = (f32[512,1536]{1,0:T(8,128)S(1)}, f32[512,1536]{1,0:T(8,128)}, u32[]{:S(2)}) copy-start(f32[512,1536]{1,0:T(8,128)} %get-tuple-element.40) | copy-start | bytes 9437188
  370.2 40.4 %collective-permute-start.1 = (bf16[512,1536]{1,0:T(8,128)(2,1)}, bf16[512,1536]{1,0:T(8,128)(2,1)}, u32[]{:S(2)}, u32[]{:S(2)}) collective-permute-start(bf16[512,1536]{1,0:T(8,128)(2,1)} %fusion.12), channel_id=1, source_target_pairs={{0,1},{1,0},{2,3},{3,2},{4,5},{5,4},{6,7},{7,6},{8,9},{9,8},{10,11... | collective-permute-start | bytes 4718600 | tf_op jit(solution)/shard_map/ppermute | solution.py:1056
  378.3 65.7 %collective-permute-start = (bf16[512,1536]{1,0:T(8,128)(2,1)}, bf16[512,1536]{1,0:T(8,128)(2,1)}, u32[]{:S(2)}, u32[]{:S(2)}) collective-permute-start(bf16[512,1536]{1,0:T(8,128)(2,1)} %fusion.11), channel_id=1, source_target_pairs={{0,1},{1,0},{2,3},{3,2},{4,5},{5,4},{6,7},{7,6},{8,9},{9,8},{10,11... | collective-permute-start | bytes 4718600 | tf_op jit(solution)/shard_map/ppermute | solution.py:1056
  410.6 33.4 %copy-start.3 = (bf16[2,1,256,1536]{3,2,1,0:T(8,128)(2,1)S(1)}, bf16[2,1,256,1536]{3,2,1,0:T(8,128)(2,1)}, u32[]{:S(2)}) copy-start(bf16[2,1,256,1536]{3,2,1,0:T(8,128)(2,1)} %param.23) | copy-start | bytes 4718596
  410.6 33.4 %copy-start.4 = (f32[1024,1536]{1,0:T(8,128)S(1)}, f32[1024,1536]{1,0:T(8,128)}, u32[]{:S(2)}) copy-start(f32[1024,1536]{1,0:T(8,128)} %get-tuple-element.46) | copy-start | bytes 18874372
  410.6 38.0 %slice-start = ((s8[4718592]{0:T(1024)(128)(4,1)}), s8[4194304]{0:T(1024)(128)(4,1)S(1)}, s32[]{:S(2)}) async-start(s8[4718592]{0:T(1024)(128)(4,1)} %bitcast.148), calls=%async_computation.2 | async-start | bytes 8388608
  444.0 4.6 slice-start.1
  448.5 3.9 copy-start.2
  482.4 62.5 %all-to-all-start = ((bf16[32,10,8,512]{3,2,1,0:T(8,128)(2,1)}), bf16[32,10,8,512]{3,2,1,0:T(8,128)(2,1)}, u32[]{:S(2)}, u32[]{:S(2)}) async-start(bf16[32,10,8,512]{3,2,1,0:T(8,128)(2,1)} %bitcast.107), calls=%async_computation | async-start | bytes 5242880 | tf_op jit(solution)/shard_map/all_to_all | solution.py:954
  486.1 3.8 copy-start.5
  489.2 2.2 copy-start.1
  491.8 80.8 %copy-start.14 = (f32[1,2,2,128]{3,1,2,0:T(2,128)}, f32[1,2,2,128]{3,1,2,0:T(2,128)S(1)}, u32[]{:S(2)}) copy-start(f32[1,2,2,128]{3,1,2,0:T(2,128)S(1)} %copy.79) | copy-start | bytes 6148
  553.4 19.1 %all-to-all-start.1 = ((bf16[32,2,8,512]{3,2,1,0:T(8,128)(2,1)}), bf16[32,2,8,512]{3,2,1,0:T(8,128)(2,1)S(1)}, u32[]{:S(2)}, u32[]{:S(2)}) async-start(bf16[32,2,8,512]{3,2,1,0:T(8,128)(2,1)} %select_reduce_fusion), calls=%async_computation.1 | async-start | bytes 1048576 | tf_op jit(solution)/shard_map/all_to_all | solution.py:964
  558.2 6.9 copy-start.19
  572.6 6.2 copy-start.8
  572.6 6.5 copy-start.6
  762.2 6.9 copy-start.15
  762.2 6.9 copy-start.16
  762.2 6.9 copy-start.17
  769.1 5.1 copy-start.12
  769.1 5.8 copy-start.11
  769.1 6.5 copy-start.7

commit v4 on v3

--- a/solution.py
+++ b/solution.py
@@ -1,5 +1,6 @@
 import functools
 import math
+import types
 
 import jax
 import jax.numpy as jnp
@@ -15,7 +16,7 @@
 
 
 EPS = 1e-06
-VMEM = 60 * 1024 * 1024
+VMEM = 62 * 1024 * 1024
 
 
 def for_sending(x):
@@ -233,6 +234,8 @@
 
 MESH = pl.DeviceIdType.MESH
 BF16, F32 = jnp.bfloat16, jnp.float32
+ALL, COLS, ROWS = 0, 1, 2
+ARRAYS = ("small", "wq", "wo", "wg", "wu", "wd")
 
 
 class Place:
@@ -298,15 +301,15 @@
         self.width = cols[1]
 
     def shape(self, grid):
-        return grid[:2] + (grid[3] // 2 if self.kind == "rows" else grid[3],) + (self.rows[1], self.width)
+        return grid[:2] + (grid[3] // 2 if self.kind == ROWS else grid[3],) + (self.rows[1], self.width)
 
     def link_buffers(self, grid):
         a, b, z, r, w = self.shape(grid)
         h = halves(w)
         out = [(a, b, z, r, w), (b, z, r, h[0][1]), (a, z, r, h[1][1]), (z, r, h[0][1]), (z, r, h[1][1])]
-        if self.kind == "all":
+        if self.kind == ALL:
             return out + [(z - 1, r, w)]
-        if self.kind == "cols":
+        if self.kind == COLS:
             return out + [(z // 2, r, w), (r, w)]
         return out + [(r, w)]
 
@@ -316,8 +319,8 @@
         self.p, self.dst, self.send, self.recv, self.local, self.kind = p, dst, send, recv, local, unit.kind
         self.r, self.all = pl.ds(*unit.rows), pl.ds(*unit.cols)
         self.h = [pl.ds(unit.cols[0] + a, b) for a, b in halves(unit.width)]
-        self.src = (lambda half: src.at[half, self.r, self.all]) if unit.kind == "cols" else (lambda half: src.at[self.r, self.all])
-        self.spot = p.pair if unit.kind == "rows" else p.z
+        self.src = (lambda half: src.at[half, self.r, self.all]) if unit.kind == COLS else (lambda half: src.at[self.r, self.all])
+        self.spot = p.pair if unit.kind == ROWS else p.z
 
     def copy(self, k, src, dst, dev):
         return pltpu.make_async_remote_copy(src, dst, self.send.at[k], self.recv.at[k], device_id=dev, device_id_type=MESH)
@@ -335,9 +338,9 @@
     def z1(self):
         p = self.p
         there = self.dst.at[p.y, p.x, p.c, self.spot, self.r, self.all]
-        if self.kind == "all":
+        if self.kind == ALL:
             return [self.copy(i - 1, self.src(0), there, p.dev(z=(p.z + i) % p.Z)) for i in range(1, p.Z)]
-        if self.kind == "cols":
+        if self.kind == COLS:
             return [self.copy(0, self.src(1 - p.half), there, p.mate)]
         return [self.copy(0, self.src(0), there, p.far)]
 
@@ -376,7 +379,7 @@
             start(self.z2())
 
         def third():
-            if self.kind == "cols":
+            if self.kind == COLS:
                 wait_recv(self.z2())
             else:
                 self.own().wait()
@@ -393,31 +396,35 @@
 
         def last():
             wait_recv(self.c0() + self.c1() + self.c2())
-            wait_send(self.z1() + (self.z2() if self.kind == "cols" else []) + self.p1() + self.p2() + self.c0() + self.c1() + self.c2())
-
-        return [first] + ([second] if self.kind == "cols" else []) + [third, fourth, fifth, last]
+            wait_send(self.z1() + (self.z2() if self.kind == COLS else []) + self.p1() + self.p2() + self.c0() + self.c1() + self.c2())
+
+        return [first] + ([second] if self.kind == COLS else []) + [third, fourth, fifth, last]
 
 
 class Scatter:
-    def __init__(self, p, unit, src, out, buffers, tmp, send, recv, local):
+    def __init__(self, p, unit, src, out, landing, rest, sems):
         self.p, self.unit, self.kind = p, unit, unit.kind
-        self.src, self.out, self.tmp, self.send, self.recv, self.local = src, out, tmp, send, recv, local
+        self.src, self.out, self.landing, self.rest = src, out, landing, rest
+        self.send, self.recv, self.local = sems
         self.r, self.cols = pl.ds(*unit.rows), pl.ds(*unit.cols)
         self.h = [pl.ds(a, b) for a, b in halves(unit.width)]
-        self.P, self.rest = buffers[0], buffers[1:]
-        self.spot = p.pair if unit.kind == "rows" else p.z
+        self.all = pl.ds(0, unit.width)
         self.n = unit.shape(p.grid)[2]
-        self.part = tmp
+        self.stage = 0
 
     def copy(self, k, src, dst, dev):
         return pltpu.make_async_remote_copy(src, dst, self.send.at[k], self.recv.at[k], device_id=dev, device_id_type=MESH)
 
     def r0(self):
         p = self.p
-        return [self.copy(0, self.src.at[:, :, 1 - p.c, :, self.r, self.cols], self.P, p.core)]
-
-    def load(self):
-        return pltpu.make_async_copy(self.src.at[:, :, self.p.c, :, self.r, self.cols], self.part, self.local)
+        return [self.copy(0, self.src.at[:, :, 1 - p.c, :, self.r, self.cols], self.landing, p.core)]
+
+    def loads(self):
+        own = self.src.at[:, :, self.p.c, :, self.r, self.cols]
+        return [
+            pltpu.make_async_copy(self.landing, self.P.at[..., self.all], self.local.at[0]),
+            pltpu.make_async_copy(own, self.T.at[..., self.all], self.local.at[1]),
+        ]
 
     def r1(self):
         p, P = self.p, self.P
@@ -429,24 +436,23 @@
 
     def r3(self):
         p, P = self.p, self.P
-        if self.kind == "all":
-            return [self.copy(4 + i, P.at[p.y, p.x, (p.z + i) % p.Z], self.rest[4].at[i - 1], p.dev(z=(p.z + i) % p.Z)) for i in range(1, p.Z)]
-        if self.kind == "cols":
-            return [self.copy(5, P.at[p.y, p.x, pl.ds(2 * (1 - p.pair), 2)], self.rest[4], p.far)]
-        return [self.copy(5, P.at[p.y, p.x, 1 - p.pair], self.rest[4], p.far)]
+        if self.kind == ALL:
+            return [self.copy(4 + i, P.at[p.y, p.x, (p.z + i) % p.Z, :, self.all], self.rest[4].at[i - 1], p.dev(z=(p.z + i) % p.Z)) for i in range(1, p.Z)]
+        if self.kind == COLS:
+            return [self.copy(5, P.at[p.y, p.x, pl.ds(2 * (1 - p.pair), 2), :, self.all], self.rest[4], p.far)]
+        return [self.copy(5, P.at[p.y, p.x, 1 - p.pair, :, self.all], self.rest[4], p.far)]
 
     def r4(self):
         p = self.p
-        return [self.copy(6, self.P.at[p.y, p.x, 2 * p.pair + 1 - p.half], self.rest[5], p.mate)]
+        return [self.copy(6, self.P.at[p.y, p.x, 2 * p.pair + 1 - p.half, :, self.all], self.rest[5], p.mate)]
 
     def add0(self):
-        P, tmp = self.P, self.part
-        b, n = P.shape[1], self.n
+        P, T, b, n = self.P, self.T, self.P.shape[1], self.n
 
         @pl.loop(0, P.shape[0] * b * n)
         def _(i):
-            at = (i // (b * n), (i // n) % b, i % n)
-            P[at] = (P[at].astype(F32) + tmp[at].astype(F32)).astype(BF16)
+            at = (i // (b * n), (i // n) % b, i % n, slice(None), self.all)
+            P[at] = P[at] + T[at]
 
     def add1(self):
         p, P, n = self.p, self.P, self.n
@@ -454,8 +460,8 @@
         @pl.loop(0, 2 * n)
         def _(i):
             b, d = i // n, i % n
-            P[p.y, b, d, :, self.h[0]] = (P[p.y, b, d, :, self.h[0]].astype(F32) + self.rest[0][b, d].astype(F32)).astype(BF16)
-            P[b, p.x, d, :, self.h[1]] = (P[b, p.x, d, :, self.h[1]].astype(F32) + self.rest[1][b, d].astype(F32)).astype(BF16)
+            P[p.y, b, d, :, self.h[0]] = P[p.y, b, d, :, self.h[0]] + self.rest[0][b, d]
+            P[b, p.x, d, :, self.h[1]] = P[b, p.x, d, :, self.h[1]] + self.rest[1][b, d]
 
     def add2(self):
         p, P = self.p, self.P
@@ -463,58 +469,91 @@
         @pl.loop(0, self.n)
         def _(d):
             for k in (0, 1):
-                P[p.y, p.x, d, :, self.h[k]] = (P[p.y, p.x, d, :, self.h[k]].astype(F32) + self.rest[2 + k][d].astype(F32)).astype(BF16)
+                P[p.y, p.x, d, :, self.h[k]] = P[p.y, p.x, d, :, self.h[k]] + self.rest[2 + k][d]
 
     def add3(self):
-        p, P, got = self.p, self.P, self.rest[4]
-        if self.kind == "all":
-            s = P[p.y, p.x, p.z].astype(F32)
+        p, got = self.p, self.rest[4]
+        mine = lambda d: self.P[p.y, p.x, d, :, self.all].astype(F32)
+        if self.kind == ALL:
+            s = mine(p.z)
             for i in range(p.Z - 1):
                 s = s + got[i].astype(F32)
             self.out[self.r, self.cols] = s
-        elif self.kind == "rows":
-            self.out[self.r, self.cols] = P[p.y, p.x, p.pair].astype(F32) + got[...].astype(F32)
+        elif self.kind == ROWS:
+            self.out[self.r, self.cols] = mine(p.pair) + got[...].astype(F32)
         else:
             theirs = 2 * p.pair + 1 - p.half
-            self.out[p.half, self.r, self.cols] = P[p.y, p.x, p.z].astype(F32) + got[p.half].astype(F32)
-            P[p.y, p.x, theirs] = (P[p.y, p.x, theirs].astype(F32) + got[1 - p.half].astype(F32)).astype(BF16)
-
-    def stages(self):
-        def first():
-            start(self.r0())
-            self.load().start()
-
-        def second():
-            self.load().wait()
-            wait_recv(self.r0())
-            self.add0()
-            start(self.r1())
-
-        def third():
+            self.out[p.half, self.r, self.cols] = mine(p.z) + got[p.half].astype(F32)
+            self.P[p.y, p.x, theirs, :, self.all] = (mine(theirs) + got[1 - p.half].astype(F32)).astype(BF16)
+
+    def first(self):
+        start(self.r0())
+
+    @property
+    def P(self):
+        return self.pool.at[self.slot]
+
+    def admit(self, pool, slot, T):
+        self.pool, self.slot, self.T = pool, slot, T
+        wait_recv(self.r0())
+        start(self.loads())
+
+    def settle(self):
+        for c in self.loads():
+            c.wait()
+        self.add0()
+        start(self.r1())
+
+    def next(self):
+        k, self.stage = self.stage, self.stage + 1
+        if k == 0:
             wait_recv(self.r1())
             wait_send(self.r1())
             self.add1()
             start(self.r2())
-
-        def fourth():
+        elif k == 1:
             wait_recv(self.r2())
             wait_send(self.r2())
             self.add2()
             start(self.r3())
-
-        def fifth():
+        elif k == 2:
             wait_recv(self.r3())
             wait_send(self.r3() + self.r0())
             self.add3()
-            if self.kind == "cols":
+            if self.kind == COLS:
                 start(self.r4())
-
-        def last():
+        else:
             wait_recv(self.r4())
             wait_send(self.r4())
             self.out[1 - self.p.half, self.r, self.cols] = self.rest[5][...].astype(F32)
-
-        return [first, second, third, fourth, fifth] + ([last] if self.kind == "cols" else [])
+        return self.stage < (4 if self.kind == COLS else 3)
+
+
+class Sums:
+    def __init__(self, pools):
+        self.pools, self.used = pools, {k: 0 for k in pools}
+        self.queue, self.under_way = [], []
+
+    def add(self, item):
+        item.first()
+        self.queue.append(item)
+
+    def tick(self, count=1):
+        for _ in range(count):
+            new = self.queue.pop(0) if self.queue else None
+            if new is not None:
+                key = ROWS if new.kind == ROWS else ALL
+                P, T = self.pools[key]
+                new.admit(P, self.used[key] % P.shape[0], T)
+                self.used[key] += 1
+            self.under_way = [i for i in self.under_way if i.next()]
+            if new is not None:
+                new.settle()
+                self.under_way.append(new)
+
+    def finish(self):
+        while self.queue or self.under_way:
+            self.tick()
 
 
 def staggered(items, starts=None):
@@ -546,34 +585,6 @@
     def finish(self):
         self.advance(len(self.steps) - self.at)
 
-
-def scatter_kernel(grid, units, n, *refs):
-    ins, outs, refs = refs[:n], refs[n : 2 * n], refs[2 * n :]
-    send, recv, local = refs[-3:]
-    buffers = list(refs[:-3])
-    p = Place(grid)
-    p.barrier()
-    items = []
-    for u, unit in enumerate(units):
-        tmp, mine = buffers.pop(0), [buffers.pop(0) for _ in unit.link_buffers(grid)]
-        items.append(Scatter(p, unit, ins[unit.array], outs[unit.array], mine, tmp, send.at[u], recv.at[u], local.at[u]))
-    Steps(staggered(items)).finish()
-
-
-def scatter(grid, grads, outs, units, collective_id):
-    n, U = len(grads), len(units)
-    dma = pltpu.SemaphoreType.DMA
-    return pl.pallas_call(
-        functools.partial(scatter_kernel, grid, units, n),
-        out_shape=[jax.ShapeDtypeStruct(o, F32) for o in outs],
-        in_specs=[pl.BlockSpec(memory_space=pl.ANY)] * n,
-        out_specs=[pl.BlockSpec(memory_space=pltpu.VMEM)] * n,
-        scratch_shapes=[pltpu.VMEM(s, BF16) for u in units for s in [u.shape(grid)] + u.link_buffers(grid)]
-        + [dma((U, 8)), dma((U, 8)), dma((U,))],
-        compiler_params=pltpu.CompilerParams(collective_id=collective_id, has_side_effects=True, vmem_limit_bytes=VMEM),
-        name="scatter",
-    )(*grads)
-
 def window_mask(start, ends, nseq, m, queries, keys):
     qpos = start + lax.broadcasted_iota(jnp.int32, (queries, 1), 0)
     first = jnp.maximum(qpos - (WIN - 1), 0)
@@ -591,82 +602,6 @@
     return expd * (1.0 / jnp.sum(expd, axis=1, keepdims=True))
 
 
-def attend_kernel(nseq, start, ends, q_ref, kv_ref, o_ref):
-    m = pl.program_id(0)
-    mask = window_mask(start[m], ends, nseq, m, q_ref.shape[0], kv_ref.shape[1])
-    p = softmax_rows(q_ref[...], kv_ref[0, :, :HD], mask)
-    o_ref[...] = jnp.dot(p.astype(jnp.bfloat16), kv_ref[0, :, HD:], preferred_element_type=jnp.float32).astype(jnp.bfloat16)
-
-
-def attend(q, window, start, ends):
-    batches, keys, _ = window.shape
-    return pl.pallas_call(
-        functools.partial(attend_kernel, ends.shape[1]),
-        out_shape=jax.ShapeDtypeStruct(q.shape, jnp.bfloat16),
-        grid_spec=pltpu.PrefetchScalarGridSpec(
-            num_scalar_prefetch=2,
-            grid=(batches, H),
-            in_specs=[
-                pl.BlockSpec((BLK, HD), lambda m, h, *_: (m, h)),
-                pl.BlockSpec((1, keys, 2 * HD), lambda m, h, *_: (m, 0, 0)),
-            ],
-            out_specs=pl.BlockSpec((BLK, HD), lambda m, h, *_: (m, h)),
-        ),
-        compiler_params=pltpu.CompilerParams(vmem_limit_bytes=VMEM),
-        name="attend",
-    )(start, ends, q, window)
-
-
-def attend_back_kernel(nseq, start, ends, q_ref, kv_ref, d_ref, dq_ref, dkv_ref, dkv):
-    m, h = pl.program_id(0), pl.program_id(1)
-    mask = window_mask(start[m], ends, nseq, m, q_ref.shape[0], kv_ref.shape[1])
-    q, k, v, d = q_ref[...], kv_ref[0, :, :HD], kv_ref[0, :, HD:], d_ref[...]
-    p = softmax_rows(q, k, mask)
-    dp = lax.dot_general(d, v, (((1,), (1,)), ((), ())), preferred_element_type=jnp.float32)
-    ds = (p * (dp - jnp.sum(p * dp, axis=1, keepdims=True))).astype(jnp.bfloat16)
-    dq_ref[...] = jnp.dot(ds, k, preferred_element_type=jnp.float32).astype(jnp.bfloat16)
-    dk = lax.dot_general(ds, q, (((0,), (0,)), ((), ())), preferred_element_type=jnp.float32)
-    dv = lax.dot_general(p.astype(jnp.bfloat16), d, (((0,), (0,)), ((), ())), preferred_element_type=jnp.float32)
-
-    @pl.when(h == 0)
-    def _():
-        dkv[:, :HD] = dk
-        dkv[:, HD:] = dv
-
-    @pl.when(h > 0)
-    def _():
-        dkv[:, :HD] += dk
-        dkv[:, HD:] += dv
-
-    @pl.when(h == pl.num_programs(1) - 1)
-    def _():
-        dkv_ref[0] = dkv[...].astype(jnp.bfloat16)
-
-
-def attend_back(q, window, datt, start, ends):
-    batches, keys, _ = window.shape
-    return pl.pallas_call(
-        functools.partial(attend_back_kernel, ends.shape[1]),
-        out_shape=[jax.ShapeDtypeStruct(q.shape, jnp.bfloat16), jax.ShapeDtypeStruct(window.shape, jnp.bfloat16)],
-        grid_spec=pltpu.PrefetchScalarGridSpec(
-            num_scalar_prefetch=2,
-            grid=(batches, H),
-            in_specs=[
-                pl.BlockSpec((BLK, HD), lambda m, h, *_: (m, h)),
-                pl.BlockSpec((1, keys, 2 * HD), lambda m, h, *_: (m, 0, 0)),
-                pl.BlockSpec((BLK, HD), lambda m, h, *_: (m, h)),
-            ],
-            out_specs=[
-                pl.BlockSpec((BLK, HD), lambda m, h, *_: (m, h)),
-                pl.BlockSpec((1, keys, 2 * HD), lambda m, h, *_: (m, 0, 0)),
-            ],
-            scratch_shapes=[pltpu.VMEM((keys, 2 * HD), jnp.float32)],
-        ),
-        compiler_params=pltpu.CompilerParams(vmem_limit_bytes=VMEM),
-        name="attend_back",
-    )(start, ends, q, window, datt)
-
-
 def geglu_parts(gate):
     c = math.sqrt(2.0 / math.pi)
     square = gate * gate
@@ -675,53 +610,6 @@
     value = gate * half
     slope = half + 0.5 * gate * (1.0 - t * t) * c * (1.0 + 3 * 0.044715 * square)
     return value, slope
-
-
-def ffn_kernel(n2_ref, n2t_ref, dy_ref, wg_ref, wu_ref, wd_ref, out_ref, dn2_ref, dwg_ref, dwu_ref, dwd_ref):
-    n2, dy = n2_ref[...], dy_ref[...]
-    wg, wu, wd = wg_ref[...], wu_ref[...], wd_ref[...]
-    f32 = jnp.float32
-    gate = jnp.dot(n2, wg, preferred_element_type=f32)
-    up = jnp.dot(n2, wu, preferred_element_type=f32)
-    value, slope = geglu_parts(gate)
-    hidden = (value * up).astype(jnp.bfloat16)
-    dh = lax.dot_general(dy, wd, (((1,), (1,)), ((), ())), preferred_element_type=f32)
-    dgate = (dh * up * slope).astype(jnp.bfloat16)
-    dup = (dh * value).astype(jnp.bfloat16)
-    out = jnp.dot(hidden, wd, preferred_element_type=f32)
-    dn2 = lax.dot_general(dgate, wg, (((1,), (1,)), ((), ())), preferred_element_type=f32)
-    dn2 += lax.dot_general(dup, wu, (((1,), (1,)), ((), ())), preferred_element_type=f32)
-    dwd_ref[...] = lax.dot_general(hidden, dy, (((0,), (0,)), ((), ())), preferred_element_type=f32).astype(jnp.bfloat16)
-    dwg_ref[...] = jnp.dot(n2t_ref[...], dgate, preferred_element_type=f32).astype(jnp.bfloat16)
-    dwu_ref[...] = jnp.dot(n2t_ref[...], dup, preferred_element_type=f32).astype(jnp.bfloat16)
-
-    @pl.when(pl.program_id(0) == 0)
-    def _():
-        out_ref[...] = out
-        dn2_ref[...] = dn2
-
-    @pl.when(pl.program_id(0) > 0)
-    def _():
-        out_ref[...] += out
-        dn2_ref[...] += dn2
-
-
-def ffn(n2, dy, wg, wu, wd, tile):
-    tok, width = n2.shape
-    hidden = wg.shape[1]
-    whole = pl.BlockSpec((tok, width), lambda i: (0, 0), pipeline_mode=pl.Buffered(1))
-    cols = pl.BlockSpec((width, tile), lambda i: (0, i))
-    rows = pl.BlockSpec((tile, width), lambda i: (i, 0))
-    return pl.pallas_call(
-        ffn_kernel,
-        grid=(hidden // tile,),
-        in_specs=[whole, pl.BlockSpec((width, tok), lambda i: (0, 0), pipeline_mode=pl.Buffered(1)), whole, cols, cols, rows],
-        out_specs=[whole, whole, cols, cols, rows],
-        out_shape=[jax.ShapeDtypeStruct((tok, width), jnp.float32)] * 2
-        + [jax.ShapeDtypeStruct(wg.shape, jnp.bfloat16), jax.ShapeDtypeStruct(wu.shape, jnp.bfloat16), jax.ShapeDtypeStruct(wd.shape, jnp.bfloat16)],
-        compiler_params=pltpu.CompilerParams(vmem_limit_bytes=VMEM),
-        name="ffn",
-    )(n2, n2.T, dy, wg, wu, wd)
 
 
 class Exchange:
@@ -885,7 +773,7 @@
     dma = pltpu.SemaphoreType.DMA
     sds = jax.ShapeDtypeStruct
     kinds = {t.array: t.kind for t in units}
-    whole = [tuple(grid[:3]) + (z // 2 if kinds[i] == "rows" else z,) + s.shape[-2:] for i, s in enumerate(shards)]
+    whole = [tuple(grid[:3]) + (z // 2 if kinds[i] == ROWS else z,) + s.shape[-2:] for i, s in enumerate(shards)]
     outs = pl.pallas_call(
         functools.partial(forward_kernel, grid, units, ends.shape[1], sources, kvw),
         out_shape=[sds(w, bf16) for w in whole]
@@ -922,66 +810,462 @@
     )(start, ends, index, x, dy, *shards)
     fulls = [o.reshape(-1, s.shape[-1]) for o, s in zip(outs, shards)]
     dy_pair, n2_pair, n1, q, window, att, mixed, gains = outs[6:]
-    return fulls, dy_pair, n2_pair, n1, q, window.reshape(batches, sources * BLK, 2 * HD), att, mixed, gains
+    return fulls, dy_pair, n2_pair, n1, q, window, att, mixed, gains
+
+
+def backward_kernel(grid, units, nseq, sources, kvw, names, *refs):
+    r = types.SimpleNamespace(**dict(zip(names, refs)))
+    rest = list(refs[len(names) :])
+    p = Place(grid)
+    count = p.count
+    landings = [rest.pop(0) for _ in units]
+    parts = [[rest.pop(0) for _ in u.link_buffers(grid)[1:]] for u in units]
+    P_all, T_all, sums, dkv_own, send, recv, local, xsend, xrecv, xlocal, msend, mrecv, sem = rest
+    tok, width = r.n1.shape
+    batches = tok // BLK
+    hidden = r.wg.shape[1]
+    grads = [r.g_small, r.g_wq, r.g_wo, r.g_wg, r.g_wu, r.g_wd]
+    outs = [r.o_small, r.o_wq, r.o_wo, r.o_wg, r.o_wu, r.o_wd]
+    items = {}
+    for u, unit in enumerate(units):
+        items[unit.array, unit.cols[0]] = Scatter(
+            p, unit, grads[unit.array], outs[unit.array], landings[u], parts[u], (send.at[u], recv.at[u], local.at[u])
+        )
+    rs = Sums({ALL: (P_all, T_all), ROWS: None})
+    p.barrier()
+    dot = functools.partial(jnp.dot, preferred_element_type=F32)
+
+    def dot_t(a, b):
+        return lax.dot_general(a, b, (((1,), (1,)), ((), ())), preferred_element_type=F32)
+
+    def t_dot(a, b):
+        return lax.dot_general(a, b, (((0,), (0,)), ((), ())), preferred_element_type=F32)
+
+    def local_copy(src, dst, k):
+        return pltpu.make_async_copy(src, dst, sem.at[k])
+
+    def fetch(src, dst, k):
+        c = local_copy(src, dst, k)
+        c.start()
+        c.wait()
+
+    def to_mate(k, src, dst):
+        return pltpu.make_async_remote_copy(src, dst, msend.at[k], mrecv.at[k], device_id=p.mate, device_id_type=MESH)
+
+    dn2_swap = to_mate(0, r.dn2_to, r.dn2_got)
+    out_swap = to_mate(1, r.out_to, r.out_got)
+    tile = 256
+    tiles = hidden // tile
+    third = tiles // 3
+    f32_tok, bf_tok = pltpu.VMEM((tok, width), F32), pltpu.VMEM((tok, width), BF16)
+    panel = grid + (width // count,)
+
+    def ffn(n2, n2t, dy, dn2, wg, wu, wd, put_g, put_u, hid, hid_t):
+        def weights(i, slot):
+            cols = pl.ds(i * tile, tile)
+            return [
+                local_copy(r.wg.at[:, cols], wg.at[slot], 3 * slot),
+                local_copy(r.wu.at[:, cols], wu.at[slot], 3 * slot + 1),
+                local_copy(r.wd.at[cols], wd.at[slot], 3 * slot + 2),
+            ]
+
+        def results(i, slot):
+            cols = pl.ds(i * tile, tile)
+            return [
+                local_copy(put_g.at[slot], r.g_wg.at[..., cols], 6 + 4 * slot),
+                local_copy(put_u.at[slot], r.g_wu.at[..., cols], 7 + 4 * slot),
+                local_copy(hid.at[slot], r.hidden.at[:, cols], 8 + 4 * slot),
+                local_copy(hid_t.at[slot], r.hidden_t.at[cols], 9 + 4 * slot),
+            ]
+
+        start(weights(0, 0))
+        first = [local_copy(r.n2, n2, 14), local_copy(r.dy, dy, 15)]
+        start(first)
+        dn2[...] = jnp.zeros_like(dn2)
+        for c in first:
+            c.wait()
+        for k in range(2):
+            n2t[:, k * tok : (k + 1) * tok] = n2[k].T
+        def step(i, slot, ahead, behind):
+            if ahead is not None:
+                start(weights(ahead, 1 - slot))
+            for c in weights(i, slot):
+                c.wait()
+            if behind is not None:
+                for c in results(behind, slot):
+                    c.wait()
+            rows = n2[...].reshape(2 * tok, width)
+            gate = dot(rows, wg[slot])
+            up = dot(rows, wu[slot])
+            value, slope = geglu_parts(gate)
+            low = (value * up).astype(BF16)
+            hid[slot] = low
+            hid_t[slot] = low.T
+            dh = dot_t(dy[...].reshape(2 * tok, width), wd[slot])
+            dg = (dh * up * slope).astype(BF16)
+            du = (dh * value).astype(BF16)
+            back = dot_t(dg, wg[slot]) + dot_t(du, wu[slot])
+            dn2[...] += back.reshape(dn2.shape)
+            put_g[slot] = dot(n2t[...], dg).astype(BF16).reshape(panel + (tile,))
+            put_u[slot] = dot(n2t[...], du).astype(BF16).reshape(panel + (tile,))
+            start(results(i, slot))
+
+        for i in range(tiles):
+            done = i % third == third - 1
+            step(i, i % 2, i + 1 if i + 1 < tiles else None, i - 2 if i % third >= 2 else None)
+            if done:
+                for j in (i - 1, i):
+                    for c in results(j, j % 2):
+                        c.wait()
+                rs.add(items[3, (i + 1 - third) * tile])
+                rs.add(items[4, (i + 1 - third) * tile])
+            if i >= third - 1:
+                rs.tick(1)
+        n2[0] = dn2[1 - p.half].astype(BF16)
+        fetch(n2.at[0], r.dn2_to, 14)
+        dn2_swap.start()
+        fetch(dn2.at[p.half], r.dn2_own, 14)
+
+    pair = pltpu.VMEM((2, tok, width), BF16)
+    pl.run_scoped(
+        ffn,
+        pair,
+        pltpu.VMEM((width, 2 * tok), BF16),
+        pair,
+        pltpu.VMEM((2, tok, width), F32),
+        pltpu.VMEM((2, width, tile), BF16),
+        pltpu.VMEM((2, width, tile), BF16),
+        pltpu.VMEM((2, tile, width), BF16),
+        pltpu.VMEM((2,) + panel + (tile,), BF16),
+        pltpu.VMEM((2,) + panel + (tile,), BF16),
+        pltpu.VMEM((2, 2 * tok, tile), BF16),
+        pltpu.VMEM((2, tile, 2 * tok), BF16),
+    )
+
+    def ffn_rest(dy, hid_t, put_rows, hid, wd, out):
+        rows, part = hidden // 2, width // 3
+        pulls = [local_copy(r.dy, dy, 0)] + [local_copy(r.hidden_t.at[pl.ds(y * rows, rows)], hid_t.at[y], 1 + y) for y in range(2)]
+        start(pulls)
+        for c in pulls:
+            c.wait()
+        for k in range(3):
+            cols = pl.ds(k * part, part)
+            puts = [local_copy(put_rows.at[y], r.g_wd.at[y, :, :, :, :, cols], 4 + y) for y in range(2)]
+            for y in range(2):
+                value = dot(hid_t[y], dy[:, :, cols].reshape(2 * tok, part))
+                put_rows[y] = value.astype(BF16).reshape(put_rows.shape[1:])
+                puts[y].start()
+            for c in puts:
+                c.wait()
+            rs.add(items[5, k * part])
+            rs.tick(1)
+        some = hidden // 3
+        for turn in range(2):
+            who = 1 - p.half if turn == 0 else p.half
+
+            def pull(k):
+                cols = pl.ds(k * some, some)
+                return [
+                    local_copy(r.hidden.at[pl.ds(pl.multiple_of(who * tok, tok), tok), cols], hid.at[k % 2], 6 + 2 * (k % 2)),
+                    local_copy(r.wd.at[cols], wd.at[k % 2], 7 + 2 * (k % 2)),
+                ]
+
+            start(pull(0))
+            for k in range(3):
+                if k < 2:
+                    start(pull(k + 1))
+                for c in pull(k):
+                    c.wait()
+                value = dot(hid[k % 2], wd[k % 2])
+                out[...] = value if k == 0 else out[...] + value
+            if turn == 0:
+                dy[0] = out[...].astype(BF16)
+                fetch(dy.at[0], r.out_to, 10)
+                out_swap.start()
+            else:
+                fetch(out, r.out_own, 10)
+
+    def weight_grad(a, b, into, array, k0, scale=None):
+        half = width // 2
+
+        def run(at, put):
+            at[...] = a.T
+            n = half // tile
+            for k in range(2):
+                puts = [local_copy(put.at[j], into.at[..., pl.ds(k * half + j * tile, tile)], k0 + j) for j in range(n)]
+                for j in range(n):
+                    c0 = k * half + j * tile
+                    value = dot(at[...], b[:, c0 : c0 + tile])
+                    value = value if scale is None else value * scale
+                    put[j] = value.astype(BF16).reshape(panel + (tile,))
+                    puts[j].start()
+                for c in puts:
+                    c.wait()
+                rs.add(items[array, k * half])
+
+        pl.run_scoped(run, pltpu.VMEM((width, tok), BF16), pltpu.VMEM((half // tile,) + panel + (tile,), BF16))
+
+    gains = r.gains
+
+    def norm_back(value, gain, grad):
+        inverse = lax.rsqrt(jnp.mean(value * value, axis=-1, keepdims=True) + EPS)
+        u = grad * gain
+        along = jnp.sum(u * value, axis=-1, keepdims=True) / width
+        return inverse * u - value * (inverse * inverse * inverse) * along, jnp.sum(grad * value * inverse, axis=0, keepdims=True)
+
+    def phase_c(dmixed, datt, dq, dgain):
+        dgain[...] = jnp.zeros_like(dgain)
+
+        def through_ffn(mixed, dn2, got2, dy, att, wo):
+            pulls = [
+                local_copy(r.mixed, mixed, 0),
+                local_copy(r.dn2_own, dn2, 1),
+                local_copy(r.dy.at[p.half], dy, 2),
+                local_copy(r.wo, wo, 3),
+                local_copy(r.att, att, 4),
+            ]
+            start(pulls)
+            dn2_swap.wait()
+            fetch(r.dn2_got, got2, 5)
+            for c in pulls:
+                c.wait()
+            total = jnp.zeros((1, width), F32)
+            for i in range(0, tok, 128):
+                rows = pl.ds(i, 128)
+                d, g = norm_back(mixed[rows], gains[1:2], dn2[rows] + got2[rows].astype(F32))
+                total = total + g
+                d = dy[rows].astype(F32) + d
+                dmixed[rows] = d
+                dy[rows] = d.astype(BF16)
+            dgain[1:2] = total
+            for j in range(0, width, 512):
+                datt[:, j : j + 512] = dot_t(dy[...], wo[j : j + 512]).astype(BF16)
+            rs.tick()
+            weight_grad(att[...], dy, r.g_wo, 2, 6)
+
+        pl.run_scoped(
+            through_ffn,
+            f32_tok,
+            f32_tok,
+            bf_tok,
+            bf_tok,
+            bf_tok,
+            pltpu.VMEM((width, width), BF16),
+        )
+        rs.tick()
+
+        def through_attention(dkvw, n1, w, small, x):
+            later = [local_copy(r.n1, n1, 0), local_copy(r.wq, w, 1), local_copy(r.small, small, 2), local_copy(r.x, x, 3)]
+            start(later)
+
+            def heads(q, win, dkv):
+                pulls = [local_copy(r.q, q, 4), local_copy(r.window, win, 5)]
+                start(pulls)
+                for c in pulls:
+                    c.wait()
+                for m in range(batches):
+                    rows = pl.ds(m * BLK, BLK)
+                    dkv[...] = jnp.zeros_like(dkv)
+                    for h0 in range(0, H, 3):
+
+                        @pl.loop(h0, h0 + 3)
+                        def _(h):
+                            cols = pl.ds(pl.multiple_of(h * HD, HD), HD)
+                            mask = window_mask(r.start[m], r.ends, nseq, m, BLK, sources * BLK)
+                            k = win[m, :, :, :, :HD].reshape(sources * BLK, HD)
+                            v = win[m, :, :, :, HD:].reshape(sources * BLK, HD)
+                            qh, d = q[rows, cols], datt[rows, cols]
+                            prob = softmax_rows(qh, k, mask)
+                            dp = dot_t(d, v)
+                            ds = (prob * (dp - jnp.sum(prob * dp, axis=1, keepdims=True))).astype(BF16)
+                            dq[rows, cols] = dot(ds, k).astype(BF16)
+                            dkv[:, :HD] += t_dot(ds, qh)
+                            dkv[:, HD:] += t_dot(prob.astype(BF16), d)
+
+                        rs.tick(1)
+                    dkvw[m] = dkv[...].astype(BF16).reshape(dkvw.shape[1:])
+
+            pl.run_scoped(heads, bf_tok, pltpu.VMEM(r.window.shape, BF16), pltpu.VMEM((sources * BLK, kvw), F32))
+            ex1 = Exchange(p, count, xsend.at[0], xrecv.at[0], xlocal.at[0])
+            ex2 = Exchange(p, count, xsend.at[1], xrecv.at[1], xlocal.at[1])
+
+            def src1(t):
+                g, c = ex1.piece(t)
+                return dkvw.at[:, :, g, :, c]
+
+            def dst1(t):
+                return r.got.at[ex1.me]
+
+            def src2(t):
+                return sums.at[t]
+
+            def dst2(t):
+                g, c = ex2.piece(ex2.me)
+                return dkv_own.at[:, g, :, c]
+
+            ex1.begin(src1, dst1)
+            for c in later:
+                c.wait()
+            weight_grad(n1[...], dq, r.g_wq, 1, 6, HD**-0.5)
+            rs.tick()
+
+            def output(mixed, own, theirs, low):
+                out_swap.wait()
+                for i in range(0, tok, 256):
+                    rows = pl.ds(i, 256)
+                    pulls = [local_copy(r.mixed.at[rows], mixed, 8), local_copy(r.out_own.at[rows], own, 9), local_copy(r.out_got.at[rows], theirs, 10)]
+                    start(pulls)
+                    for c in pulls:
+                        c.wait()
+                    low[...] = (mixed[...] + own[...] + theirs[...].astype(F32)).astype(BF16)
+                    fetch(low, r.block_out.at[rows], 11)
+
+            some, some_low = pltpu.VMEM((256, width), F32), pltpu.VMEM((256, width), BF16)
+            pl.run_scoped(output, some, some, some_low, some_low)
+            rs.tick(0)
+
+            def to_input(dn1, got):
+                for j in range(0, width, 512):
+                    dn1[:, j : j + 512] = dot_t(dq[...], w[j : j + 512]) * (HD**-0.5)
+                ex1.end(src1, dst1)
+                fetch(r.got, got, 8)
+
+                @pl.loop(0, count)
+                def _(d):
+                    for m in range(batches):
+                        s = jnp.zeros(sums.shape[2:], F32)
+                        for i in range(sources):
+                            k = m * sources + i
+                            s = s + jnp.where(r.valid[d, k] > 0, got[r.index[d, k], m, i].astype(F32), 0.0)
+                        sums[d, m] = s.astype(BF16)
+
+                ex2.begin(src2, dst2)
+                rs.tick(0)
+                ex2.end(src2, dst2)
+                dkv = dkv_own[...].reshape(tok, kvw)
+                part = width // grid[0]
+                for j in range(grid[0]):
+                    dn1[:, j * part : (j + 1) * part] += dot_t(dkv, small[j, ..., :kvw].reshape(part, kvw))
+                total = jnp.zeros((1, width), F32)
+                for i in range(0, tok, 128):
+                    rows = pl.ds(i, 128)
+                    d, g = norm_back(x[rows].astype(F32), gains[0:1], dn1[rows])
+                    total = total + g
+                    x[rows] = (dmixed[rows] + d).astype(BF16)
+                dgain[0:1] = total
+                store = local_copy(x, r.grad_tokens, 3)
+                store.start()
+                for j in range(grid[0]):
+                    value = t_dot(n1[:, j * part : (j + 1) * part], dkv)
+                    small[j, ..., :kvw] = value.astype(BF16).reshape(panel[1:] + (kvw,))
+                both = jnp.concatenate([dgain[...], jnp.zeros((120, width), F32)], axis=0)
+                small[..., kvw:] = both.T.astype(BF16).reshape(panel + (128,))
+                fetch(small, r.g_small, 2)
+                rs.add(items[0, 0])
+                rs.tick()
+                store.wait()
+
+            pl.run_scoped(to_input, f32_tok, pltpu.VMEM(r.got.shape, BF16))
+
+        pl.run_scoped(
+            through_attention,
+            pltpu.VMEM((batches, sources, BLK // 16, 16, kvw), BF16),
+            bf_tok,
+            pltpu.VMEM((width, width), BF16),
+            pltpu.VMEM(panel + (kvw + 128,), BF16),
+            bf_tok,
+        )
+
+    def rest_of_it(P_rows, T_rows):
+        rs.pools[ROWS] = (P_rows, T_rows)
+        pl.run_scoped(
+            ffn_rest,
+            pair,
+            pltpu.VMEM((2, hidden // 2, 2 * tok), BF16),
+            pltpu.VMEM((2, 2, 2, p.Z // 2, hidden // 16, width // 3), BF16),
+            pltpu.VMEM((2, tok, hidden // 3), BF16),
+            pltpu.VMEM((2, hidden // 3, width), BF16),
+            f32_tok,
+        )
+        pl.run_scoped(phase_c, f32_tok, bf_tok, bf_tok, pltpu.VMEM((8, width), F32))
+        rs.finish()
+
+    slot_rows = [u for u in units if u.kind == ROWS][0].shape(grid)
+    pl.run_scoped(rest_of_it, pltpu.VMEM((3,) + slot_rows, BF16), pltpu.VMEM(slot_rows, BF16))
+
+
+def backward(grid, fulls, shapes, saved, start, ends, index, valid, units, sources, kvw, collective_id):
+    any_, vmem, smem = (pl.BlockSpec(memory_space=s) for s in (pl.ANY, pltpu.VMEM, pltpu.SMEM))
+    sds, dma = jax.ShapeDtypeStruct, pltpu.SemaphoreType.DMA
+    a, b, c, z = grid
+    count = a * b * c * z
+    tok, width = saved["n1"].shape
+    batches = tok // BLK
+    hidden = fulls[3].shape[1]
+    U = len(units)
+    kinds = {t.array: t.kind for t in units}
+    whole = [grid[:3] + (z // 2 if kinds[i] == ROWS else z,) + s[-2:] for i, s in enumerate(shapes)]
+    fulls = [fulls[0].reshape(whole[0])] + fulls[1:]
+    inputs = dict(start=(start, smem), ends=(ends, smem), index=(index, smem), valid=(valid, smem))
+    inputs.update({k: (v, any_) for k, v in zip(ARRAYS, fulls)})
+    inputs.update({k: (v, any_) for k, v in saved.items()})
+    inputs.update(gains=(saved["gains"], vmem))
+    outputs = {"o_" + k: (sds(s, F32), vmem) for k, s in zip(ARRAYS, shapes)}
+    low, high = (sds((tok, width), BF16), any_), (sds((tok, width), F32), any_)
+    outputs.update(block_out=low, grad_tokens=low, dn2_to=low, dn2_got=low, out_to=low, out_got=low, dn2_own=high, out_own=high)
+    wide = kvw * (BLK // 16) // count
+    outputs.update(hidden=(sds((2 * tok, hidden), BF16), any_), hidden_t=(sds((hidden, 2 * tok), BF16), any_))
+    outputs.update(got=(sds((count, batches, sources, 16, wide), BF16), any_))
+    outputs.update({"g_" + k: (sds(w, BF16), any_) for k, w in zip(ARRAYS, whole)})
+    names = list(inputs) + list(outputs)
+    slot = (a, b, z, width // count, width // 2)
+    results = pl.pallas_call(
+        functools.partial(backward_kernel, grid, units, ends.shape[1], sources, kvw, names),
+        out_shape=[s for s, _ in outputs.values()] + [sds(u.shape(grid), BF16) for u in units],
+        in_specs=[s for _, s in inputs.values()],
+        out_specs=[s for _, s in outputs.values()] + [any_] * U,
+        scratch_shapes=[pltpu.VMEM(s, BF16) for u in units for s in u.link_buffers(grid)[1:]]
+        + [
+            pltpu.VMEM((5,) + slot, BF16),
+            pltpu.VMEM(slot, BF16),
+            pltpu.VMEM((count, batches, 16, wide), BF16),
+            pltpu.VMEM((batches, BLK // 16, 16, kvw), BF16),
+            dma((U, 8)),
+            dma((U, 8)),
+            dma((U, 2)),
+            dma((2, count - 1)),
+            dma((2, count - 1)),
+            dma((2,)),
+            dma((2,)),
+            dma((2,)),
+            dma((16,)),
+        ],
+        compiler_params=pltpu.CompilerParams(collective_id=collective_id, has_side_effects=True, vmem_limit_bytes=VMEM),
+        name="backward",
+    )(*[v for v, _ in inputs.values()])
+    found = dict(zip(outputs, results))
+    return found["block_out"], found["grad_tokens"], results[: len(ARRAYS)]
 
 def place_of(perm):
     return jnp.argsort(perm, axis=1).astype(jnp.int32)
 
 
-def windows_of(kv, perm, sources):
-    axes = ("dp", "fsdp")
-    batches, rows, cols = kv.shape
-    count = perm.shape[1]
-    part = rows // count
-    pieces = kv.reshape(batches, count, part, cols).transpose(1, 0, 2, 3)
-    spread = lax.all_to_all(pieces, axes, split_axis=0, concat_axis=0, tiled=True)
-    holder = place_of(perm)
-    block = perm[:, :, None] - (sources - 1) + jnp.arange(sources, dtype=jnp.int32)
-    source = jnp.take_along_axis(holder[:, None, :], jnp.maximum(block, 0), axis=2)
-    index = (source * batches + jnp.arange(batches, dtype=jnp.int32)[:, None, None]).transpose(1, 0, 2).reshape(-1)
-    picked = jnp.take(spread.reshape(count * batches, part, cols), index, axis=0).reshape(count, batches * sources, part, cols)
-    arrived = lax.all_to_all(picked, axes, split_axis=0, concat_axis=0, tiled=True)
-    return arrived.transpose(1, 0, 2, 3).reshape(batches, sources * rows, cols)
-
-
-def window_sums(grads, perm, sources):
-    axes = ("dp", "fsdp")
-    batches, wide, cols = grads.shape
-    rows = wide // sources
-    count = perm.shape[1]
-    part = rows // count
-    pieces = grads.reshape(batches * sources, count, part, cols).transpose(1, 0, 2, 3)
-    spread = lax.all_to_all(pieces, axes, split_axis=0, concat_axis=0, tiled=True)
-    holder = place_of(perm)
-    block = perm[:, :, None] + (sources - 1) - jnp.arange(sources, dtype=jnp.int32)
-    reader = jnp.take_along_axis(holder[:, None, :], jnp.minimum(block, count - 1), axis=2)
-    slot = jnp.arange(batches, dtype=jnp.int32)[:, None, None] * sources + jnp.arange(sources, dtype=jnp.int32)
-    index = (reader * (batches * sources) + slot).transpose(1, 0, 2)
-    picked = jnp.take(spread.reshape(count * batches * sources, part, cols), index.reshape(-1), axis=0)
-    picked = picked.reshape(count, batches, sources, part, cols).astype(jnp.float32)
-    valid = (block < count).transpose(1, 0, 2)[..., None, None]
-    summed = jnp.sum(jnp.where(valid, picked, 0.0), axis=2).astype(jnp.bfloat16)
-    arrived = lax.all_to_all(summed, axes, split_axis=0, concat_axis=0, tiled=True)
-    return arrived.transpose(1, 0, 2, 3).reshape(batches, rows, cols)
-
-
 def fast_body(grid, tokens, w_query, w_keyval, w_out, w_gate, w_up, w_down, gain_attn, gain_ffn, cotangent, block_perm, extra_len):
-    f32, bf16 = jnp.float32, jnp.bfloat16
     batches, _, rows, width = tokens.shape
     tok = batches * rows
     me = lax.axis_index(("dp", "fsdp"))
+    count = lax.axis_size(("dp", "fsdp"))
     sources = WIN // BLK + 1
-    scale = HD ** (-0.5)
     kvw = w_keyval.shape[1]
     gains = jnp.stack([gain_attn, gain_ffn], axis=1)
     small = jnp.concatenate([w_keyval, jnp.pad(gains, ((0, 0), (0, 126)))], axis=1)
     sub = w_down.shape[0]
     half = w_gate.shape[1] // 2
     shards = [small, w_query, w_out, by_parity(w_gate, sub), by_parity(w_up, sub), w_down]
-    units = [Unit(i, "all", (0, s.shape[0]), (0, s.shape[1])) for i, s in enumerate(shards[:3])]
+    units = [Unit(i, ALL, (0, s.shape[0]), (0, s.shape[1])) for i, s in enumerate(shards[:3])]
     for k in (0, 1):
-        units += [Unit(i, "cols", (0, w_gate.shape[0]), (k * half // 2, half // 2)) for i in (3, 4)]
-        units += [Unit(5, "rows", (0, sub), (k * width // 2, width // 2))]
+        units += [Unit(i, COLS, (0, w_gate.shape[0]), (k * half // 2, half // 2)) for i in (3, 4)]
+        units += [Unit(5, ROWS, (0, sub), (k * width // 2, width // 2))]
     holder = place_of(block_perm)
     block = block_perm[:, :, None] - (sources - 1) + jnp.arange(sources, dtype=jnp.int32)
     index = jnp.take_along_axis(holder[:, None, :], jnp.maximum(block, 0), axis=2)
@@ -991,39 +1275,19 @@
     x = tokens.reshape(tok, width)
     dy = cotangent.reshape(tok, width)
     fulls, dy_pair, n2_pair, n1b, query, window, att, mixed, gains = forward(grid, shards, units, x, dy, start, ends, index, sources, kvw, 0)
-    small, wq, wo, wg, wu, wd = fulls
-    wkv = small[:, :kvw]
-    g1, g2 = gains[0], gains[1]
-    x = x.astype(f32)
-    r1 = lax.rsqrt(jnp.mean(x * x, axis=-1, keepdims=True) + EPS)
-    r2 = lax.rsqrt(jnp.mean(mixed * mixed, axis=-1, keepdims=True) + EPS)
-    out, d_n2, d_wgate, d_wup, d_down = ffn(n2_pair.reshape(2 * tok, width), dy_pair.reshape(2 * tok, width), wg, wu, wd, 256)
-    d_n2 = from_mate(d_n2.reshape(2, tok, width))
-    out = from_mate(out.reshape(2, tok, width))
-    block_out = (mixed + out).astype(bf16)
-    d_mixed_norm, d_g2 = norm_back(mixed, r2, g2, d_n2)
-    d_mixed = dy.astype(f32) + d_mixed_norm
-    d_branch = d_mixed.astype(bf16)
-    d_wout = jnp.einsum("ta,td->ad", att, d_branch, preferred_element_type=f32).astype(bf16)
-    d_att = jnp.einsum("td,ad->ta", d_branch, wo, preferred_element_type=f32).astype(bf16)
-    d_query, d_window = attend_back(query, window, d_att, start, ends)
-    d_keyval = window_sums(d_window, block_perm, sources).reshape(tok, kvw)
-    d_wquery = (jnp.einsum("td,ta->da", n1b, d_query, preferred_element_type=f32) * scale).astype(bf16)
-    d_wkeyval = jnp.einsum("td,tc->dc", n1b, d_keyval, preferred_element_type=f32)
-    d_n1 = jnp.einsum("ta,da->td", d_query, wq, preferred_element_type=f32) * scale
-    d_n1 = d_n1 + jnp.einsum("tc,dc->td", d_keyval, wkv, preferred_element_type=f32)
-    d_x_norm, d_g1 = norm_back(x, r1, g1, d_n1)
-    grad_tokens = (d_mixed + d_x_norm).astype(bf16)
-    d_gains = jnp.pad(jnp.stack([d_g1, d_g2], axis=1), ((0, 0), (0, 126)))
-    d_small = jnp.concatenate([d_wkeyval, d_gains], axis=1).astype(bf16)
-    grads = [d_small, d_wquery, d_wout, d_wgate, d_wup, d_down]
-    kinds = ["all"] * 3 + ["cols"] * 2 + ["rows"]
-    grads = [
-        g.reshape(tuple(grid[:3]) + (grid[3] // 2 if k == "rows" else grid[3], -1, g.shape[1]))
-        for g, k in zip(grads, kinds)
-    ]
-    order = units[3:] + units[2:3] + units[1:2] + units[:1]
-    small, dq, do, dg, du, dd = scatter(grid, grads, [s.shape for s in shards], order, 1)
+    block = block_perm[:, :, None] + (sources - 1) - jnp.arange(sources, dtype=jnp.int32)
+    reader = jnp.take_along_axis(holder[:, None, :], jnp.minimum(block, count - 1), axis=2)
+    reader = reader.transpose(1, 0, 2).reshape(-1, batches * sources)
+    valid = (block < count).astype(jnp.int32).transpose(1, 0, 2).reshape(-1, batches * sources)
+    saved = dict(n2=n2_pair, dy=dy_pair, n1=n1b, q=query, window=window, att=att, mixed=mixed, x=x, gains=gains)
+    back = [Unit(i, ALL, (0, s.shape[0]), (c, min(width // 2, s.shape[1] - c))) for i, s in enumerate(shards[:3]) for c in range(0, s.shape[1], width // 2)]
+    for k in range(3):
+        back += [Unit(i, COLS, (0, w_gate.shape[0]), (k * half // 3, half // 3)) for i in (3, 4)]
+        back += [Unit(5, ROWS, (0, sub), (k * width // 3, width // 3))]
+    block_out, grad_tokens, grads = backward(
+        grid, fulls, [s.shape for s in shards], saved, start, ends, reader, valid, back, sources, kvw, 1
+    )
+    small, dq, do, dg, du, dd = grads
     dg, du = from_parity(dg, sub), from_parity(du, sub)
     return (
         block_out.reshape(tokens.shape),
@@ -1047,14 +1311,6 @@
 def from_parity(w, sub):
     _, rows, part = w.shape
     return w.reshape(2, rows, -1, sub).transpose(1, 2, 0, 3).reshape(rows, 2 * part)
-
-
-def from_mate(parts):
-    z = lax.axis_index("fsdp")
-    count = lax.axis_size("fsdp")
-    theirs = lax.dynamic_index_in_dim(parts, 1 - z % 2, 0, keepdims=False)
-    got = lax.ppermute(theirs.astype(jnp.bfloat16), "fsdp", [(i, i ^ 1) for i in range(count)])
-    return lax.dynamic_index_in_dim(parts, z % 2, 0, keepdims=False) + got.astype(jnp.float32)
 
 
 def solution(mesh):

time: 787 us -> 665 us (0.84)
  waiting for transfers between devices: 107 us -> 0 us
  Pallas kernels: 536 us -> 608 us
  matrix products: 32.9 us -> 0 us
  local copies, waits for them, and re-layouts: 61.9 us -> 38.4 us
  other arithmetic: 24.8 us -> 7.26 us
  starting transfers between devices: 13.1 us -> 0 us
    pallas_call x3 -> x1, Pallas kernels: 282 us -> 354 us  [backward(): pl.pallas_call(functools.partial(backward_kernel, grid, units, ends.shape...]
    ppermute x2 -> x0, waiting for transfers between devices: 60.9 us -> none  [from_mate(): lax.ppermute(theirs.astype(jnp.bfloat16), 'fsdp', [(i, i ^ 1) for i in ra...]
    all_to_all x2 -> x0, waiting for transfers between devices: 45.9 us -> none  [the longest x1 45.1 us: window_sums(): lax.all_to_all(pieces, axes, split_axis=0, concat_axis=0, tiled=True)]
    dot_general x6 -> x0, matrix products: 32.9 us -> none  [the longest x1 7.2 us: fast_body(): jnp.einsum('ta,td->ad', att, d_branch, preferred_element_type=f32)]
    reduce_sum x4 -> x0, other arithmetic: 8.37 us -> none  [the longest x1 4.1 us: window_sums(): summed = jnp.sum(jnp.where(valid, picked, 0.0), axis=2).astype(jnp.bfloat16)]
    all_to_all x2 -> x0, starting transfers between devices: 8.26 us -> none  [the longest x1 4.73 us: window_sums(): lax.all_to_all(summed, axes, split_axis=0, concat_axis=0, tiled=True)]
  transfers between devices with their start and end apart: 4 -> 0, of which waited for: 4 -> 0; matrix products, arithmetic and copies ran while one was open for 5% -> 0% of each run, Pallas kernels for 0% -> 0%
where the time goes in v4:
time: 665 us; the launch traced here: 655 us
  Pallas kernels  608 us (91%)
  local copies, waits for them, and re-layouts  38.4 us (6%)
  other arithmetic  7.26 us (1%)
    pallas_call x1, Pallas kernels, backward(): pl.pallas_call(functools.partial(backward_kernel, grid, units, ends.shape...  354 us
    pallas_call x1, Pallas kernels, forward(): pl.pallas_call(functools.partial(forward_kernel, grid, units, ends.shape[...  254 us

profile of v4, /device:TPU:0, one launch (start us, length us, event | category | flops | bytes accessed | tf_op | source)
XLA Modules:
  0.0 655.1 jit_solution(6540127339612211871)
XLA Ops:
  0.6 1.4 multiply_reduce_fusion.refs_0_
  2.0 0.7 pad_maximum_fusion
  2.7 0.7 broadcast_add_fusion.2
  3.4 0.7 reduce_window_sum.11.refs_1_
  4.2 0.7 broadcast_add_fusion
  5.7 0.8 copy.62
  6.5 0.8 sort.17
  7.4 1.4 fusion.1.refs_5_
  9.0 3.1 gather_fusion.1
  12.3 3.1 gather_fusion
  15.8 0.7 copy.72.refs_2_
  16.8 0.7 copy.71.refs_2_
  17.5 1.4 reshape.98
  19.0 1.9 reshape.99.refs_8_
  20.9 1.4 reshape.100
  22.4 1.9 reshape.101.refs_9_
  24.2 254.1 %forward.1 = (bf16[2,2,2,4,48,640]{5,4,3,2,1,0:T(8,128)(2,1)}, bf16[2,2,2,4,48,1536]{5,4,3,2,1,0:T(8,128)(2,1)}, bf16[2,2,2,4,48,1536]{5,4,3,2,1,0:T(8,128)(2,1)...) custom-call(s32[2]{0:T(128)} %multiply_reduce_fusion.refs_0_, ...), custom_call_target="tpu_custom_call" | custom-call | tf_op jit(solution)/shard_map/forward/pallas_call | solution.py:777
  278.4 354.0 %backward.1 = (f32[48,640]{1,0:T(8,128)}, f32[48,1536]{1,0:T(8,128)}, f32[48,1536]{1,0:T(8,128)}, f32[2,48,2304]{2,1,0:T(8,128)}, f32[2,48,2304]{2,1,0:T(8,128)}...) custom-call(s32[2]{0:T(128)} %multiply_reduce_fusion.refs_0_, ...), custom_call_target="tpu_custom_call" | custom-call | tf_op jit(solution)/shard_map/backward/pallas_call | solution.py:1222
  632.4 1.5 slice_reduce_fusion
  633.9 1.5 slice.9
  635.5 2.6 reshape.109
  638.1 1.4 copy.73
  639.4 3.0 reshape.110
  642.4 2.3 reshape.111
  644.8 1.4 copy.74
  646.2 3.0 reshape.112
  649.2 1.1 copy.86
  650.3 0.8 copy-done
  651.1 1.1 copy.87
  652.3 0.7 copy.88
  653.0 0.7 copy.89
  653.7 0.9 copy.90
  (35 shorter events, 2.2 us)
Async XLA Ops:
  12.3 5.2 copy-start.3
  18.9 2.0 copy-start.4
  646.2 3.0 copy-start.1
  649.2 2.0 copy-start
  651.1 1.2 copy-start.6
  651.1 1.9 copy-start.5
  651.1 2.6 copy-start.2

commit v5 on v4

--- a/solution.py
+++ b/solution.py
@@ -1016,13 +1016,12 @@
     def phase_c(dmixed, datt, dq, dgain):
         dgain[...] = jnp.zeros_like(dgain)
 
-        def through_ffn(mixed, dn2, got2, dy, att, wo):
+        def through_ffn(mixed, dn2, got2, dy, wo):
             pulls = [
                 local_copy(r.mixed, mixed, 0),
                 local_copy(r.dn2_own, dn2, 1),
                 local_copy(r.dy.at[p.half], dy, 2),
                 local_copy(r.wo, wo, 3),
-                local_copy(r.att, att, 4),
             ]
             start(pulls)
             dn2_swap.wait()
@@ -1040,8 +1039,7 @@
             dgain[1:2] = total
             for j in range(0, width, 512):
                 datt[:, j : j + 512] = dot_t(dy[...], wo[j : j + 512]).astype(BF16)
-            rs.tick()
-            weight_grad(att[...], dy, r.g_wo, 2, 6)
+            fetch(dy, r.dn2_to, 5)
 
         pl.run_scoped(
             through_ffn,
@@ -1049,10 +1047,8 @@
             f32_tok,
             bf_tok,
             bf_tok,
-            bf_tok,
             pltpu.VMEM((width, width), BF16),
         )
-        rs.tick()
 
         def through_attention(dkvw, n1, w, small, x):
             later = [local_copy(r.n1, n1, 0), local_copy(r.wq, w, 1), local_copy(r.small, small, 2), local_copy(r.x, x, 3)]
@@ -1082,7 +1078,7 @@
                             dkv[:, :HD] += t_dot(ds, qh)
                             dkv[:, HD:] += t_dot(prob.astype(BF16), d)
 
-                        rs.tick(1)
+                        rs.tick(1 if h0 > 0 and m == 0 else 0)
                     dkvw[m] = dkv[...].astype(BF16).reshape(dkvw.shape[1:])
 
             pl.run_scoped(heads, bf_tok, pltpu.VMEM(r.window.shape, BF16), pltpu.VMEM((sources * BLK, kvw), F32))
@@ -1106,6 +1102,16 @@
             ex1.begin(src1, dst1)
             for c in later:
                 c.wait()
+
+            def out_grad(att, dbranch):
+                pulls = [local_copy(r.att, att, 4), local_copy(r.dn2_to, dbranch, 5)]
+                start(pulls)
+                for c in pulls:
+                    c.wait()
+                weight_grad(att[...], dbranch, r.g_wo, 2, 6)
+
+            pl.run_scoped(out_grad, bf_tok, bf_tok)
+            rs.tick()
             weight_grad(n1[...], dq, r.g_wq, 1, 6, HD**-0.5)
             rs.tick()
 
@@ -1122,7 +1128,7 @@
 
             some, some_low = pltpu.VMEM((256, width), F32), pltpu.VMEM((256, width), BF16)
             pl.run_scoped(output, some, some, some_low, some_low)
-            rs.tick(0)
+            rs.tick(2)
 
             def to_input(dn1, got):
                 for j in range(0, width, 512):
@@ -1140,7 +1146,7 @@
                         sums[d, m] = s.astype(BF16)
 
                 ex2.begin(src2, dst2)
-                rs.tick(0)
+                rs.tick(1)
                 ex2.end(src2, dst2)
                 dkv = dkv_own[...].reshape(tok, kvw)
                 part = width // grid[0]
@@ -1246,8 +1252,11 @@
     found = dict(zip(outputs, results))
     return found["block_out"], found["grad_tokens"], results[: len(ARRAYS)]
 
-def place_of(perm):
-    return jnp.argsort(perm, axis=1).astype(jnp.int32)
+def holders_of(perm, block):
+    count = perm.shape[1]
+    same = perm[:, None, None, :] == block[..., None]
+    found = jnp.max(jnp.where(same, jnp.arange(count, dtype=jnp.int32), 0), axis=-1)
+    return found.transpose(1, 0, 2).reshape(count, -1)
 
 
 def fast_body(grid, tokens, w_query, w_keyval, w_out, w_gate, w_up, w_down, gain_attn, gain_ffn, cotangent, block_perm, extra_len):
@@ -1266,18 +1275,15 @@
     for k in (0, 1):
         units += [Unit(i, COLS, (0, w_gate.shape[0]), (k * half // 2, half // 2)) for i in (3, 4)]
         units += [Unit(5, ROWS, (0, sub), (k * width // 2, width // 2))]
-    holder = place_of(block_perm)
-    block = block_perm[:, :, None] - (sources - 1) + jnp.arange(sources, dtype=jnp.int32)
-    index = jnp.take_along_axis(holder[:, None, :], jnp.maximum(block, 0), axis=2)
-    index = index.transpose(1, 0, 2).reshape(-1, batches * sources)
+    lags = jnp.arange(sources, dtype=jnp.int32)
+    index = holders_of(block_perm, jnp.maximum(block_perm[:, :, None] - (sources - 1) + lags, 0))
     start = lax.dynamic_slice_in_dim(block_perm, me, 1, axis=1)[:, 0] * BLK
     ends = jnp.cumsum(extra_len + (WIN - 1), axis=1).astype(jnp.int32)
     x = tokens.reshape(tok, width)
     dy = cotangent.reshape(tok, width)
     fulls, dy_pair, n2_pair, n1b, query, window, att, mixed, gains = forward(grid, shards, units, x, dy, start, ends, index, sources, kvw, 0)
-    block = block_perm[:, :, None] + (sources - 1) - jnp.arange(sources, dtype=jnp.int32)
-    reader = jnp.take_along_axis(holder[:, None, :], jnp.minimum(block, count - 1), axis=2)
-    reader = reader.transpose(1, 0, 2).reshape(-1, batches * sources)
+    block = block_perm[:, :, None] + (sources - 1) - lags
+    reader = holders_of(block_perm, jnp.minimum(block, count - 1))
     valid = (block < count).astype(jnp.int32).transpose(1, 0, 2).reshape(-1, batches * sources)
     saved = dict(n2=n2_pair, dy=dy_pair, n1=n1b, q=query, window=window, att=att, mixed=mixed, x=x, gains=gains)
     back = [Unit(i, ALL, (0, s.shape[0]), (c, min(width // 2, s.shape[1] - c))) for i, s in enumerate(shards[:3]) for c in range(0, s.shape[1], width // 2)]

time: 665 us -> 654 us (0.983)
  local copies, waits for them, and re-layouts: 38.4 us -> 31.5 us
    gather x6 -> x0, local copies, waits for them, and re-layouts: 6.8 us -> none  [the longest x3 3.4 us: fast_body(): jnp.take_along_axis(holder[:, None, :], jnp.minimum(block, count - 1), ax...]
where the time goes in v5:
time: 654 us; the launch traced here: 649 us
  Pallas kernels  609 us (93%)
  local copies, waits for them, and re-layouts  31.5 us (5%)
  other arithmetic  7.42 us (1%)
    pallas_call x1, Pallas kernels, backward(): pl.pallas_call(functools.partial(backward_kernel, grid, units, ends.shape...  355 us
    pallas_call x1, Pallas kernels, forward(): pl.pallas_call(functools.partial(forward_kernel, grid, units, ends.shape[...  254 us

profile of v5, /device:TPU:0, one launch (start us, length us, event | category | flops | bytes accessed | tf_op | source)
XLA Modules:
  0.0 648.9 jit_solution(12194418689957248421)
XLA Ops:
  0.6 1.4 multiply_reduce_fusion.refs_0_
  2.0 0.7 pad_maximum_fusion
  2.7 0.7 broadcast_add_fusion.2
  3.4 0.7 reduce_window_sum.11.refs_1_
  4.2 0.7 fusion.3
  5.0 0.6 fusion.2.refs_3_
  5.7 1.2 select_reduce_fusion
  7.0 0.7 copy.68.refs_2_
  7.7 0.7 copy.67.refs_2_
  8.3 1.4 fusion.1.refs_5_
  9.8 2.3 reshape.99
  12.1 0.1 copy.76
  12.2 1.9 reshape.100.refs_8_
  14.1 1.4 reshape.101
  15.5 0.1 copy.75
  15.6 1.9 reshape.102.refs_9_
  17.5 253.8 %forward.1 = (bf16[2,2,2,4,48,640]{5,4,3,2,1,0:T(8,128)(2,1)}, bf16[2,2,2,4,48,1536]{5,4,3,2,1,0:T(8,128)(2,1)}, bf16[2,2,2,4,48,1536]{5,4,3,2,1,0:T(8,128)(2,1)...) custom-call(s32[2]{0:T(128)} %multiply_reduce_fusion.refs_0_, ...), custom_call_target="tpu_custom_call" | custom-call | tf_op jit(solution)/shard_map/forward/pallas_call | solution.py:777
  271.3 355.2 %backward.1 = (f32[48,640]{1,0:T(8,128)}, f32[48,1536]{1,0:T(8,128)}, f32[48,1536]{1,0:T(8,128)}, f32[2,48,2304]{2,1,0:T(8,128)}, f32[2,48,2304]{2,1,0:T(8,128)}...) custom-call(s32[2]{0:T(128)} %multiply_reduce_fusion.refs_0_, ...), custom_call_target="tpu_custom_call" | custom-call | tf_op jit(solution)/shard_map/backward/pallas_call | solution.py:1228
  626.5 1.5 slice_reduce_fusion
  628.0 1.5 slice.9
  629.6 2.5 reshape.110
  632.1 1.4 copy.69
  633.5 3.0 reshape.111
  636.5 2.3 reshape.112
  638.8 1.4 copy.70
  640.2 3.0 reshape.113
  643.2 1.1 copy.82
  644.4 0.8 copy-done
  645.2 1.1 copy.83
  646.3 0.7 copy.84
  647.1 0.7 copy.85
  647.8 0.9 copy.86
  (20 shorter events, 0.3 us)
Async XLA Ops:
  12.1 2.0 copy-start.3
  640.2 3.0 copy-start.1
  643.2 2.0 copy-start
  645.2 1.2 copy-start.5
  645.2 1.9 copy-start.4
  645.2 2.6 copy-start.2

commit v6 on v5

--- a/solution.py
+++ b/solution.py
@@ -1128,7 +1128,7 @@
 
             some, some_low = pltpu.VMEM((256, width), F32), pltpu.VMEM((256, width), BF16)
             pl.run_scoped(output, some, some, some_low, some_low)
-            rs.tick(2)
+            rs.tick(0)
 
             def to_input(dn1, got):
                 for j in range(0, width, 512):

time: 654 us -> 649 us (level)
  no operation moved by 1% of the time
where the time goes in v6:
time: 649 us; the launch traced here: 643 us
  Pallas kernels  604 us (93%)
  local copies, waits for them, and re-layouts  31.5 us (5%)
  other arithmetic  7.42 us (1%)
    pallas_call x1, Pallas kernels, backward(): pl.pallas_call(functools.partial(backward_kernel, grid, units, ends.shape...  350 us
    pallas_call x1, Pallas kernels, forward(): pl.pallas_call(functools.partial(forward_kernel, grid, units, ends.shape[...  254 us

profile of v6, /device:TPU:0, one launch (start us, length us, event | category | flops | bytes accessed | tf_op | source)
XLA Modules:
  0.0 643.4 jit_solution(14083805155541509401)
XLA Ops:
  0.6 1.4 multiply_reduce_fusion.refs_0_
  2.0 0.7 pad_maximum_fusion
  2.7 0.7 broadcast_add_fusion.2
  3.4 0.7 reduce_window_sum.11.refs_1_
  4.2 0.7 fusion.3
  5.0 0.6 fusion.2.refs_3_
  5.7 1.2 select_reduce_fusion
  7.0 0.7 copy.68.refs_2_
  7.7 0.7 copy.67.refs_2_
  8.3 1.4 fusion.1.refs_5_
  9.8 2.3 reshape.99
  12.1 0.1 copy.76
  12.2 1.9 reshape.100.refs_8_
  14.1 1.4 reshape.101
  15.5 0.1 copy.75
  15.6 1.9 reshape.102.refs_9_
  17.5 253.8 %forward.1 = (bf16[2,2,2,4,48,640]{5,4,3,2,1,0:T(8,128)(2,1)}, bf16[2,2,2,4,48,1536]{5,4,3,2,1,0:T(8,128)(2,1)}, bf16[2,2,2,4,48,1536]{5,4,3,2,1,0:T(8,128)(2,1)...) custom-call(s32[2]{0:T(128)} %multiply_reduce_fusion.refs_0_, ...), custom_call_target="tpu_custom_call" | custom-call | tf_op jit(solution)/shard_map/forward/pallas_call | solution.py:777
  271.3 349.7 %backward.1 = (f32[48,640]{1,0:T(8,128)}, f32[48,1536]{1,0:T(8,128)}, f32[48,1536]{1,0:T(8,128)}, f32[2,48,2304]{2,1,0:T(8,128)}, f32[2,48,2304]{2,1,0:T(8,128)}...) custom-call(s32[2]{0:T(128)} %multiply_reduce_fusion.refs_0_, ...), custom_call_target="tpu_custom_call" | custom-call | tf_op jit(solution)/shard_map/backward/pallas_call | solution.py:1228
  621.0 1.5 slice_reduce_fusion
  622.5 1.5 slice.9
  624.1 2.5 reshape.110
  626.6 1.4 copy.69
  628.0 3.0 reshape.111
  631.0 2.3 reshape.112
  633.3 1.4 copy.70
  634.7 3.0 reshape.113
  637.7 1.1 copy.82
  638.9 0.8 copy-done
  639.7 1.1 copy.83
  640.8 0.7 copy.84
  641.6 0.7 copy.85
  642.3 0.9 copy.86
  (20 shorter events, 0.3 us)
Async XLA Ops:
  12.1 2.0 copy-start.3
  634.7 3.0 copy-start.1
  637.7 2.0 copy-start
  639.7 1.2 copy-start.5
  639.7 1.9 copy-start.4
  639.7 2.6 copy-start.2
